TPU v7x, 32 devices: a whole 2x2x4 slice. The times are simulated.
32 devices in a mesh: dp: 4 (over z), tp: 4 (over x, core), expert: 2 (over y).
Axes of the slice: x: 2, y: 2, z: 4, core: 2. Of those that a mesh axis runs over, the one named last changes fastest.
Arguments:
- prefix_in: bfloat16 [8, 576, 2048], P('dp', 'expert'), may hold values from -6 to 6
- suffix_in: bfloat16 [8, 51, 1024], P(('dp', 'expert')), may hold values from -6 to 6
- noisy_actions: bfloat16 [8, 50, 32], P(('dp', 'expert')), may hold values from -6 to 6
- prefix_len: int32 [8], P('dp'), may hold values from 144 to 576, as said below
- action_live: int32 [8, 32], P(('dp', 'expert')), may hold values from 0 to 1, as said below
- pre_query: bfloat16 [2048, 2048], P(('dp', 'expert'), 'tp'), may hold values from -0.125 to 0.125
- pre_keyval: bfloat16 [2048, 512], P(('dp', 'expert')), may hold values from -0.125 to 0.125
- pre_output: bfloat16 [2048, 2048], P('tp', ('dp', 'expert')), may hold values from -1.5 to 1.5
- pre_gate: bfloat16 [2048, 16384], P(('dp', 'expert'), 'tp'), may hold values from -0.125 to 0.125
- pre_up: bfloat16 [2048, 16384], P(('dp', 'expert'), 'tp'), may hold values from -0.125 to 0.125
- pre_down: bfloat16 [16384, 2048], P('tp', ('dp', 'expert')), may hold values from -0.046875 to 0.046875
- pre_norm_attn: bfloat16 [2048], P(('dp', 'expert')), may hold values from 0.099609375 to 1.8984375
- pre_norm_ffn: bfloat16 [2048], P(('dp', 'expert')), may hold values from 0.099609375 to 1.8984375
- act_query: bfloat16 [1024, 2048], P(('dp', 'expert'), 'tp'), may hold values from -0.1875 to 0.1875
- act_keyval: bfloat16 [1024, 512], P(('dp', 'expert')), may hold values from -0.1875 to 0.1875
- act_output: bfloat16 [2048, 1024], P('tp', ('dp', 'expert')), may hold values from -1.5 to 1.5
- act_gate: bfloat16 [1024, 4096], P(('dp', 'expert'), 'tp'), may hold values from -0.1875 to 0.1875
- act_up: bfloat16 [1024, 4096], P(('dp', 'expert'), 'tp'), may hold values from -0.1875 to 0.1875
- act_down: bfloat16 [4096, 1024], P('tp', ('dp', 'expert')), may hold values from -0.09375 to 0.09375
- act_norm_attn: bfloat16 [1024], P(('dp', 'expert')), may hold values from 0.099609375 to 1.8984375
- act_norm_ffn: bfloat16 [1024], P(('dp', 'expert')), may hold values from 0.099609375 to 1.8984375
- action_embed: bfloat16 [32, 1024], P(('dp', 'expert')), may hold values from -1.5 to 1.5
- prefix_cot: bfloat16 [8, 576, 2048], P('dp', 'expert'), may hold values from -6 to 6
- suffix_cot: bfloat16 [8, 51, 1024], P(('dp', 'expert')), may hold values from -6 to 6
Outputs:
- prefix_out: bfloat16 [8, 576, 2048], P('dp', 'expert')
- suffix_out: bfloat16 [8, 51, 1024], P(('dp', 'expert'))
- prefix_in_grad: float32 [8, 576, 2048], P('dp', 'expert')
- suffix_in_grad: float32 [8, 51, 1024], P(('dp', 'expert'))
- pre_query_grad: float32 [2048, 2048], P(('dp', 'expert'), 'tp')
- pre_keyval_grad: float32 [2048, 512], P(('dp', 'expert'))
- pre_output_grad: float32 [2048, 2048], P('tp', ('dp', 'expert'))
- pre_gate_grad: float32 [2048, 16384], P(('dp', 'expert'), 'tp')
- pre_up_grad: float32 [2048, 16384], P(('dp', 'expert'), 'tp')
- pre_down_grad: float32 [16384, 2048], P('tp', ('dp', 'expert'))
- pre_norm_attn_grad: float32 [2048], P(('dp', 'expert'))
- pre_norm_ffn_grad: float32 [2048], P(('dp', 'expert'))
- act_query_grad: float32 [1024, 2048], P(('dp', 'expert'), 'tp')
- act_keyval_grad: float32 [1024, 512], P(('dp', 'expert'))
- act_output_grad: float32 [2048, 1024], P('tp', ('dp', 'expert'))
- act_gate_grad: float32 [1024, 4096], P(('dp', 'expert'), 'tp')
- act_up_grad: float32 [1024, 4096], P(('dp', 'expert'), 'tp')
- act_down_grad: float32 [4096, 1024], P('tp', ('dp', 'expert'))
- act_norm_attn_grad: float32 [1024], P(('dp', 'expert'))
- act_norm_ffn_grad: float32 [1024], P(('dp', 'expert'))
- action_embed_grad: float32 [32, 1024], P(('dp', 'expert'))
Inputs may be any that keep to these rules, and one draw needn't show every extreme that they name: `prefix_len`: prefix positions at or beyond an item's length are never attended; among the items of each index of dp one has the full 576 and another 576 // 4. `action_live`: 1 marks a live action dimension; each item has 7 to 18 live ones, some item 7 and another 18.
All inputs are finite; a program needn't handle non-finite values.
Results may differ from a plain program's by a relative error of at most 0.014.
Values may be sent and summed in bfloat16 or wider, within the bound.
No kernel may reach another device: no remote copies, remote signals or barrier semaphores. Data moves between devices by JAX's collectives and lax.ppermute only.
A program may use at most 320 MiB of HBM per device.

v0:
```python
import jax
import jax.numpy as jnp
from jax import lax
from jax.sharding import PartitionSpec as P

HD = 256


EPSILON = 1e-06


def rms_scale(values, gain):
    return values * lax.rsqrt(jnp.mean(values * values, axis=-1, keepdims=True) + EPSILON) * gain


def gelu_tanh(values):
    return jax.nn.gelu(values, approximate=True)


def geglu(gate, upward):
    return gelu_tanh(gate) * upward


def project(left, right):
    return jnp.dot(left, right, preferred_element_type=jnp.float32)


def project_back(left, right):
    return lax.dot_general(
        left, right, (((1,), (1,)), ((), ())), preferred_element_type=jnp.float32
    )


def outer_sum(left, right):
    return lax.dot_general(
        left, right, (((0,), (0,)), ((), ())), preferred_element_type=jnp.float32
    )


def attn_scores(queries, keys, allowed, scale):
    scores = jnp.einsum("bqhe,bke->bhqk", queries, keys, preferred_element_type=jnp.float32) * scale
    return jnp.where(allowed[:, None], scores, -1e30)


def attend(queries, keyval, allowed, scale, head_size):
    masked = attn_scores(queries, keyval[..., :head_size], allowed, scale)
    top = jnp.max(masked, axis=-1, keepdims=True)
    expo = jnp.exp(masked - top)
    denom = jnp.sum(expo, axis=-1, keepdims=True)
    probs = (expo / denom).astype(jnp.bfloat16)
    attended = jnp.einsum(
        "bhqk,bke->bqhe", probs, keyval[..., head_size:], preferred_element_type=jnp.float32
    )
    return (attended.astype(jnp.bfloat16), top + jnp.log(denom))


def attend_back(queries, keyval, allowed, scale, head_size, logsum, grad_att):
    keys = keyval[..., :head_size]
    masked = attn_scores(queries, keys, allowed, scale)
    probs = jnp.exp(masked - logsum)
    grad_probs = jnp.einsum(
        "bqhe,bke->bhqk", grad_att, keyval[..., head_size:], preferred_element_type=jnp.float32
    )
    delta = jnp.sum(probs * grad_probs, axis=-1, keepdims=True)
    grad_scores = (probs * (grad_probs - delta)).astype(jnp.bfloat16)
    grad_queries = (
        jnp.einsum("bhqk,bke->bqhe", grad_scores, keys, preferred_element_type=jnp.float32) * scale
    )
    grad_keys = (
        jnp.einsum("bhqk,bqhe->bke", grad_scores, queries, preferred_element_type=jnp.float32)
        * scale
    )
    grad_values = jnp.einsum(
        "bhqk,bqhe->bke", probs.astype(jnp.bfloat16), grad_att, preferred_element_type=jnp.float32
    )
    return (grad_queries, jnp.concatenate([grad_keys, grad_values], axis=-1))


def ffn_forward(resid, gain, w_gate, w_up, w_down):
    normed = rms_scale(resid, gain.astype(jnp.float32)).astype(jnp.bfloat16)
    gate = project(normed, w_gate)
    upward = project(normed, w_up)
    hidden = geglu(gate, upward).astype(jnp.bfloat16)
    return (normed, gate, upward, hidden, project(hidden, w_down))


def ffn_backward(normed, gate, upward, hidden, cotangent, w_gate, w_up, w_down):
    grad_down = outer_sum(hidden, cotangent)
    grad_hidden = project_back(cotangent, w_down)
    grad_gate, grad_upward = jax.vjp(geglu, gate, upward)[1](grad_hidden)
    grad_gate = grad_gate.astype(jnp.bfloat16)
    grad_upward = grad_upward.astype(jnp.bfloat16)
    normed_cot = project_back(grad_gate, w_gate) + project_back(grad_upward, w_up)
    return (grad_down, outer_sum(normed, grad_gate), outer_sum(normed, grad_upward), normed_cot)


def head_sums(first, second):
    return lax.psum((first, second), "tp")


def norm_back(values, gain, cotangent):
    return jax.vjp(rms_scale, values, gain.astype(jnp.float32))[1](cotangent)


def local(
    prefix_in,
    suffix_in,
    noisy_actions,
    prefix_len,
    action_live,
    pre_query,
    pre_keyval,
    pre_output,
    pre_gate,
    pre_up,
    pre_down,
    pre_norm_attn,
    pre_norm_ffn,
    act_query,
    act_keyval,
    act_output,
    act_gate,
    act_up,
    act_down,
    act_norm_attn,
    act_norm_ffn,
    action_embed,
    prefix_cot,
    suffix_cot,
):
    gathered = (
        lax.all_gather(pre_query, ("dp", "expert"), axis=0, tiled=True),
        lax.all_gather(pre_keyval, ("dp", "expert"), axis=0, tiled=True),
        lax.all_gather(pre_gate, ("dp", "expert"), axis=0, tiled=True),
        lax.all_gather(pre_up, ("dp", "expert"), axis=0, tiled=True),
        lax.all_gather(act_query, ("dp", "expert"), axis=0, tiled=True),
        lax.all_gather(act_keyval, ("dp", "expert"), axis=0, tiled=True),
        lax.all_gather(act_gate, ("dp", "expert"), axis=0, tiled=True),
        lax.all_gather(act_up, ("dp", "expert"), axis=0, tiled=True),
        lax.all_gather(action_embed, ("dp", "expert"), axis=0, tiled=True),
        lax.all_gather(pre_norm_attn, ("dp", "expert"), axis=0, tiled=True),
        lax.all_gather(pre_norm_ffn, ("dp", "expert"), axis=0, tiled=True),
        lax.all_gather(act_norm_attn, ("dp", "expert"), axis=0, tiled=True),
        lax.all_gather(act_norm_ffn, ("dp", "expert"), axis=0, tiled=True),
        lax.all_gather(pre_output, ("dp", "expert"), axis=1, tiled=True),
        lax.all_gather(pre_down, ("dp", "expert"), axis=1, tiled=True),
        lax.all_gather(act_output, ("dp", "expert"), axis=1, tiled=True),
        lax.all_gather(act_down, ("dp", "expert"), axis=1, tiled=True),
    )
    (
        full_pq,
        full_pkv,
        full_pg,
        full_pu,
        full_aq,
        full_akv,
        full_ag,
        full_au,
        full_embed,
        gain_pa,
        gain_pf,
        gain_aa,
        gain_af,
        full_po,
        full_pd,
        full_ao,
        full_ad,
    ) = gathered
    pre_items, half_rows, width = prefix_in.shape
    suf_items, suf_len, act_width = suffix_in.shape
    head_size = HD
    scale = HD ** (-0.5)
    heads_local = full_pq.shape[1] // head_size
    group = lax.axis_index("expert")
    prefix_x = prefix_in.astype(jnp.float32).reshape(pre_items * half_rows, width)
    chosen = jnp.where(action_live[:, None, :] == 1, noisy_actions, jnp.zeros_like(noisy_actions))
    embedded = jnp.einsum("ita,ad->itd", chosen, full_embed, preferred_element_type=jnp.float32)
    suffix_x = suffix_in.astype(jnp.float32) + jnp.concatenate(
        [jnp.zeros((suf_items, 1, act_width), jnp.float32), embedded], axis=1
    )
    suffix_x = suffix_x.reshape(suf_items * suf_len, act_width)
    normed_pre = rms_scale(prefix_x, gain_pa.astype(jnp.float32)).astype(jnp.bfloat16)
    normed_suf = rms_scale(suffix_x, gain_aa.astype(jnp.float32)).astype(jnp.bfloat16)
    queries_pre = (
        project(normed_pre, full_pq)
        .astype(jnp.bfloat16)
        .reshape(pre_items, half_rows, heads_local, head_size)
    )
    queries_suf = (
        project(normed_suf, full_aq)
        .astype(jnp.bfloat16)
        .reshape(suf_items, suf_len, heads_local, head_size)
    )
    keyval_pre = (
        project(normed_pre, full_pkv)
        .astype(jnp.bfloat16)
        .reshape(pre_items, half_rows, 2 * head_size)
    )
    keyval_suf = (
        project(normed_suf, full_akv)
        .astype(jnp.bfloat16)
        .reshape(suf_items, suf_len, 2 * head_size)
    )
    keyval_all = lax.all_gather(keyval_pre, "expert", axis=1, tiled=True)
    full_len = keyval_all.shape[1]
    key_live = jnp.arange(full_len)[None, :] < prefix_len[:, None]
    pre_allowed = jnp.broadcast_to(key_live[:, None, :], (pre_items, half_rows, full_len))
    own_live = lax.dynamic_slice_in_dim(key_live, group * suf_items, suf_items, 0)
    blocks = jnp.minimum(jnp.arange(suf_len), 1)
    later = blocks[None, :] <= blocks[:, None]
    suf_allowed = jnp.concatenate(
        [jnp.broadcast_to(own_live[:, None, :], (suf_items, suf_len, full_len)), later[None]],
        axis=2,
    )

    def suffix_keys(keyval_whole):
        own_keys = lax.dynamic_slice_in_dim(keyval_whole, group * suf_items, suf_items, 0)
        return jnp.concatenate([own_keys, keyval_suf], axis=1)

    att_pre, logsum_pre = attend(queries_pre, keyval_all, pre_allowed, scale, head_size)
    att_suf, logsum_suf = attend(
        queries_suf, suffix_keys(keyval_all), suf_allowed, scale, head_size
    )
    att_pre = att_pre.reshape(pre_items * half_rows, heads_local * head_size)
    att_suf = att_suf.reshape(suf_items * suf_len, heads_local * head_size)
    branch_pre, branch_suf = head_sums(project(att_pre, full_po), project(att_suf, full_ao))
    resid_pre = prefix_x + branch_pre
    resid_suf = suffix_x + branch_suf
    ffn_pre = ffn_forward(resid_pre, gain_pf, full_pg, full_pu, full_pd)
    ffn_suf = ffn_forward(resid_suf, gain_af, full_ag, full_au, full_ad)
    final_pre, final_suf = head_sums(ffn_pre[4], ffn_suf[4])
    prefix_out = (resid_pre + final_pre).astype(jnp.bfloat16).reshape(pre_items, half_rows, width)
    suffix_out = (resid_suf + final_suf).astype(jnp.bfloat16).reshape(suf_items, suf_len, act_width)
    again = (
        lax.all_gather(pre_query, ("dp", "expert"), axis=0, tiled=True),
        lax.all_gather(pre_keyval, ("dp", "expert"), axis=0, tiled=True),
        lax.all_gather(pre_gate, ("dp", "expert"), axis=0, tiled=True),
        lax.all_gather(pre_up, ("dp", "expert"), axis=0, tiled=True),
        lax.all_gather(act_query, ("dp", "expert"), axis=0, tiled=True),
        lax.all_gather(act_keyval, ("dp", "expert"), axis=0, tiled=True),
        lax.all_gather(act_gate, ("dp", "expert"), axis=0, tiled=True),
        lax.all_gather(act_up, ("dp", "expert"), axis=0, tiled=True),
        lax.all_gather(action_embed, ("dp", "expert"), axis=0, tiled=True),
        lax.all_gather(pre_norm_attn, ("dp", "expert"), axis=0, tiled=True),
        lax.all_gather(pre_norm_ffn, ("dp", "expert"), axis=0, tiled=True),
        lax.all_gather(act_norm_attn, ("dp", "expert"), axis=0, tiled=True),
        lax.all_gather(act_norm_ffn, ("dp", "expert"), axis=0, tiled=True),
        lax.all_gather(pre_output, ("dp", "expert"), axis=1, tiled=True),
        lax.all_gather(pre_down, ("dp", "expert"), axis=1, tiled=True),
        lax.all_gather(act_output, ("dp", "expert"), axis=1, tiled=True),
        lax.all_gather(act_down, ("dp", "expert"), axis=1, tiled=True),
    )
    keyval_back = lax.all_gather(keyval_pre, "expert", axis=1, tiled=True)
    (
        back_pq,
        back_pkv,
        back_pg,
        back_pu,
        back_aq,
        back_akv,
        back_ag,
        back_au,
        back_embed,
        back_gpa,
        back_gpf,
        back_gaa,
        back_gaf,
        back_po,
        back_pd,
        back_ao,
        back_ad,
    ) = again
    cot_pre = prefix_cot.reshape(pre_items * half_rows, width)
    cot_suf = suffix_cot.reshape(suf_items * suf_len, act_width)
    down_pre, gate_w_pre, up_w_pre, mcot_pre = ffn_backward(
        ffn_pre[0], ffn_pre[1], ffn_pre[2], ffn_pre[3], cot_pre, back_pg, back_pu, back_pd
    )
    down_suf, gate_w_suf, up_w_suf, mcot_suf = ffn_backward(
        ffn_suf[0], ffn_suf[1], ffn_suf[2], ffn_suf[3], cot_suf, back_ag, back_au, back_ad
    )
    mcot_pre, mcot_suf = lax.psum((mcot_pre, mcot_suf), "tp")
    mid_part_pre, ffn_gain_pre = norm_back(resid_pre, back_gpf, mcot_pre)
    mid_part_suf, ffn_gain_suf = norm_back(resid_suf, back_gaf, mcot_suf)
    mid_pre = cot_pre.astype(jnp.float32) + mid_part_pre
    mid_suf = cot_suf.astype(jnp.float32) + mid_part_suf
    bcot_pre = mid_pre.astype(jnp.bfloat16)
    bcot_suf = mid_suf.astype(jnp.bfloat16)
    out_w_pre = outer_sum(att_pre, bcot_pre)
    out_w_suf = outer_sum(att_suf, bcot_suf)
    acot_pre = (
        project_back(bcot_pre, back_po)
        .astype(jnp.bfloat16)
        .reshape(pre_items, half_rows, heads_local, head_size)
    )
    acot_suf = (
        project_back(bcot_suf, back_ao)
        .astype(jnp.bfloat16)
        .reshape(suf_items, suf_len, heads_local, head_size)
    )
    qcot_pre, kvcot_pre = attend_back(
        queries_pre, keyval_back, pre_allowed, scale, head_size, logsum_pre, acot_pre
    )
    qcot_suf, kvcot_suf = attend_back(
        queries_suf, suffix_keys(keyval_back), suf_allowed, scale, head_size, logsum_suf, acot_suf
    )
    key_terms = kvcot_pre + lax.dynamic_update_slice_in_dim(
        jnp.zeros_like(kvcot_pre), kvcot_suf[:, :full_len], group * suf_items, 0
    )
    key_half = lax.psum_scatter(key_terms, "expert", scatter_dimension=1, tiled=True)
    qcot_pre = qcot_pre.astype(jnp.bfloat16).reshape(pre_items * half_rows, heads_local * head_size)
    qcot_suf = qcot_suf.astype(jnp.bfloat16).reshape(suf_items * suf_len, heads_local * head_size)
    query_w_pre = outer_sum(normed_pre, qcot_pre)
    query_w_suf = outer_sum(normed_suf, qcot_suf)
    key_half, key_own, ncot_pre, ncot_suf = lax.psum(
        (
            key_half,
            kvcot_suf[:, full_len:],
            project_back(qcot_pre, back_pq),
            project_back(qcot_suf, back_aq),
        ),
        "tp",
    )
    key_half = key_half.astype(jnp.bfloat16).reshape(pre_items * half_rows, 2 * head_size)
    key_own = key_own.astype(jnp.bfloat16).reshape(suf_items * suf_len, 2 * head_size)
    keyval_w_pre = outer_sum(normed_pre, key_half)
    keyval_w_suf = outer_sum(normed_suf, key_own)
    ncot_pre = ncot_pre + project_back(key_half, back_pkv)
    ncot_suf = ncot_suf + project_back(key_own, back_akv)
    in_part_pre, attn_gain_pre = norm_back(prefix_x, back_gpa, ncot_pre)
    in_part_suf, attn_gain_suf = norm_back(suffix_x, back_gaa, ncot_suf)
    prefix_grad = (mid_pre + in_part_pre).reshape(pre_items, half_rows, width)
    suffix_grad = (mid_suf + in_part_suf).reshape(suf_items, suf_len, act_width)
    embed_w = jnp.einsum(
        "ita,itd->ad",
        chosen.astype(jnp.float32),
        suffix_grad[:, 1:],
        precision=lax.Precision.HIGHEST,
    )
    g_pq, g_pkv, g_pg, g_pu, g_aq, g_akv, g_ag, g_au, g_embed, g_gpa, g_gpf, g_gaa, g_gaf = (
        lax.psum_scatter(query_w_pre, ("dp", "expert"), scatter_dimension=0, tiled=True),
        lax.psum_scatter(keyval_w_pre, ("dp", "expert"), scatter_dimension=0, tiled=True),
        lax.psum_scatter(gate_w_pre, ("dp", "expert"), scatter_dimension=0, tiled=True),
        lax.psum_scatter(up_w_pre, ("dp", "expert"), scatter_dimension=0, tiled=True),
        lax.psum_scatter(query_w_suf, ("dp", "expert"), scatter_dimension=0, tiled=True),
        lax.psum_scatter(keyval_w_suf, ("dp", "expert"), scatter_dimension=0, tiled=True),
        lax.psum_scatter(gate_w_suf, ("dp", "expert"), scatter_dimension=0, tiled=True),
        lax.psum_scatter(up_w_suf, ("dp", "expert"), scatter_dimension=0, tiled=True),
        lax.psum_scatter(embed_w, ("dp", "expert"), scatter_dimension=0, tiled=True),
        lax.psum_scatter(attn_gain_pre, ("dp", "expert"), scatter_dimension=0, tiled=True),
        lax.psum_scatter(ffn_gain_pre, ("dp", "expert"), scatter_dimension=0, tiled=True),
        lax.psum_scatter(attn_gain_suf, ("dp", "expert"), scatter_dimension=0, tiled=True),
        lax.psum_scatter(ffn_gain_suf, ("dp", "expert"), scatter_dimension=0, tiled=True),
    )
    g_po, g_pd, g_ao, g_ad = (
        lax.psum_scatter(out_w_pre, ("dp", "expert"), scatter_dimension=1, tiled=True),
        lax.psum_scatter(down_pre, ("dp", "expert"), scatter_dimension=1, tiled=True),
        lax.psum_scatter(out_w_suf, ("dp", "expert"), scatter_dimension=1, tiled=True),
        lax.psum_scatter(down_suf, ("dp", "expert"), scatter_dimension=1, tiled=True),
    )
    return (
        prefix_out,
        suffix_out,
        prefix_grad,
        suffix_grad,
        g_pq,
        g_pkv,
        g_po,
        g_pg,
        g_pu,
        g_pd,
        g_gpa,
        g_gpf,
        g_aq,
        g_akv,
        g_ao,
        g_ag,
        g_au,
        g_ad,
        g_gaa,
        g_gaf,
        g_embed,
    )


def solution(mesh):
    return jax.shard_map(
        local,
        mesh=mesh,
        in_specs=(
            P("dp", "expert", None),
            P(("dp", "expert"), None, None),
            P(("dp", "expert"), None, None),
            P("dp"),
            P(("dp", "expert"), None),
            P(("dp", "expert"), "tp"),
            P(("dp", "expert"), None),
            P("tp", ("dp", "expert")),
            P(("dp", "expert"), "tp"),
            P(("dp", "expert"), "tp"),
            P("tp", ("dp", "expert")),
            P(("dp", "expert")),
            P(("dp", "expert")),
            P(("dp", "expert"), "tp"),
            P(("dp", "expert"), None),
            P("tp", ("dp", "expert")),
            P(("dp", "expert"), "tp"),
            P(("dp", "expert"), "tp"),
            P("tp", ("dp", "expert")),
            P(("dp", "expert")),
            P(("dp", "expert")),
            P(("dp", "expert"), None),
            P("dp", "expert", None),
            P(("dp", "expert"), None, None),
        ),
        out_specs=(
            P("dp", "expert", None),
            P(("dp", "expert"), None, None),
            P("dp", "expert", None),
            P(("dp", "expert"), None, None),
            P(("dp", "expert"), "tp"),
            P(("dp", "expert"), None),
            P("tp", ("dp", "expert")),
            P(("dp", "expert"), "tp"),
            P(("dp", "expert"), "tp"),
            P("tp", ("dp", "expert")),
            P(("dp", "expert")),
            P(("dp", "expert")),
            P(("dp", "expert"), "tp"),
            P(("dp", "expert"), None),
            P("tp", ("dp", "expert")),
            P(("dp", "expert"), "tp"),
            P(("dp", "expert"), "tp"),
            P("tp", ("dp", "expert")),
            P(("dp", "expert")),
            P(("dp", "expert")),
            P(("dp", "expert"), None),
        ),
        check_vma=False,
    )
```

profile of v0, /device:TPU:0, one launch (start us, length us, event | category | flops | bytes accessed | tf_op | source)
XLA Modules:
  0.0 4157.7 jit_solution(15135756747529524800)
XLA Ops:
  10.7 22.3 all-gather
  38.5 23.7 all-gather.19.cloned.1.call-done
  68.2 30.6 all-gather.2
  98.9 17.9 all-gather.3
  119.6 24.6 all-gather.33.cloned.1.call-done
  145.8 48.5 %all-gather.23.cloned.1.call-done = bf16[2048,512]{1,0:T(8,128)(2,1)} async-done(((bf16[256,512]{1,0:T(8,128)(2,1)}), bf16[2048,512]{1,0:T(8,128)(2,1)}) %all-gather.23.cloned.1.call-update) | async-done | bytes 2097168 | tf_op jit(solution)/shard_map/all_gather | solution.py:132
  200.8 16.8 all-gather.21.cloned.1.call-done
  224.0 46.6 %all-gather.25.cloned.1.call-done = bf16[512,2048]{1,0:T(8,128)(2,1)} async-done(((bf16[512,256]{1,0:T(8,128)(2,1)}), bf16[512,2048]{1,0:T(8,128)(2,1)}) %all-gather.25.cloned.1.call-update) | async-done | bytes 2097168 | tf_op jit(solution)/shard_map/all_gather | solution.py:145
  275.8 34.6 all-gather.37.cloned.1.call-done
  316.7 18.5 all-gather.1
  335.2 26.6 all-gather.4
  361.8 49.1 %all-reduce.23.cloned.1.call-done = (f32[576,2048]{1,0:T(8,128)}, f32[51,1024]{1,0:T(8,128)}) async-done(((f32[576,2048]{1,0:T(8,128)}, f32[51,1024]{1,0:T(8,128)}), (f32[576,2048]{1,0:T(8,128)}, f32[51,1024]{1,0:T(8,128)})) %all-reduce.23.cloned.1.call-update) | async-done | bytes 4927504 | tf_op jit(solution)/shard_map/psum | solution.py:98
  417.3 45.4 %all-gather.39.cloned.1.call-done = bf16[1024,1024]{1,0:T(8,128)(2,1)} async-done(((bf16[128,1024]{1,0:T(8,128)(2,1)}), bf16[1024,1024]{1,0:T(8,128)(2,1)}) %all-gather.39.cloned.1.call-update) | async-done | bytes 2097168 | tf_op jit(solution)/shard_map/all_gather | solution.py:138
  464.8 47.9 %all-gather.41.cloned.1.call-done = bf16[1024,1024]{1,0:T(8,128)(2,1)} async-done(((bf16[128,1024]{1,0:T(8,128)(2,1)}), bf16[1024,1024]{1,0:T(8,128)(2,1)}) %all-gather.41.cloned.1.call-update) | async-done | bytes 2097168 | tf_op jit(solution)/shard_map/all_gather | solution.py:139
  514.8 49.8 %all-gather.43.cloned.1.call-done = bf16[1024,1024]{1,0:T(8,128)(2,1)} async-done(((bf16[1024,128]{1,0:T(8,128)(2,1)}), bf16[1024,1024]{1,0:T(8,128)(2,1)}) %all-gather.43.cloned.1.call-update) | async-done | bytes 2097168 | tf_op jit(solution)/shard_map/all_gather | solution.py:148
  572.2 220.4 %all-gather.27.cloned.1.call-done = bf16[2048,4096]{1,0:T(8,128)(2,1)} async-done(((bf16[256,4096]{1,0:T(8,128)(2,1)}), bf16[2048,4096]{1,0:T(8,128)(2,1)}) %all-gather.27.cloned.1.call-update) | async-done | bytes 16777232 | tf_op jit(solution)/shard_map/all_gather | solution.py:134
  792.6 15.6 fusion.109
  808.3 212.6 %all-gather.29.cloned.1.call-done = bf16[2048,4096]{1,0:T(8,128)(2,1)} async-done(((bf16[256,4096]{1,0:T(8,128)(2,1)}), bf16[2048,4096]{1,0:T(8,128)(2,1)}) %all-gather.29.cloned.1.call-update) | async-done | bytes 16777232 | tf_op jit(solution)/shard_map/all_gather | solution.py:135
  1020.8 16.4 fusion.110
  1037.2 211.7 %all-gather.31.cloned.1.call-done = bf16[4096,2048]{1,0:T(8,128)(2,1)} async-done(((bf16[4096,256]{1,0:T(8,128)(2,1)}), bf16[4096,2048]{1,0:T(8,128)(2,1)}) %all-gather.31.cloned.1.call-update) | async-done | bytes 16777232 | tf_op jit(solution)/shard_map/all_gather | solution.py:146
  1248.9 26.8 multiply_convert_fusion
  1275.6 16.6 fusion.116
  1292.3 15.7 convolution_add_fusion.1
  1310.8 93.5 %all-reduce.21.cloned.1.call-done = (f32[576,2048]{1,0:T(8,128)}, f32[51,1024]{1,0:T(8,128)}) async-done(((f32[576,2048]{1,0:T(8,128)}, f32[51,1024]{1,0:T(8,128)}), (f32[576,2048]{1,0:T(8,128)}, f32[51,1024]{1,0:T(8,128)})) %all-reduce.21.cloned.1.call-update) | async-done | bytes 4927504 | tf_op jit(solution)/shard_map/psum | solution.py:281
  1411.5 5.6 multiply_reduce_fusion
  1437.4 16.4 fusion.111
  1462.3 9.9 reduce-scatter.14.cloned.1.call-done
  1472.2 46.8 %all-reduce.24 = (bf16[2,288,512]{2,1,0:T(8,128)(2,1)}, bf16[1,51,512]{2,1,0:T(8,128)(2,1)S(1)}) all-reduce(f32[2,288,512]{2,1,0:T(8,128)} %reduce-scatter.14.cloned.1.call-done, f32[1,51,512]{2,1,0:T(8,128)} %pad_maximum_fusion.2), channel_id=1, replica_groups=mesh['dp'=4,'tp'=4,'expert'=2] {'tp'}, use_global_device_ids=true, to_apply=%region_20.21 | all-reduce | flops 321024 | bytes 1926144 | tf_op jit(solution)/shard_map/psum | solution.py:314
  1519.0 150.7 %all-reduce.19.cloned.1.call-done = (f32[576,2048]{1,0:T(8,128)}, f32[51,1024]{1,0:T(8,128)}, f32[576,2048]{1,0:T(8,128)}, f32[51,1024]{1,0:T(8,128)}) async-done(((f32[576,2048]{1,0:T(8,128)}, f32[51,1024]{1,0:T(8,128)}, f32[576,2048]{1,0:T(8,128)}, f32[51,1024]{1,0:T(8,128)}), (f32[576,2048]{1,0:T(8,128)}, f32[51,1024]{1,0:T(8,128)}, f32[576,2048]{1,0:T(8,128)}, ...) | async-done | bytes 9854992 | tf_op jit(solution)/shard_map/psum | solution.py:98
  1694.8 6.2 fusion.34
  1709.5 21.6 fusion.121
  1731.7 21.7 fusion.122
  1753.6 22.0 fusion.123
  1779.8 7.1 multiply_reduce_fusion.1
  1786.9 37.5 all-reduce.6
  1827.6 6.4 add_convert_fusion
  1834.0 5.7 fusion.8
  1841.2 86.2 %reduce-scatter.36.cloned.1.call-done = f32[128,1024]{1,0:T(8,128)} async-done(((f32[1024,1024]{1,0:T(8,128)}), f32[128,1024]{1,0:T(8,128)}) %reduce-scatter.36.cloned.1.call-update) | async-done | bytes 524304 | tf_op jit(solution)/shard_map/reduce_scatter | solution.py:347
  1927.3 92.7 %reduce-scatter.38.cloned.1.call-done = f32[1024,128]{1,0:T(8,128)} async-done(((f32[1024,1024]{1,0:T(8,128)}), f32[1024,128]{1,0:T(8,128)}) %reduce-scatter.38.cloned.1.call-update) | async-done | bytes 524304 | tf_op jit(solution)/shard_map/reduce_scatter | solution.py:358
  2020.0 71.5 %reduce-scatter.28.cloned.1.call-done = f32[128,512]{1,0:T(8,128)} async-done(((f32[1024,512]{1,0:T(8,128)}), f32[128,512]{1,0:T(8,128)}) %reduce-scatter.28.cloned.1.call-update) | async-done | bytes 262160 | tf_op jit(solution)/shard_map/reduce_scatter | solution.py:344
  2091.5 71.4 %reduce-scatter.32.cloned.1.call-done = f32[512,128]{1,0:T(8,128)} async-done(((f32[512,1024]{1,0:T(8,128)}), f32[512,128]{1,0:T(8,128)}) %reduce-scatter.32.cloned.1.call-update) | async-done | bytes 262160 | tf_op jit(solution)/shard_map/reduce_scatter | solution.py:357
  2162.9 91.1 %reduce-scatter.16.cloned.1.call-done = f32[256,512]{1,0:T(8,128)} async-done(((f32[2048,512]{1,0:T(8,128)}), f32[256,512]{1,0:T(8,128)}) %reduce-scatter.16.cloned.1.call-update) | async-done | bytes 524304 | tf_op jit(solution)/shard_map/reduce_scatter | solution.py:340
  2254.0 92.7 %reduce-scatter.20.cloned.1.call-done = f32[512,256]{1,0:T(8,128)} async-done(((f32[512,2048]{1,0:T(8,128)}), f32[512,256]{1,0:T(8,128)}) %reduce-scatter.20.cloned.1.call-update) | async-done | bytes 524304 | tf_op jit(solution)/shard_map/reduce_scatter | solution.py:355
  2346.7 71.3 %reduce-scatter.30.cloned.1.call-done = f32[128,512]{1,0:T(8,128)} async-done(((f32[1024,512]{1,0:T(8,128)}), f32[128,512]{1,0:T(8,128)}) %reduce-scatter.30.cloned.1.call-update) | async-done | bytes 262160 | tf_op jit(solution)/shard_map/reduce_scatter | solution.py:345
  2418.0 91.1 %reduce-scatter.18.cloned.1.call-done = f32[256,512]{1,0:T(8,128)} async-done(((f32[2048,512]{1,0:T(8,128)}), f32[256,512]{1,0:T(8,128)}) %reduce-scatter.18.cloned.1.call-update) | async-done | bytes 524304 | tf_op jit(solution)/shard_map/reduce_scatter | solution.py:341
  2509.1 547.9 %reduce-scatter.22.cloned.1.call-done = f32[256,4096]{1,0:T(8,128)} async-done(((f32[2048,4096]{1,0:T(8,128)}), f32[256,4096]{1,0:T(8,128)}) %reduce-scatter.22.cloned.1.call-update) | async-done | bytes 4194320 | tf_op jit(solution)/shard_map/reduce_scatter | solution.py:342
  3056.9 547.0 %reduce-scatter.24.cloned.1.call-done = f32[256,4096]{1,0:T(8,128)} async-done(((f32[2048,4096]{1,0:T(8,128)}), f32[256,4096]{1,0:T(8,128)}) %reduce-scatter.24.cloned.1.call-update) | async-done | bytes 4194320 | tf_op jit(solution)/shard_map/reduce_scatter | solution.py:343
  3603.9 546.7 %reduce-scatter.26.cloned.1.call-done = f32[4096,256]{1,0:T(8,128)} async-done(((f32[4096,2048]{1,0:T(8,128)}), f32[4096,256]{1,0:T(8,128)}) %reduce-scatter.26.cloned.1.call-update) | async-done | bytes 4194320 | tf_op jit(solution)/shard_map/reduce_scatter | solution.py:356
  (390 shorter events, 140.4 us)
Async XLA Ops:
  7.2 55.0 %all-gather.19.cloned.1.call-start = ((), (), s32[]{:S(2)}) async-start(), calls=%async_computation.13 | async-start | bytes 2359296 | tf_op jit(solution)/shard_map/all_gather | solution.py:133
  7.9 110.0 %all-gather.35.cloned.1.call-start = ((), (), s32[]{:S(2)}) async-start(), calls=%async_computation.21 | async-start | bytes 1179648 | tf_op jit(solution)/shard_map/all_gather | solution.py:136
  8.7 135.6 %all-gather.33.cloned.1.call-start = ((), (), s32[]{:S(2)}) async-start(), calls=%async_computation.20 | async-start | bytes 1179648 | tf_op jit(solution)/shard_map/all_gather | solution.py:137
  9.4 184.9 %all-gather.23.cloned.1.call-start = ((), (), s32[]{:S(2)}) async-start(), calls=%async_computation.15 | async-start | bytes 2359296 | tf_op jit(solution)/shard_map/all_gather | solution.py:132
  10.0 207.6 %all-gather.21.cloned.1.call-start = ((), (), s32[]{:S(2)}) async-start(), calls=%async_computation.14 | async-start | bytes 1769472 | tf_op jit(solution)/shard_map/all_gather | solution.py:204
  66.7 203.9 %all-gather.25.cloned.1.call-start = ((), (), s32[]{:S(2)}) async-start(), calls=%async_computation.16 | async-start | bytes 2359296 | tf_op jit(solution)/shard_map/all_gather | solution.py:145
  67.3 243.1 %all-gather.37.cloned.1.call-start = ((), (), s32[]{:S(2)}) async-start(), calls=%async_computation.22 | async-start | bytes 1179648 | tf_op jit(solution)/shard_map/all_gather | solution.py:147
  68.0 342.8 %all-reduce.23.cloned.1.call-start = ((), (), s32[]{:S(2)}) async-start(), calls=%async_computation.42 | async-start | bytes 9895936 | tf_op jit(solution)/shard_map/psum | solution.py:98
  117.3 293.6 %copy-start.6 = (f32[1,51,1024]{2,1,0:T(8,128)}, f32[1,51,1024]{2,1,0:T(8,128)S(1)}, u32[]{:S(2)}) copy-start(f32[1,51,1024]{2,1,0:T(8,128)S(1)} %get-tuple-element.111) | copy-start | bytes 626692
  312.6 150.1 %all-gather.39.cloned.1.call-start = ((), (), s32[]{:S(2)}) async-start(), calls=%async_computation.23 | async-start | bytes 2359296 | tf_op jit(solution)/shard_map/all_gather | solution.py:138
  313.4 199.4 %all-gather.41.cloned.1.call-start = ((), (), s32[]{:S(2)}) async-start(), calls=%async_computation.24 | async-start | bytes 2359296 | tf_op jit(solution)/shard_map/all_gather | solution.py:139
  314.0 250.6 %all-gather.43.cloned.1.call-start = ((), (), s32[]{:S(2)}) async-start(), calls=%async_computation.25 | async-start | bytes 2359296 | tf_op jit(solution)/shard_map/all_gather | solution.py:148
  314.7 477.9 %all-gather.27.cloned.1.call-start = ((), (), s32[]{:S(2)}) async-start(), calls=%async_computation.17 | async-start | bytes 18874368 | tf_op jit(solution)/shard_map/all_gather | solution.py:134
  315.3 705.5 %all-gather.29.cloned.1.call-start = ((), (), s32[]{:S(2)}) async-start(), calls=%async_computation.18 | async-start | bytes 18874368 | tf_op jit(solution)/shard_map/all_gather | solution.py:135
  316.0 932.8 %all-gather.31.cloned.1.call-start = ((), (), s32[]{:S(2)}) async-start(), calls=%async_computation.19 | async-start | bytes 18874368 | tf_op jit(solution)/shard_map/all_gather | solution.py:146
  316.6 1087.6 %all-reduce.21.cloned.1.call-start = ((), (), s32[]{:S(2)}) async-start(), calls=%async_computation.41 | async-start | bytes 9895936 | tf_op jit(solution)/shard_map/psum | solution.py:281
  412.0 993.9 %copy-start.25 = (f32[51,1024]{1,0:T(8,128)}, f32[51,1024]{1,0:T(8,128)S(1)}, u32[]{:S(2)}) copy-start(f32[51,1024]{1,0:T(8,128)S(1)} %get-tuple-element.107) | copy-start | bytes 626692
  417.2 147.4 %copy-start.47 = (bf16[1,51,1024]{2,1,0:T(8,128)(2,1)S(1)}, bf16[1,51,1024]{2,1,0:T(8,128)(2,1)}, u32[]{:S(2)}) copy-start(bf16[1,51,1024]{2,1,0:T(8,128)(2,1)} %param.47) | copy-start | bytes 313348
  417.3 149.8 %copy-start.32 = (bf16[51,1024]{1,0:T(8,128)(2,1)}, bf16[51,1024]{1,0:T(8,128)(2,1)S(1)}, u32[]{:S(2)}) copy-start(bf16[51,1024]{1,0:T(8,128)(2,1)S(1)} %multiply_convert_fusion.9) | copy-start | bytes 313348
  567.2 741.5 %copy-start.49 = (bf16[51,1024]{1,0:T(8,128)(2,1)}, bf16[51,1024]{1,0:T(8,128)(2,1)S(1)}, u32[]{:S(2)}) copy-start(bf16[51,1024]{1,0:T(8,128)(2,1)S(1)} %get-tuple-element.117) | copy-start | bytes 313348
  572.2 220.4 %copy-start.38 = (bf16[576,2048]{1,0:T(8,128)(2,1)}, bf16[576,2048]{1,0:T(8,128)(2,1)S(1)}, u32[]{:S(2)}) copy-start(bf16[576,2048]{1,0:T(8,128)(2,1)S(1)} %multiply_convert_fusion.3) | copy-start | bytes 7077892
  808.2 440.6 %copy-start.34 = (bf16[2,288,2048]{2,1,0:T(8,128)(2,1)S(1)}, bf16[2,288,2048]{2,1,0:T(8,128)(2,1)}, u32[]{:S(2)}) copy-start(bf16[2,288,2048]{2,1,0:T(8,128)(2,1)} %param.46) | copy-start | bytes 7077892
  1308.0 164.2 %reduce-scatter.14.cloned.1.call-start = ((), (), s32[]{:S(2)}) async-start(), calls=%async_computation.26 | async-start | bytes 3538944 | tf_op jit(solution)/shard_map/reduce_scatter | solution.py:309
  1437.2 232.5 %all-reduce.19.cloned.1.call-start = ((), (), s32[]{:S(2)}) async-start(), calls=%async_computation.40 | async-start | bytes 19791872 | tf_op jit(solution)/shard_map/psum | solution.py:98
  1460.4 209.3 %copy-start.7 = (f32[1,51,1024]{2,1,0:T(8,128)S(1)}, f32[1,51,1024]{2,1,0:T(8,128)}, u32[]{:S(2)}) copy-start(f32[1,51,1024]{2,1,0:T(8,128)} %copy-done.6) | copy-start | bytes 626692
  1460.4 209.3 %copy-start.71 = (f32[8,1,128]{2,1,0:T(1,128)S(1)}, f32[8,1,128]{2,1,0:T(1,128)}, u32[]{:S(2)}) copy-start(f32[8,1,128]{2,1,0:T(1,128)} %copy-done.70) | copy-start | bytes 12292
  1460.4 209.3 %copy-start.85 = (f32[51]{0:T(128)S(1)}, f32[51]{0:T(128)}, u32[]{:S(2)}) copy-start(f32[51]{0:T(128)} %copy-done.84) | copy-start | bytes 616
  1460.4 209.3 %copy-start.28 = (bf16[1024,512]{1,0:T(8,128)(2,1)S(1)}, bf16[1024,512]{1,0:T(8,128)(2,1)}, u32[]{:S(2)}) copy-start(bf16[1024,512]{1,0:T(8,128)(2,1)} %all-gather.33.cloned.1.call-done) | copy-start | bytes 3145732
  1460.4 210.8 %copy-start.100 = (f32[51]{0:T(128)S(1)}, f32[51]{0:T(128)}, u32[]{:S(2)}) copy-start(f32[51]{0:T(128)} %copy-done.99) | copy-start | bytes 616
  1460.4 210.8 %copy-start.31 = (f32[51,1024]{1,0:T(8,128)S(1)}, f32[51,1024]{1,0:T(8,128)}, u32[]{:S(2)}) copy-start(f32[51,1024]{1,0:T(8,128)} %copy-done.30) | copy-start | bytes 626692
  1460.5 211.6 %copy-start.78 = (bf16[1,50,32]{1,2,0:T(8,128)(2,1)S(1)}, bf16[1,50,32]{1,2,0:T(8,128)(2,1)}, u32[]{:S(2)}) copy-start(bf16[1,50,32]{1,2,0:T(8,128)(2,1)} %param.26) | copy-start | bytes 9604
  1460.5 211.6 %copy-start.95 = (pred[32]{0:T(512)(128)(4,1)S(1)}, pred[32]{0:T(512)(128)(4,1)}, u32[]{:S(2)}) copy-start(pred[32]{0:T(512)(128)(4,1)} %copy-done.94) | copy-start | bytes 100
  1460.5 212.6 %copy-start.33 = (bf16[51,1024]{1,0:T(8,128)(2,1)S(1)}, bf16[51,1024]{1,0:T(8,128)(2,1)}, u32[]{:S(2)}) copy-start(bf16[51,1024]{1,0:T(8,128)(2,1)} %copy-done.32) | copy-start | bytes 313348
  1460.5 379.3 %all-reduce.17.cloned.1.call-start = ((), (), s32[]{:S(2)}) async-start(), calls=%async_computation.39 | async-start | bytes 262144
  1462.3 210.7 %copy-start.52 = (bf16[51,1024]{1,0:T(8,128)(2,1)S(1)}, bf16[51,1024]{1,0:T(8,128)(2,1)}, u32[]{:S(2)}) copy-start(bf16[51,1024]{1,0:T(8,128)(2,1)} %copy-done.51) | copy-start | bytes 313348
  1519.0 156.8 %copy-start.66 = (bf16[1,51,512]{2,1,0:T(8,128)(2,1)}, bf16[1,51,512]{2,1,0:T(8,128)(2,1)S(1)}, u32[]{:S(2)}) copy-start(bf16[1,51,512]{2,1,0:T(8,128)(2,1)S(1)} %get-tuple-element.97) | copy-start | bytes 156676
  1673.0 168.2 %reduce-scatter.34.cloned.1.call-start = ((), (), s32[]{:S(2)}) async-start(), calls=%async_computation.36 | async-start | bytes 4718592 | tf_op jit(solution)/shard_map/reduce_scatter | solution.py:346
  1675.8 251.5 %reduce-scatter.36.cloned.1.call-start = ((), (), s32[]{:S(2)}) async-start(), calls=%async_computation.37 | async-start | bytes 4718592 | tf_op jit(solution)/shard_map/reduce_scatter | solution.py:347
  1679.4 340.6 %reduce-scatter.38.cloned.1.call-start = ((), (), s32[]{:S(2)}) async-start(), calls=%async_computation.38 | async-start | bytes 4718592 | tf_op jit(solution)/shard_map/reduce_scatter | solution.py:358
  1683.0 408.5 %reduce-scatter.28.cloned.1.call-start = ((), (), s32[]{:S(2)}) async-start(), calls=%async_computation.33 | async-start | bytes 2359296 | tf_op jit(solution)/shard_map/reduce_scatter | solution.py:344
  1685.7 477.2 %reduce-scatter.32.cloned.1.call-start = ((), (), s32[]{:S(2)}) async-start(), calls=%async_computation.35 | async-start | bytes 2359296 | tf_op jit(solution)/shard_map/reduce_scatter | solution.py:357
  1687.6 566.4 %reduce-scatter.16.cloned.1.call-start = ((), (), s32[]{:S(2)}) async-start(), calls=%async_computation.27 | async-start | bytes 4718592 | tf_op jit(solution)/shard_map/reduce_scatter | solution.py:340
  1693.8 652.9 %reduce-scatter.20.cloned.1.call-start = ((), (), s32[]{:S(2)}) async-start(), calls=%async_computation.29 | async-start | bytes 4718592 | tf_op jit(solution)/shard_map/reduce_scatter | solution.py:355
  1701.0 717.0 %reduce-scatter.30.cloned.1.call-start = ((), (), s32[]{:S(2)}) async-start(), calls=%async_computation.34 | async-start | bytes 2359296 | tf_op jit(solution)/shard_map/reduce_scatter | solution.py:345
  1703.7 805.4 %reduce-scatter.18.cloned.1.call-start = ((), (), s32[]{:S(2)}) async-start(), calls=%async_computation.28 | async-start | bytes 4718592 | tf_op jit(solution)/shard_map/reduce_scatter | solution.py:341
  1709.2 1347.7 %reduce-scatter.22.cloned.1.call-start = ((), (), s32[]{:S(2)}) async-start(), calls=%async_computation.30 | async-start | bytes 37748736 | tf_op jit(solution)/shard_map/reduce_scatter | solution.py:342
  1731.1 1872.8 %reduce-scatter.24.cloned.1.call-start = ((), (), s32[]{:S(2)}) async-start(), calls=%async_computation.31 | async-start | bytes 37748736 | tf_op jit(solution)/shard_map/reduce_scatter | solution.py:343
  1753.4 2397.2 %reduce-scatter.26.cloned.1.call-start = ((), (), s32[]{:S(2)}) async-start(), calls=%async_computation.32 | async-start | bytes 37748736 | tf_op jit(solution)/shard_map/reduce_scatter | solution.py:356
  (91 other events, 1683.2 us)
Sparse Core Ops, SparseCore 0:
  10.2 51.9 all-gather.18
  64.3 38.8 all-gather.34
  105.3 38.8 all-gather.32
  146.2 48.0 all-gather.22
  196.3 21.2 all-gather.20
  219.5 51.0 all-gather.24
  272.6 37.7 all-gather.36
  314.0 96.7 all-reduce.22
  413.2 49.4 all-gather.38
  464.9 47.7 all-gather.40
  515.0 49.5 all-gather.42
  566.8 225.8 all-gather.26
  795.0 225.7 all-gather.28
  1022.9 225.9 all-gather.30
  1308.1 96.0 all-reduce.20
  1437.3 34.8 reduce-scatter.13
  1475.6 194.0 all-reduce.18
  1673.1 69.7 all-reduce.16
  1747.5 87.7 reduce-scatter.33
  1839.4 87.8 reduce-scatter.35
  1932.0 88.0 reduce-scatter.37
  2024.1 67.3 reduce-scatter.27
  2095.6 67.2 reduce-scatter.31
  2166.9 87.0 reduce-scatter.15
  2258.6 88.0 reduce-scatter.19
  2350.7 67.3 reduce-scatter.29
  2422.1 86.9 reduce-scatter.17
  2513.9 543.0 reduce-scatter.21
  3061.8 542.0 reduce-scatter.23
  3608.6 542.0 reduce-scatter.25
where the time goes:
time: 4170 us; the launch traced here: 4160 us
  waiting for transfers between devices  3600 us (86%)
  matrix products  262 us (6%)
  blocking collectives  200 us (5%)
  other arithmetic  42.7 us (1%)
    reduce_scatter x1, waiting for transfers between devices, local(): lax.psum_scatter(gate_w_pre, ('dp', 'expert'), scatter_dimension=0, tiled...  548 us
    reduce_scatter x1, waiting for transfers between devices, local(): lax.psum_scatter(up_w_pre, ('dp', 'expert'), scatter_dimension=0, tiled=T...  547 us
    reduce_scatter x1, waiting for transfers between devices, local(): lax.psum_scatter(down_pre, ('dp', 'expert'), scatter_dimension=1, tiled=T...  547 us
    all_gather x1, waiting for transfers between devices, local(): lax.all_gather(pre_gate, ('dp', 'expert'), axis=0, tiled=True)  220 us
    all_gather x1, waiting for transfers between devices, local(): lax.all_gather(pre_up, ('dp', 'expert'), axis=0, tiled=True)  213 us
    all_gather x1, waiting for transfers between devices, local(): lax.all_gather(pre_down, ('dp', 'expert'), axis=1, tiled=True)  212 us
    psum x2, waiting for transfers between devices, head_sums(): return lax.psum((first, second), 'tp')  200 us
    dot_general x12, matrix products, outer_sum(): lax.dot_general(left, right, (((0,), (0,)), ((), ())), preferred_element_...  94.4 us
  transfers between devices with their start and end apart: 30, of which 27 were waited for; matrix products, arithmetic and copies ran while one was open for 5% of the time, Pallas kernels for 0%

commit v1 on v0

v1 whole, which is shorter than its diff:
```python
import functools

import jax
import jax.numpy as jnp
from jax import lax
from jax.sharding import PartitionSpec as P

HD = 256
EPSILON = 1e-06
PAD = 64
F32 = jnp.float32
BF16 = jnp.bfloat16


def rms_scale(values, gain):
    return values * lax.rsqrt(jnp.mean(values * values, axis=-1, keepdims=True) + EPSILON) * gain


def gelu_tanh(values):
    return jax.nn.gelu(values, approximate=True)


def geglu(gate, upward):
    return gelu_tanh(gate) * upward


def project(left, right):
    return jnp.dot(left, right, preferred_element_type=F32)


def project_back(left, right):
    return lax.dot_general(left, right, (((1,), (1,)), ((), ())), preferred_element_type=F32)


def outer_sum(left, right):
    return lax.dot_general(left, right, (((0,), (0,)), ((), ())), preferred_element_type=F32)


def norm_back(values, gain, cotangent):
    return jax.vjp(rms_scale, values, gain.astype(F32))[1](cotangent)


def attend(queries, keys, values, allowed, scale):
    scores = jnp.einsum("bqhe,bke->bhqk", queries, keys, preferred_element_type=F32) * scale
    masked = jnp.where(allowed[:, None], scores, -1e30)
    expo = jnp.exp(masked - jnp.max(masked, axis=-1, keepdims=True))
    probs = expo / jnp.sum(expo, axis=-1, keepdims=True)
    attended = jnp.einsum(
        "bhqk,bke->bqhe", probs.astype(BF16), values, preferred_element_type=F32
    )
    return attended.astype(BF16), probs


def attend_back(queries, keys, values, probs, grad_att, scale):
    grad_probs = jnp.einsum("bqhe,bke->bhqk", grad_att, values, preferred_element_type=F32)
    delta = jnp.sum(probs * grad_probs, axis=-1, keepdims=True)
    grad_scores = (probs * (grad_probs - delta)).astype(BF16)
    grad_queries = jnp.einsum("bhqk,bke->bqhe", grad_scores, keys, preferred_element_type=F32)
    grad_keys = jnp.einsum("bhqk,bqhe->bke", grad_scores, queries, preferred_element_type=F32)
    grad_values = jnp.einsum(
        "bhqk,bqhe->bke", probs.astype(BF16), grad_att, preferred_element_type=F32
    )
    return grad_queries * scale, grad_keys * scale, grad_values


def swap(value, axis, size, mask):
    return lax.ppermute(value, axis, [(i, i ^ mask) for i in range(size)])


def column_blocks(value, count):
    width = value.shape[1] // count
    return [value[:, i * width : (i + 1) * width] for i in range(count)]


def halves_down(value, axis):
    other = value.ndim - 1 if axis == value.ndim - 2 else value.ndim - 2
    size = value.shape[axis] // 2
    first = lax.slice_in_dim(value, 0, size, axis=axis)
    second = lax.slice_in_dim(value, size, 2 * size, axis=axis)
    return jnp.concatenate([first, second], axis=other)


def after(*values):
    return lax.optimization_barrier(values)


def own_first(value, dp, group):
    blocks = column_blocks(value, 2 * dp)
    even, odd = blocks[0::2], blocks[1::2]
    own = [jnp.where(group == 0, a, b) for a, b in zip(even, odd)]
    other = [jnp.where(group == 0, b, a) for a, b in zip(even, odd)]
    return jnp.concatenate(own + other, axis=1)


def own_first_undo(value, dp, group):
    blocks = column_blocks(value, 2 * dp)
    own, other = blocks[:dp], blocks[dp:]
    out = []
    for a, b in zip(own, other):
        out += [jnp.where(group == 0, a, b), jnp.where(group == 0, b, a)]
    return jnp.concatenate(out, axis=1)


class Rows:
    def __init__(self, part, suf_part, dp, core, x_index):
        self.part, self.dp, self.core, self.x_index = part, dp, core, x_index
        self.suf_part = suf_part
        self.size = part + suf_part // 2

    def pack(self, pre, suf):
        return jnp.concatenate([pre, halves_down(suf, 0)], axis=0)

    def unpack(self, value):
        return value[: self.part], halves_down(value[self.part :], 1)

    def tp_sum(self, pre, suf):
        width = pre.shape[1]
        pre = pre.astype(BF16).reshape(2, 2, self.part, width)
        suf = halves_down(suf.astype(BF16).reshape(4, self.suf_part, -1), 1)
        suf = suf.reshape(2, 2, -1, width)

        def pick(index, axis, *values):
            return jnp.concatenate(
                [lax.dynamic_index_in_dim(v, index, axis, keepdims=False) for v in values],
                axis=-2,
            )

        got = swap(pick(1 - self.core, 1, pre, suf), "tp", 4, 1)
        pair = pick(self.core, 1, pre, suf).astype(F32) + got.astype(F32)
        got = swap(pick(1 - self.x_index, 0, pair).astype(BF16), "tp", 4, 2)
        return self.unpack(pick(self.x_index, 0, pair) + got.astype(F32))

    def tp_gather(self, block):
        other = swap(block, "tp", 4, 2)
        low = jnp.where(self.x_index == 0, block, other)
        high = jnp.where(self.x_index == 0, other, block)
        pair = jnp.stack([low, high])
        got = swap(pair, "tp", 4, 1)
        even = jnp.where(self.core == 0, pair, got)
        odd = jnp.where(self.core == 0, got, pair)
        blocks = [even[0], odd[0], even[1], odd[1]]
        pre = jnp.concatenate([b[: self.part] for b in blocks], axis=0)
        suf = jnp.concatenate([halves_down(b[self.part :], 1) for b in blocks], axis=0)
        return pre, suf

    def pieces(self, value):
        n = value.shape[0] // self.size
        pre = [value[i * self.size : i * self.size + self.part] for i in range(n)]
        suf = [
            halves_down(value[i * self.size + self.part : (i + 1) * self.size], 1)
            for i in range(n)
        ]
        return pre, suf

    def spread(self, block, far):
        pair = jnp.concatenate([block, far], axis=0)
        got = swap(pair, "tp", 4, 1)
        first, second = self.pieces(pair), self.pieces(got)
        return jnp.concatenate(first[0] + second[0], axis=0), jnp.concatenate(
            first[1] + second[1], axis=0
        )

    def halves(self, value):
        size = value.shape[-2] // 2
        first = lax.slice_in_dim(value, 0, size, axis=value.ndim - 2)
        return first, lax.slice_in_dim(value, size, 2 * size, axis=value.ndim - 2)

    def first(self, pre, suf):
        pre, suf = self.halves(pre), self.halves(suf)
        return (pre[0], suf[0]), jnp.concatenate([pre[1], suf[1]], axis=-2)

    def second(self, keep, got):
        half = keep[0].shape[-2]
        got_pre = lax.slice_in_dim(got, 0, half, axis=got.ndim - 2)
        got_suf = lax.slice_in_dim(got, half, got.shape[-2], axis=got.ndim - 2)
        pre = self.halves(keep[0].astype(F32) + got_pre.astype(F32))
        suf = self.halves(keep[1].astype(F32) + got_suf.astype(F32))
        send = jnp.concatenate([pre[1], suf[1]], axis=-2).astype(BF16)
        return jnp.concatenate([pre[0], suf[0]], axis=-2), send

    def third(self, keep, got):
        return keep + got.astype(F32)


def local(
    dp,
    prefix_in,
    suffix_in,
    noisy_actions,
    prefix_len,
    action_live,
    pre_query,
    pre_keyval,
    pre_output,
    pre_gate,
    pre_up,
    pre_down,
    pre_norm_attn,
    pre_norm_ffn,
    act_query,
    act_keyval,
    act_output,
    act_gate,
    act_up,
    act_down,
    act_norm_attn,
    act_norm_ffn,
    action_embed,
    prefix_cot,
    suffix_cot,
):
    shards = 2 * dp
    both = ("dp", "expert")
    group = lax.axis_index("expert")
    t_index = lax.axis_index("tp")
    core, x_index = lax.rem(t_index, 2), t_index // 2
    pre_items, half_rows, width = prefix_in.shape
    _, suf_len, act_width = suffix_in.shape
    rows = pre_items * half_rows
    part = rows // 4
    suf_part = PAD // 4
    pack = Rows(part, suf_part, dp, core, x_index)
    scale = HD ** (-0.5)
    d_slice, q_cols = pre_query.shape
    a_slice = act_query.shape[0]
    heads = q_cols // HD
    hid = pre_gate.shape[1] // dp
    hid_act = act_gate.shape[1] // dp

    def half_cols(value):
        return lax.dynamic_slice_in_dim(value, core * HD, HD, 1)

    w1 = q_cols + HD
    small = [pre_norm_attn, pre_norm_ffn, act_norm_attn, act_norm_ffn, action_embed.reshape(-1)]
    small = jnp.concatenate(small)
    small_rows = -(-small.shape[0] // (16 * w1)) * 16
    small = jnp.pad(small, (0, small_rows * w1 - small.shape[0])).reshape(small_rows, w1)
    packed_in = jnp.concatenate(
        [
            jnp.concatenate([pre_query, half_cols(pre_keyval)], axis=1),
            jnp.concatenate([act_query, half_cols(act_keyval)], axis=1),
            small,
        ],
        axis=0,
    )
    z_index = lax.axis_index("dp")
    in_z = [packed_in] + [swap(packed_in, "dp", dp, d) for d in range(1, dp)]
    in_far = [swap(block, "expert", 2, 1) for block in in_z]

    def columns_out(pre, act):
        act_blocks = halves_down(jnp.stack(column_blocks(act, dp)), 2)
        return jnp.concatenate([jnp.stack(column_blocks(pre, dp)), act_blocks], axis=2)

    def columns_in(moved, pre, act):
        halves = jnp.concatenate(moved, axis=0)
        w_pre = halves[:, :, :hid].reshape(width, hid)
        w_act = halves_down(halves[:, :, hid:], 1).reshape(act_width, hid_act)
        return w_pre, w_act

    def dp_move(value):
        return lax.all_to_all(value, "dp", 0, 0, tiled=True)

    gate_out = columns_out(pre_gate, act_gate)
    up_out = columns_out(pre_up, act_up)
    down_out = jnp.concatenate(
        [
            pre_down.reshape(dp, hid, d_slice),
            halves_down(act_down.reshape(dp, hid_act, a_slice), 1),
        ],
        axis=1,
    )
    packed_out = jnp.concatenate([pre_output, act_output], axis=1)

    def own_rows(value):
        return lax.dynamic_slice_in_dim(value, t_index * part, part, 0)

    def own_suffix(value):
        return lax.dynamic_slice_in_dim(value, t_index * suf_part, suf_part, 0)

    def pad_suffix(value):
        return jnp.pad(value, ((0, PAD - suf_len), (0, 0)))

    def own_block(pre, suf):
        return pack.pack(own_first(pre, dp, group), own_first(suf, dp, group))

    def undo_block(block):
        pre, suf = pack.unpack(block)
        return own_first_undo(pre, dp, group), own_first_undo(suf, dp, group)

    cot_mine = own_rows(prefix_cot.reshape(rows, width))
    cot_suf_mine = own_suffix(pad_suffix(suffix_cot[0]))
    cot_block = own_block(cot_mine, cot_suf_mine)

    *in_near, gate_out, up_out, down_out, packed_out, cot_block = after(
        *in_z, gate_out, up_out, down_out, packed_out, cot_block
    )
    full_out = lax.all_gather(packed_out, both, axis=0)
    gate_own = dp_move(gate_out)
    full_in = jnp.zeros((dp, 2) + packed_in.shape, BF16)
    for d in range(dp):
        z = jnp.bitwise_xor(z_index, d)
        full_in = lax.dynamic_update_slice(full_in, in_near[d][None, None], (z, group, 0, 0))
        full_in = lax.dynamic_update_slice(full_in, in_far[d][None, None], (z, 1 - group, 0, 0))
    full_in = full_in.reshape((shards,) + packed_in.shape)

    w_pq = full_in[:, :d_slice, :q_cols].reshape(width, q_cols)
    w_pkv = full_in[:, :d_slice, q_cols:].reshape(width, HD)
    w_aq = full_in[:, d_slice : d_slice + a_slice, :q_cols].reshape(act_width, q_cols)
    w_akv = full_in[:, d_slice : d_slice + a_slice, q_cols:].reshape(act_width, HD)
    rest = full_in[:, d_slice + a_slice :].reshape(shards, small_rows * w1)
    gains, at = [], 0
    for size in (d_slice, d_slice, a_slice, a_slice):
        gains.append(rest[:, at : at + size].reshape(1, shards * size).astype(F32))
        at += size
    gain_pa, gain_pf, gain_aa, gain_af = gains
    embed = rest[:, at : at + action_embed.size].reshape(-1, act_width)
    prefix_x = prefix_in.astype(F32).reshape(rows, width)
    chosen = jnp.where(
        action_live[0][None, :] == 1, noisy_actions[0], jnp.zeros_like(noisy_actions[0])
    )
    chosen = jnp.pad(chosen, ((1, PAD - suf_len), (0, 0)))
    suffix_x = pad_suffix(suffix_in[0].astype(F32)) + project(chosen, embed)
    normed_pre = rms_scale(prefix_x, gain_pa).astype(BF16)
    normed_suf = rms_scale(suffix_x, gain_aa).astype(BF16)
    kv_pre = project(normed_pre, w_pkv).astype(BF16)
    kv_pre = kv_pre.reshape(pre_items, half_rows, HD)
    kv_got = swap(kv_pre, "expert", 2, 1)
    kv_suf = project(normed_suf, w_akv).astype(BF16)
    queries_pre = project(normed_pre, w_pq).astype(BF16).reshape(pre_items, half_rows, heads, HD)
    queries_suf = project(normed_suf, w_aq).astype(BF16).reshape(1, PAD, heads, HD)
    queries_pre, queries_suf, kv_suf, kv_got = after(queries_pre, queries_suf, kv_suf, kv_got)
    kv_pre = jnp.concatenate([kv_pre, kv_got], axis=1)
    full_len = kv_pre.shape[1]
    kv_mine = jnp.concatenate([kv_pre.reshape(pre_items * full_len, HD), kv_suf], axis=0)
    kv_other = swap(kv_mine, "tp", 4, 1)
    keys = jnp.where(core == 0, kv_mine, kv_other)
    values = jnp.where(core == 0, kv_other, kv_mine)

    def split_keys(value):
        pre = value[: pre_items * full_len].reshape(pre_items, full_len, HD)
        own = lax.dynamic_index_in_dim(pre, group, 0, keepdims=True)
        return pre, jnp.concatenate([own, value[None, pre_items * full_len :]], axis=1)

    keys_pre, keys_suf = split_keys(keys)
    values_pre, values_suf = split_keys(values)
    place = jnp.arange(full_len)
    first = place < half_rows
    place = jnp.where(first, place + group * half_rows, place - half_rows + (1 - group) * half_rows)
    key_live = place[None, :] < prefix_len[:, None]
    pre_allowed = jnp.broadcast_to(key_live[:, None, :], (pre_items, half_rows, full_len))
    own_live = lax.dynamic_index_in_dim(key_live, group, 0, keepdims=True)
    blocks = jnp.minimum(jnp.arange(PAD), 1)
    later = (blocks[None, :] <= blocks[:, None]) & (jnp.arange(PAD) < suf_len)[None, :]
    suf_allowed = jnp.concatenate(
        [jnp.broadcast_to(own_live[:, None, :], (1, PAD, full_len)), later[None]], axis=2
    )
    att_pre, probs_pre = attend(queries_pre, keys_pre, values_pre, pre_allowed, scale)
    att_suf, probs_suf = attend(queries_suf, keys_suf, values_suf, suf_allowed, scale)
    att_pre = att_pre.reshape(rows, q_cols)
    att_suf = att_suf.reshape(PAD, q_cols)

    att_pre, att_suf, full_out = after(att_pre, att_suf, full_out)
    w_po = jnp.concatenate([full_out[i, :, :d_slice] for i in range(shards)], axis=1)
    w_ao = jnp.concatenate([full_out[i, :, d_slice:] for i in range(shards)], axis=1)
    x_mine = own_rows(prefix_x)
    xs_mine = own_suffix(suffix_x)
    branch, branch_suf = project(att_pre, w_po).astype(BF16), project(att_suf, w_ao).astype(BF16)
    branch, branch_suf, gate_own, up_out = after(branch, branch_suf, gate_own, up_out)
    gate_got = swap(gate_own, "expert", 2, 1)
    up_own = dp_move(up_out)
    branch, branch_suf = pack.tp_sum(branch, branch_suf)
    resid = x_mine + branch
    resid_suf = xs_mine + branch_suf
    normed_block = own_block(
        rms_scale(resid, gain_pf).astype(BF16), rms_scale(resid_suf, gain_af).astype(BF16)
    )

    normed_z = [normed_block] + [swap(normed_block, "dp", dp, d) for d in range(1, dp)]
    normed_chunks, normed_sufs, gates, ups = [], [], [], []
    for d in range(dp):
        pre, suf = pack.spread(normed_z[d], swap(normed_z[d], "tp", 4, 2))
        if d == 0:
            pre, suf, up_own = after(pre, suf, up_own)
            up_got = swap(up_own, "expert", 2, 1)
            pre, gate_got = after(pre, gate_got)
            w_pg, w_ag = columns_in((gate_own, gate_got), pre_gate, act_gate)
        normed_chunks.append(pre)
        normed_sufs.append(suf)
        gates.append((project(pre, w_pg), project(suf, w_ag)))
    normed_last, down_out = after(normed_z[-1], down_out)
    down_own = dp_move(down_out)
    gates[-1], up_got = after(gates[-1], up_got)
    w_pu, w_au = columns_in((up_own, up_got), pre_up, act_up)
    for d in range(dp):
        ups.append((project(normed_chunks[d], w_pu), project(normed_sufs[d], w_au)))
    cot_far = swap(cot_block, "tp", 4, 2)
    ups[0], cot_far = after(ups[0], cot_far)
    cot_chunks = [pack.spread(cot_block, cot_far)]
    ups[-1], down_own, cot_block = after(ups[-1], down_own, cot_block)
    down_got = swap(down_own, "expert", 2, 1)
    cot_z = [swap(cot_block, "dp", dp, d) for d in range(1, dp)]
    cot_chunks += [pack.spread(z, swap(z, "tp", 4, 2)) for z in cot_z]
    down = jnp.concatenate([down_own, down_got], axis=0)
    w_pd = jnp.concatenate([down[i, :hid] for i in range(shards)], axis=1)
    act_down_blocks = halves_down(down[:, hid:], 2)
    w_ad = jnp.concatenate([act_down_blocks[i] for i in range(shards)], axis=1)

    def inner(gate, upward, cot, w_d):
        hidden, pull = jax.vjp(geglu, gate, upward)
        gate_cot, up_cot = pull(project_back(cot, w_d))
        return hidden.astype(BF16), gate_cot.astype(BF16), up_cot.astype(BF16)

    def back(gate_cot, up_cot, w_g, w_u):
        return (project_back(gate_cot, w_g) + project_back(up_cot, w_u)).astype(BF16)

    inners, inners_suf, pairs, sent, homes = {}, {}, {}, {}, {}

    def partial_of(d):
        pre = back(*inners[d][1:], w_pg, w_pu)
        suf = back(*inners_suf[d][1:], w_ag, w_au)
        suf = halves_down(suf.reshape(4, suf_part, act_width), 1).reshape(-1, width)
        return pre, suf

    def inner_of(d, *ties):
        cot, cot_suf = cot_chunks[d]
        gate, gate_suf, upward, upward_suf, *ties = after(*gates[d], *ups[d], *ties)
        inners[d] = inner(gate, upward, cot, w_pd)
        inners_suf[d] = inner(gate_suf, upward_suf, cot_suf, w_ad)
        return ties

    order = list(range(1, dp)) + [0]
    inner_of(0)
    last = inners[0][0]
    for i, d in enumerate(order):
        if d > 0:
            inner_of(d, last)
        if i > 0:
            e = order[i - 1]
            *inners[d], pairs[e] = after(*inners[d], pairs[e])
            keep, got = pairs[e][0], pairs[e][1]
            keep, send = pack.second(keep, got)
            *inners[d], send = after(*inners[d], send)
            pairs[e] = keep, swap(send, "tp", 4, 2)
        pre, suf = partial_of(d)
        last = pre
        keep, send = pack.first(pre, suf)
        pairs[d] = keep, swap(send, "tp", 4, 1)
        if i > 1:
            e = order[i - 2]
            *pairs[d], keep, got = after(*pairs[d], *pairs[e])
            homes[e] = swap(pack.third(keep, got).astype(BF16), "dp", dp, e)
    hiddens = [inners[d][0] for d in range(dp)]
    hid_suf = [inners_suf[d][0] for d in range(dp)]
    *hiddens, last, keep, got = after(*hiddens, last, *pairs[0])
    keep, send = pack.second(keep, got)
    pairs[0] = keep, swap(send, "tp", 4, 2)
    *hiddens, send = after(*hiddens, send)
    hidden_all = jnp.concatenate(hiddens, axis=0)
    outs = project(hidden_all, w_pd).astype(BF16).reshape(dp, rows, width)
    outs_suf = project(jnp.concatenate(hid_suf, axis=0), w_ad).astype(BF16)
    outs_suf = outs_suf.reshape(dp * 4, suf_part, act_width)
    outs_suf = halves_down(outs_suf, 1).reshape(dp, -1, width)
    for e in order[-2:-1]:
        outs, keep, got = after(outs, *pairs[e])
        homes[e] = swap(pack.third(keep, got).astype(BF16), "dp", dp, e)
    outs_keep, outs_send = pack.first(outs, outs_suf)
    outs_got = swap(outs_send, "tp", 4, 1)

    normed_suf_all = jnp.concatenate(normed_sufs, axis=0)
    cot_suf_all = jnp.concatenate([c[1] for c in cot_chunks], axis=0)
    h_suf, g_suf, u_suf = (
        jnp.concatenate([inners_suf[d][i] for d in range(dp)], axis=0) for i in range(3)
    )
    chunked = dp > 4
    if not chunked:
        normed_all = jnp.concatenate(normed_chunks, axis=0)
        cot_all = jnp.concatenate([c[0] for c in cot_chunks], axis=0)

    def outer_chunks(left, right):
        return sum(outer_sum(a, b) for a, b in zip(left, right))

    def normed_outer(i):
        right = [inners[d][i] for d in range(dp)]
        if chunked:
            return outer_chunks(normed_chunks, right)
        return outer_sum(normed_all, jnp.concatenate(right, axis=0))

    def columns_back(pre, act):
        pre = pre.reshape(shards, d_slice, hid)
        act = halves_down(act.reshape(shards, a_slice, hid_act), 2)
        whole = jnp.concatenate([pre, act], axis=2)
        return whole[:dp], swap(whole[dp:], "expert", 2, 1)

    def both_sum(own, got):
        return (own.astype(F32) + got.astype(F32)).astype(BF16)

    def columns_end(whole):
        pre = jnp.concatenate([whole[i, :, :hid] for i in range(dp)], axis=1)
        act = halves_down(whole[:, :, hid:], 1)
        act = jnp.concatenate([act[i] for i in range(dp)], axis=1)
        return pre.astype(F32), act.astype(F32)

    gate_grad = columns_back(
        normed_outer(1).astype(BF16), outer_sum(normed_suf_all, g_suf).astype(BF16)
    )
    g0, keep, got = after(gate_grad[0], *pairs[0])
    gate_grad = g0, gate_grad[1]
    home = pack.third(keep, got)
    up_grad = columns_back(
        normed_outer(2).astype(BF16), outer_sum(normed_suf_all, u_suf).astype(BF16)
    )

    for d in range(1, dp):
        home = home + homes[d].astype(F32)
    mcot, mcot_suf = undo_block(home)
    mid_part, ffn_gain = norm_back(resid, gain_pf, mcot)
    mid_part_suf, ffn_gain_suf = norm_back(resid_suf, gain_af, mcot_suf)
    mid = cot_mine.astype(F32) + mid_part
    mid_suf = cot_suf_mine.astype(F32) + mid_part_suf
    mid_block, hidden_all, outs_got = after(
        pack.pack(mid, mid_suf).astype(BF16), hidden_all, outs_got
    )
    bcot, bcot_suf = pack.tp_gather(mid_block)
    if chunked:
        down_pre = outer_chunks(
            [hidden_all[d * rows : (d + 1) * rows] for d in range(dp)], [c[0] for c in cot_chunks]
        ).astype(BF16)
    else:
        down_pre = outer_sum(hidden_all, cot_all).astype(BF16)
    down_act = outer_sum(h_suf, cot_suf_all).astype(BF16)
    down_grad = jnp.concatenate(
        [
            jnp.stack(column_blocks(down_pre, shards)),
            halves_down(jnp.stack(column_blocks(down_act, shards)), 1),
        ],
        axis=1,
    )
    down_grad = down_grad[:dp], swap(down_grad[dp:], "expert", 2, 1)
    bcot, bcot_suf, gate_grad, outs_got = after(bcot, bcot_suf, gate_grad, outs_got)
    outs_keep, outs_send = pack.second(outs_keep, outs_got)
    outs_got = swap(outs_send, "tp", 4, 2)
    gate_grad = dp_move(both_sum(*gate_grad))
    acot_pre = project_back(bcot, w_po).astype(BF16).reshape(pre_items, half_rows, heads, HD)
    acot_suf = project_back(bcot_suf, w_ao).astype(BF16).reshape(1, PAD, heads, HD)
    qcot_pre, kcot_pre, vcot_pre = attend_back(
        queries_pre, keys_pre, values_pre, probs_pre, acot_pre, scale
    )
    qcot_suf, kcot_suf, vcot_suf = attend_back(
        queries_suf, keys_suf, values_suf, probs_suf, acot_suf, scale
    )

    def join(pre, suf):
        mine = lax.dynamic_index_in_dim(pre, group, 0, keepdims=True) + suf[:, :full_len]
        pre = lax.dynamic_update_slice_in_dim(pre, mine, group, 0)
        pre = pre.reshape(pre_items * full_len, HD)
        return jnp.concatenate([pre, suf[0, full_len:]], axis=0)

    kcot, vcot = join(kcot_pre, kcot_suf), join(vcot_pre, vcot_suf)
    got = swap(jnp.where(core == 0, vcot, kcot).astype(BF16), "tp", 4, 1)
    kvcot = jnp.where(core == 0, kcot, vcot) + got.astype(F32)
    kv_pre_cot = kvcot[: pre_items * full_len].reshape(pre_items, 2, half_rows, HD)
    got = swap(kv_pre_cot[:, 1].astype(BF16), "expert", 2, 1)
    kv_pre_cot = kv_pre_cot[:, 0] + got.astype(F32)
    kvcot = jnp.concatenate(
        [kv_pre_cot.reshape(rows, HD), kvcot[pre_items * full_len :]], axis=0
    )
    got = swap(kvcot.astype(BF16), "tp", 4, 2)
    kvcot = (kvcot + got.astype(F32)).astype(BF16)
    kvcot, gate_grad, up_grad, outs_got = after(kvcot, gate_grad, up_grad, outs_got)
    outs = pack.third(outs_keep, outs_got)
    outs = [outs[0]] + [swap(outs[d].astype(BF16), "dp", dp, d).astype(F32) for d in range(1, dp)]
    up_grad = dp_move(both_sum(*up_grad))
    key_half, key_own = kvcot[:rows], kvcot[rows:]
    qcot_pre = qcot_pre.astype(BF16).reshape(rows, q_cols)
    qcot_suf = qcot_suf.astype(BF16).reshape(PAD, q_cols)
    ncot = project_back(qcot_pre, w_pq) + 0.5 * project_back(key_half, w_pkv)
    ncot_suf = project_back(qcot_suf, w_aq) + 0.5 * project_back(key_own, w_akv)
    ncot, ncot_suf = pack.tp_sum(ncot, ncot_suf)
    in_part, attn_gain = norm_back(x_mine, gain_pa, ncot)
    in_part_suf, attn_gain_suf = norm_back(xs_mine, gain_aa, ncot_suf)
    grad_mine = mid + in_part
    grad_suf_mine = mid_suf + in_part_suf
    embed_w = lax.dot_general(
        own_suffix(chosen).astype(F32),
        grad_suf_mine,
        (((0,), (0,)), ((), ())),
        precision=lax.Precision.HIGHEST,
    )
    tail = jnp.concatenate(
        [
            attn_gain.reshape(shards, -1),
            ffn_gain.reshape(shards, -1),
            attn_gain_suf.reshape(shards, -1),
            ffn_gain_suf.reshape(shards, -1),
            embed_w.reshape(shards, -1),
        ],
        axis=1,
    )

    out_w = jnp.concatenate(
        [
            jnp.stack(column_blocks(outer_sum(att_pre, bcot).astype(BF16), shards)),
            jnp.stack(column_blocks(outer_sum(att_suf, bcot_suf).astype(BF16), shards)),
        ],
        axis=2,
    )
    in_w = jnp.concatenate(
        [
            jnp.concatenate(
                [
                    outer_sum(normed_pre, qcot_pre).astype(BF16).reshape(shards, d_slice, q_cols),
                    outer_sum(normed_pre, key_half).astype(BF16).reshape(shards, d_slice, HD),
                ],
                axis=2,
            ),
            jnp.concatenate(
                [
                    outer_sum(normed_suf, qcot_suf).astype(BF16).reshape(shards, a_slice, q_cols),
                    outer_sum(normed_suf, key_own).astype(BF16).reshape(shards, a_slice, HD),
                ],
                axis=2,
            ),
        ],
        axis=1,
    )

    def scatter_y(value):
        value = value.reshape((dp, 2) + value.shape[1:])
        send = lax.dynamic_index_in_dim(value, 1 - group, 1, keepdims=False)
        keep = lax.dynamic_index_in_dim(value, group, 1, keepdims=False)
        return keep, swap(send, "expert", 2, 1)

    def scatter_z(moved):
        return jnp.sum(dp_move(both_sum(*moved)).astype(F32), axis=0)

    out_w = scatter_y(out_w)
    in_w = scatter_y(in_w)
    in_w, up_grad, down_grad = after(in_w, up_grad, down_grad)
    down_grad = dp_move(both_sum(*down_grad))
    out_w = scatter_z(out_w)
    in_w = scatter_z(in_w)
    g_po, g_ao = out_w[:, :d_slice], out_w[:, d_slice:]
    g_pq, g_aq = in_w[:d_slice, :q_cols], in_w[d_slice:, :q_cols]
    kv_w = in_w[:, q_cols:].astype(BF16)
    kv_other = swap(kv_w, "tp", 4, 1).astype(F32)
    kv_w = kv_w.astype(F32)
    kv_w = jnp.concatenate(
        [jnp.where(core == 0, kv_w, kv_other), jnp.where(core == 0, kv_other, kv_w)], axis=1
    )
    g_pkv, g_akv = kv_w[:d_slice], kv_w[d_slice:]

    out_pre, out_suf = undo_block(sum(outs))
    out_block = pack.pack(resid + out_pre, resid_suf + out_suf).astype(BF16)
    out_pre, out_suf = pack.tp_gather(out_block)
    prefix_out = out_pre.reshape(pre_items, half_rows, width)
    suffix_out = out_suf[None, :suf_len]
    grad_pre, grad_suf = pack.tp_gather(pack.pack(grad_mine, grad_suf_mine).astype(BF16))
    prefix_grad = grad_pre.astype(F32).reshape(pre_items, half_rows, width)
    suffix_grad = grad_suf.astype(F32)[None, :suf_len]
    g_pg, g_ag = columns_end(gate_grad)
    g_pu, g_au = columns_end(up_grad)
    g_pd = down_grad[:, :hid].reshape(dp * hid, d_slice).astype(F32)
    g_ad = halves_down(down_grad[:, hid:], 2).reshape(dp * hid_act, a_slice).astype(F32)
    tail = jnp.broadcast_to(tail[:, None, None], (shards, 4, 1, tail.shape[1]))
    tail = tail.reshape(4 * shards, 1, -1)
    tail = lax.all_to_all(tail, ("dp", "expert", "tp"), 0, 0, tiled=True)
    tail = jnp.sum(tail, axis=0)[0]
    tails, at = [], 0
    for size in (d_slice, d_slice, a_slice, a_slice, action_embed.size):
        tails.append(tail[at : at + size])
        at += size
    g_gpa, g_gpf, g_gaa, g_gaf, g_embed = tails
    g_embed = g_embed.reshape(action_embed.shape)
    return (
        prefix_out,
        suffix_out,
        prefix_grad,
        suffix_grad,
        g_pq,
        g_pkv,
        g_po,
        g_pg,
        g_pu,
        g_pd,
        g_gpa,
        g_gpf,
        g_aq,
        g_akv,
        g_ao,
        g_ag,
        g_au,
        g_ad,
        g_gaa,
        g_gaf,
        g_embed,
    )


def solution(mesh):
    return jax.shard_map(
        functools.partial(local, mesh.shape["dp"]),
        mesh=mesh,
        in_specs=(
            P("dp", "expert", None),
            P(("dp", "expert"), None, None),
            P(("dp", "expert"), None, None),
            P("dp"),
            P(("dp", "expert"), None),
            P(("dp", "expert"), "tp"),
            P(("dp", "expert"), None),
            P("tp", ("dp", "expert")),
            P(("dp", "expert"), "tp"),
            P(("dp", "expert"), "tp"),
            P("tp", ("dp", "expert")),
            P(("dp", "expert")),
            P(("dp", "expert")),
            P(("dp", "expert"), "tp"),
            P(("dp", "expert"), None),
            P("tp", ("dp", "expert")),
            P(("dp", "expert"), "tp"),
            P(("dp", "expert"), "tp"),
            P("tp", ("dp", "expert")),
            P(("dp", "expert")),
            P(("dp", "expert")),
            P(("dp", "expert"), None),
            P("dp", "expert", None),
            P(("dp", "expert"), None, None),
        ),
        out_specs=(
            P("dp", "expert", None),
            P(("dp", "expert"), None, None),
            P("dp", "expert", None),
            P(("dp", "expert"), None, None),
            P(("dp", "expert"), "tp"),
            P(("dp", "expert"), None),
            P("tp", ("dp", "expert")),
            P(("dp", "expert"), "tp"),
            P(("dp", "expert"), "tp"),
            P("tp", ("dp", "expert")),
            P(("dp", "expert")),
            P(("dp", "expert")),
            P(("dp", "expert"), "tp"),
            P(("dp", "expert"), None),
            P("tp", ("dp", "expert")),
            P(("dp", "expert"), "tp"),
            P(("dp", "expert"), "tp"),
            P("tp", ("dp", "expert")),
            P(("dp", "expert")),
            P(("dp", "expert")),
            P(("dp", "expert"), None),
        ),
        check_vma=False,
    )
```

time: 4170 us -> 1290 us (0.31)
  waiting for transfers between devices: 3600 us -> 539 us
  blocking collectives: 200 us -> 0 us
  local copies, waits for them, and re-layouts: 29.5 us -> 201 us
  starting transfers between devices: 2.88 us -> 158 us
  other arithmetic: 42.7 us -> 150 us
  matrix products: 262 us -> 213 us
    reduce_scatter x13 -> x0, waiting for transfers between devices: 2320 us -> none  [the longest x1 548 us: local(): lax.psum_scatter(gate_w_pre, ('dp', 'expert'), scatter_dimension=0, tiled...]
    all_gather x13 -> x1, waiting for transfers between devices: 983 us -> 0.02 us  [local(): full_out = lax.all_gather(packed_out, both, axis=0)]
    ppermute x0 -> x69, waiting for transfers between devices: none -> 387 us  [swap(): return lax.ppermute(value, axis, [(i, i ^ mask) for i in range(size)])]
    psum x3 -> x0, waiting for transfers between devices: 293 us -> none  [the longest x2 200 us: head_sums(): return lax.psum((first, second), 'tp')]
    all_to_all x0 -> x9, waiting for transfers between devices: none -> 151 us  [the longest x8 136 us: dp_move(): return lax.all_to_all(value, 'dp', 0, 0, tiled=True)]
    all_gather x5 -> x0, blocking collectives: 116 us -> none  [the longest x1 30.6 us: local(): lax.all_gather(action_embed, ('dp', 'expert'), axis=0, tiled=True)]
    unnamed x234 -> x613, local copies, waits for them, and re-layouts: 23.3 us -> 124 us
    all_to_all x0 -> x9, starting transfers between devices: none -> 85.9 us  [the longest x8 71.6 us: dp_move(): return lax.all_to_all(value, 'dp', 0, 0, tiled=True)]
  transfers between devices with their start and end apart: 30 -> 79, of which waited for: 27 -> 31; matrix products, arithmetic and copies ran while one was open for 5% -> 40% of each run, Pallas kernels for 0% -> 0%
where the time goes in v1:
time: 1290 us; the launch traced here: 1280 us
  waiting for transfers between devices  539 us (42%)
  matrix products  213 us (17%)
  local copies, waits for them, and re-layouts  201 us (16%)
  starting transfers between devices  158 us (12%)
  other arithmetic  150 us (12%)
  between operations  19.7 us (2%)
    ppermute x69, waiting for transfers between devices, swap(): return lax.ppermute(value, axis, [(i, i ^ mask) for i in range(size)])  387 us
    all_to_all x8, waiting for transfers between devices, dp_move(): return lax.all_to_all(value, 'dp', 0, 0, tiled=True)  136 us
    unnamed x613, local copies, waits for them, and re-layouts  124 us
    dot_general x30, matrix products, project_back(): lax.dot_general(left, right, (((1,), (1,)), ((), ())), preferred_element_...  81.1 us
    ppermute x69, starting transfers between devices, swap(): return lax.ppermute(value, axis, [(i, i ^ mask) for i in range(size)])  72.6 us
    all_to_all x8, starting transfers between devices, dp_move(): return lax.all_to_all(value, 'dp', 0, 0, tiled=True)  71.6 us
    dot_general x25, matrix products, project(): return jnp.dot(left, right, preferred_element_type=F32)  63.9 us
    dot_general x12, matrix products, outer_sum(): lax.dot_general(left, right, (((0,), (0,)), ((), ())), preferred_element_...  55.2 us
  transfers between devices with their start and end apart: 79, of which 31 were waited for; matrix products, arithmetic and copies ran while one was open for 40% of the time, Pallas kernels for 0%

profile of v1, /device:TPU:0, one launch (start us, length us, event | category | flops | bytes accessed | tf_op | source)
XLA Modules:
  0.0 1281.0 jit_solution(4093178051759978697)
XLA Ops:
  47.4 5.5 maximum_maximum_fusion.4
  57.0 4.6 collective-permute-done.1
  68.0 10.7 collective-permute-done.4
  79.9 16.2 %collective-permute-done.5 = bf16[400,768]{1,0:T(8,128)(2,1)S(1)} collective-permute-done((bf16[400,768]{1,0:T(8,128)(2,1)}, bf16[400,768]{1,0:T(8,128)(2,1)S(1)}, u32[]{:S(2)}, u32[]{:S(2)}) %collective-permute-start.5) | collective-permute-done | bytes 614432 | tf_op jit(solution)/shard_map/ppermute | solution.py:67
  97.3 8.3 collective-permute-done.6
  114.0 4.6 convolution_convert_fusion.10
  129.8 27.4 %all-to-all-start = ((bf16[4,256,1152]{2,1,0:T(8,128)(2,1)}), bf16[4,256,1152]{2,1,0:T(8,128)(2,1)}, u32[]{:S(2)}, u32[]{:S(2)}) async-start(bf16[4,256,1152]{2,1,0:T(8,128)(2,1)} %get-tuple-element.160), calls=%async_computation | async-start | bytes 4718592 | tf_op jit(solution)/shard_map/all_to_all | solution.py:261
  179.1 33.4 %all-to-all-done = bf16[4,256,1152]{2,1,0:T(8,128)(2,1)} async-done(((bf16[4,256,1152]{2,1,0:T(8,128)(2,1)}), bf16[4,256,1152]{2,1,0:T(8,128)(2,1)}, u32[]{:S(2)}, u32[]{:S(2)}) %all-to-all-start) | async-done | bytes 2359328 | tf_op jit(solution)/shard_map/all_to_all | solution.py:261
  228.0 22.1 %collective-permute-done.10 = bf16[152,2048]{1,0:T(8,128)(2,1)S(1)} collective-permute-done((bf16[152,2048]{1,0:T(8,128)(2,1)S(1)}, bf16[152,2048]{1,0:T(8,128)(2,1)S(1)}, u32[]{:S(2)}, u32[]{:S(2)}) %collective-permute-start.10) | collective-permute-done | bytes 622624 | tf_op jit(solution)/shard_map/ppermute | solution.py:67
  271.8 42.0 %collective-permute-done.27 = bf16[152,2048]{1,0:T(8,128)(2,1)S(1)} collective-permute-done((bf16[152,2048]{1,0:T(8,128)(2,1)}, bf16[152,2048]{1,0:T(8,128)(2,1)S(1)}, u32[]{:S(2)}, u32[]{:S(2)}) %collective-permute-start.27) | collective-permute-done | bytes 622624 | tf_op jit(solution)/shard_map/ppermute | solution.py:67
  314.8 41.0 %collective-permute-done.21 = bf16[152,2048]{1,0:T(8,128)(2,1)S(1)} collective-permute-done((bf16[152,2048]{1,0:T(8,128)(2,1)}, bf16[152,2048]{1,0:T(8,128)(2,1)S(1)}, u32[]{:S(2)}, u32[]{:S(2)}) %collective-permute-start.21) | collective-permute-done | bytes 622624 | tf_op jit(solution)/shard_map/ppermute | solution.py:67
  361.6 11.1 collective-permute-done.22
  374.0 9.1 collective-permute-done.15
  386.6 4.7 all-to-all-start.2
  391.5 20.6 %collective-permute-done.13 = bf16[4,256,1152]{2,1,0:T(8,128)(2,1)} collective-permute-done((bf16[4,256,1152]{2,1,0:T(8,128)(2,1)}, bf16[4,256,1152]{2,1,0:T(8,128)(2,1)}, u32[]{:S(2)}, u32[]{:S(2)}) %collective-permute-start.13) | collective-permute-done | bytes 2359328 | tf_op jit(solution)/shard_map/ppermute | solution.py:67
  477.5 6.5 fusion.338
  483.9 12.0 collective-permute-start.24
  520.6 20.1 %collective-permute-done.30 = bf16[152,2048]{1,0:T(8,128)(2,1)S(1)} collective-permute-done((bf16[152,2048]{1,0:T(8,128)(2,1)}, bf16[152,2048]{1,0:T(8,128)(2,1)S(1)}, u32[]{:S(2)}, u32[]{:S(2)}) %collective-permute-start.30) | collective-permute-done | bytes 622624 | tf_op jit(solution)/shard_map/ppermute | solution.py:67
  545.6 5.9 collective-permute-done.31
  551.7 6.5 collective-permute-done.35
  571.6 9.9 multiply_convert_fusion.9
  589.1 10.0 multiply_convert_fusion.3
  623.9 9.9 multiply_convert_fusion.6
  647.4 10.1 multiply_convert_fusion.4
  679.1 13.3 %fusion.20 = bf16[2048,1024]{1,0:T(8,128)(2,1)S(1)} fusion(bf16[2304,2048]{1,0:T(8,128)(2,1)} %get-tuple-element.510, bf16[576,1024]{1,0:T(8,128)(2,1)} %copy-done.198, bf16[576,1024]{1,0:T(8,128)(2,1)S(1)} %copy-done.197, bf16[576,1024]{1,0:T(8,128)(2,1)S(1)} %copy-done.195, bf16[576,1024]{1,0:T(8,128)(2,1)S(1)} %copy-done.193), kind=kOutput, calls=%fused_computation.40 | convolution fusion | flops 9684647936 | bytes 18350080 | tf_op jit(solution)/shard_map/dot_general | solution.py:36
  692.5 13.1 %fusion.17 = bf16[2048,1024]{1,0:T(8,128)(2,1)S(1)} fusion(bf16[2304,2048]{1,0:T(8,128)(2,1)} %get-tuple-element.510, bf16[576,1024]{1,0:T(8,128)(2,1)S(1)} %copy-done.205, bf16[576,1024]{1,0:T(8,128)(2,1)S(1)} %copy-done.203, bf16[576,1024]{1,0:T(8,128)(2,1)S(1)} %copy-done.201, bf16[576,1024]{1,0:T(8,128)(2,1)S(1)} %copy-done.199), kind=kOutput, calls=%fused_computation.39 | convolution fusion | flops 9684647936 | bytes 18350080 | tf_op jit(solution)/shard_map/dot_general | solution.py:36
  705.6 4.6 add_convert_fusion.5
  730.4 13.3 %convolution_convert_fusion = bf16[2304,2048]{1,0:T(8,128)(2,1)S(1)} fusion(bf16[2304,1024]{1,0:T(8,128)(2,1)} %constant_dynamic-update-slice_fusion.140, bf16[1024,2048]{1,0:T(8,128)(2,1)} %copy-done.155), kind=kOutput, calls=%fused_computation.1 | convolution fusion | flops 9668395008 | bytes 18350080 | tf_op jit(solution)/shard_map/dot_general | solution.py:28
  758.3 30.4 %collective-permute-done.45 = bf16[152,2048]{1,0:T(8,128)(2,1)S(1)} collective-permute-done((bf16[152,2048]{1,0:T(8,128)(2,1)S(1)}, bf16[152,2048]{1,0:T(8,128)(2,1)S(1)}, u32[]{:S(2)}, u32[]{:S(2)}) %collective-permute-start.45) | collective-permute-done | bytes 622624 | tf_op jit(solution)/shard_map/ppermute | solution.py:67
  795.9 14.1 %convolution_convert_fusion.1 = bf16[1024,2048]{1,0:T(8,128)(2,1)S(1)} fusion(bf16[2304,1024]{1,0:T(8,128)(2,1)} %constant_dynamic-update-slice_fusion.140, bf16[2304,2048]{1,0:T(8,128)(2,1)} %get-tuple-element.430), kind=kOutput, calls=%fused_computation.41 | convolution fusion | flops 9665773568 | bytes 18350080 | tf_op jit(solution)/shard_map/dot_general | solution.py:36
  811.3 15.0 %collective-permute-done.48 = bf16[152,2048]{1,0:T(8,128)(2,1)S(1)} collective-permute-done((bf16[152,2048]{1,0:T(8,128)(2,1)S(1)}, bf16[152,2048]{1,0:T(8,128)(2,1)S(1)}, u32[]{:S(2)}, u32[]{:S(2)}) %collective-permute-start.48) | collective-permute-done | bytes 622624 | tf_op jit(solution)/shard_map/ppermute | solution.py:67
  833.0 8.2 convert_add_fusion
  868.2 16.6 %all-to-all-start.3 = ((bf16[4,256,1152]{2,1,0:T(8,128)(2,1)}), bf16[4,256,1152]{2,1,0:T(8,128)(2,1)}, u32[]{:S(2)}, u32[]{:S(2)}) async-start(bf16[4,256,1152]{2,1,0:T(8,128)(2,1)} %add_convert_fusion.4), calls=%async_computation.3 | async-start | bytes 4718592 | tf_op jit(solution)/shard_map/all_to_all | solution.py:261
  902.1 33.1 %collective-permute-done.52 = bf16[2,288,256]{2,1,0:T(8,128)(2,1)S(1)} collective-permute-done((bf16[2,288,256]{2,1,0:T(8,128)(2,1)S(1)}, bf16[2,288,256]{2,1,0:T(8,128)(2,1)S(1)}, u32[]{:S(2)}, u32[]{:S(2)}) %collective-permute-start.52) | collective-permute-done | bytes 294944 | tf_op jit(solution)/shard_map/ppermute | solution.py:67
  939.5 5.3 collective-permute-done.53
  946.4 5.5 all-to-all-start.6
  962.9 5.3 fusion.292
  990.9 7.8 collective-permute-done.56
  998.7 30.5 %collective-permute-done.57 = bf16[152,2048]{1,0:T(8,128)(2,1)} collective-permute-done((bf16[152,2048]{1,0:T(8,128)(2,1)}, bf16[152,2048]{1,0:T(8,128)(2,1)}, u32[]{:S(2)}, u32[]{:S(2)}) %collective-permute-start.57) | collective-permute-done | bytes 622624 | tf_op jit(solution)/shard_map/ppermute | solution.py:67
  1032.7 13.5 %collective-permute-done.62 = bf16[152,2048]{1,0:T(8,128)(2,1)S(1)} collective-permute-done((bf16[152,2048]{1,0:T(8,128)(2,1)S(1)}, bf16[152,2048]{1,0:T(8,128)(2,1)S(1)}, u32[]{:S(2)}, u32[]{:S(2)}) %collective-permute-start.62) | collective-permute-done | bytes 622624 | tf_op jit(solution)/shard_map/ppermute | solution.py:67
  1052.0 14.3 %all-to-all-start.8 = ((f32[32,1,4864]{2,1,0:T(1,128)}), f32[32,1,4864]{2,1,0:T(1,128)S(1)}, u32[]{:S(2)}, u32[]{:S(2)}) async-start(f32[32,1,4864]{2,1,0:T(1,128)} %broadcast_in_dim.160), calls=%async_computation.8 | async-start | bytes 1245184 | tf_op jit(solution)/shard_map/all_to_all | solution.py:666
  1068.5 15.1 %all-to-all-done.8 = f32[32,1,4864]{2,1,0:T(1,128)S(1)} async-done(((f32[32,1,4864]{2,1,0:T(1,128)}), f32[32,1,4864]{2,1,0:T(1,128)S(1)}, u32[]{:S(2)}, u32[]{:S(2)}) %all-to-all-start.8) | async-done | bytes 622624 | tf_op jit(solution)/shard_map/all_to_all | solution.py:666
  1083.6 4.8 all-to-all-start.4
  1093.5 14.7 %collective-permute-done.63 = bf16[152,2048]{1,0:T(8,128)(2,1)S(1)} collective-permute-done((bf16[152,2048]{1,0:T(8,128)(2,1)S(1)}, bf16[152,2048]{1,0:T(8,128)(2,1)S(1)}, u32[]{:S(2)}, u32[]{:S(2)}) %collective-permute-start.63) | collective-permute-done | bytes 622624 | tf_op jit(solution)/shard_map/ppermute | solution.py:67
  1109.7 11.0 collective-permute-done.59
  1125.1 17.6 %all-to-all-done.4 = bf16[4,256,1152]{2,1,0:T(8,128)(2,1)} async-done(((bf16[4,256,1152]{2,1,0:T(8,128)(2,1)}), bf16[4,256,1152]{2,1,0:T(8,128)(2,1)}, u32[]{:S(2)}, u32[]{:S(2)}) %all-to-all-start.4) | async-done | bytes 2359328 | tf_op jit(solution)/shard_map/all_to_all | solution.py:261
  1169.5 38.6 %all-to-all-done.5 = bf16[4,384,768]{2,1,0:T(8,128)(2,1)} async-done(((bf16[4,384,768]{2,1,0:T(8,128)(2,1)}), bf16[4,384,768]{2,1,0:T(8,128)(2,1)}, u32[]{:S(2)}, u32[]{:S(2)}) %all-to-all-start.5) | async-done | bytes 2359328 | tf_op jit(solution)/shard_map/all_to_all | solution.py:261
  1222.7 43.3 %all-to-all-done.7 = bf16[4,1152,256]{2,1,0:T(8,128)(2,1)} async-done(((bf16[4,1152,256]{2,1,0:T(8,128)(2,1)}), bf16[4,1152,256]{2,1,0:T(8,128)(2,1)}, u32[]{:S(2)}, u32[]{:S(2)}) %all-to-all-start.7) | async-done | bytes 2359328 | tf_op jit(solution)/shard_map/all_to_all | solution.py:261
  (1212 shorter events, 520.5 us)
Async XLA Ops:
  7.2 157.5 %all-gather.3.cloned.1.call-start = ((), (), s32[]{:S(2)}) async-start(), calls=%async_computation.9 | async-start | bytes 3538944 | tf_op jit(solution)/shard_map/all_gather | solution.py:297
  14.4 42.6 %collective-permute-start = (bf16[400,768]{1,0:T(8,128)(2,1)S(1)}, bf16[400,768]{1,0:T(8,128)(2,1)}, u32[]{:S(2)}, u32[]{:S(2)}) collective-permute-start(bf16[400,768]{1,0:T(8,128)(2,1)S(1)} %pad_maximum_fusion.39), channel_id=1, source_target_pairs={{0,8},{8,0},{16,24},{24,16},{1,9},{9,1},{17,25},{25,17},{2,10},{10... | collective-permute-start | bytes 1843208 | tf_op jit(solution)/shard_map/ppermute | solution.py:67
  17.5 44.1 %collective-permute-start.1 = (bf16[400,768]{1,0:T(8,128)(2,1)S(1)}, bf16[400,768]{1,0:T(8,128)(2,1)}, u32[]{:S(2)}, u32[]{:S(2)}) collective-permute-start(bf16[400,768]{1,0:T(8,128)(2,1)S(1)} %pad_maximum_fusion.39), channel_id=1, source_target_pairs={{0,16},{8,24},{16,0},{24,8},{1,17},{9,25},{17,1},{25,9},{2,18},{10... | collective-permute-start | bytes 1843208 | tf_op jit(solution)/shard_map/ppermute | solution.py:67
  20.1 41.5 %collective-permute-start.2 = (bf16[400,768]{1,0:T(8,128)(2,1)S(1)}, bf16[400,768]{1,0:T(8,128)(2,1)}, u32[]{:S(2)}, u32[]{:S(2)}) collective-permute-start(bf16[400,768]{1,0:T(8,128)(2,1)S(1)} %pad_maximum_fusion.39), channel_id=1, source_target_pairs={{0,24},{8,16},{16,8},{24,0},{1,25},{9,17},{17,9},{25,1},{2,26},{10... | collective-permute-start | bytes 1843208 | tf_op jit(solution)/shard_map/ppermute | solution.py:67
  20.1 44.1 %collective-permute-start.3 = (bf16[400,768]{1,0:T(8,128)(2,1)S(1)}, bf16[400,768]{1,0:T(8,128)(2,1)}, u32[]{:S(2)}, u32[]{:S(2)}) collective-permute-start(bf16[400,768]{1,0:T(8,128)(2,1)S(1)} %pad_maximum_fusion.39), channel_id=1, source_target_pairs={{0,1},{1,0},{2,3},{3,2},{4,5},{5,4},{6,7},{7,6},{8,9},{9,8},{10,11... | collective-permute-start | bytes 1843208 | tf_op jit(solution)/shard_map/ppermute | solution.py:67
  66.5 39.2 %collective-permute-start.6 = (bf16[400,768]{1,0:T(8,128)(2,1)}, bf16[400,768]{1,0:T(8,128)(2,1)S(1)}, u32[]{:S(2)}, u32[]{:S(2)}) collective-permute-start(bf16[400,768]{1,0:T(8,128)(2,1)} %collective-permute-done.2), channel_id=1, source_target_pairs={{0,1},{1,0},{2,3},{3,2},{4,5},{5,4},{6,7},{7,6},{8,9},{9,8},{10,11... | collective-permute-start | bytes 1843208 | tf_op jit(solution)/shard_map/ppermute | solution.py:67
  129.8 82.8 %all-to-all-start = ((bf16[4,256,1152]{2,1,0:T(8,128)(2,1)}), bf16[4,256,1152]{2,1,0:T(8,128)(2,1)}, u32[]{:S(2)}, u32[]{:S(2)}) async-start(bf16[4,256,1152]{2,1,0:T(8,128)(2,1)} %get-tuple-element.160), calls=%async_computation | async-start | bytes 4718592 | tf_op jit(solution)/shard_map/all_to_all | solution.py:261
  220.1 287.6 %collective-permute-start.18 = (bf16[152,2048]{1,0:T(8,128)(2,1)}, bf16[152,2048]{1,0:T(8,128)(2,1)}, u32[]{:S(2)}, u32[]{:S(2)}) collective-permute-start(bf16[152,2048]{1,0:T(8,128)(2,1)} %maximum_maximum_fusion.7), channel_id=1, source_target_pairs={{0,4},{2,6},{4,0},{6,2},{1,5},{3,7},{5,1},{7,3},{8,12},{10,14},{12... | collective-permute-start | bytes 1867784 | tf_op jit(solution)/shard_map/ppermute | solution.py:67
  257.4 129.2 %all-to-all-start.1 = ((bf16[4,256,1152]{2,1,0:T(8,128)(2,1)}), bf16[4,256,1152]{2,1,0:T(8,128)(2,1)S(1)}, u32[]{:S(2)}, u32[]{:S(2)}) async-start(bf16[4,256,1152]{2,1,0:T(8,128)(2,1)} %get-tuple-element.164), calls=%async_computation.1 | async-start | bytes 4718592 | tf_op jit(solution)/shard_map/all_to_all | solution.py:261
  261.0 52.7 %collective-permute-start.27 = (bf16[152,2048]{1,0:T(8,128)(2,1)}, bf16[152,2048]{1,0:T(8,128)(2,1)S(1)}, u32[]{:S(2)}, u32[]{:S(2)}) collective-permute-start(bf16[152,2048]{1,0:T(8,128)(2,1)} %maximum_maximum_fusion.8), channel_id=1, source_target_pairs={{0,8},{8,0},{16,24},{24,16},{1,9},{9,1},{17,25},{25,17},{2,10},{10... | collective-permute-start | bytes 1867784 | tf_op jit(solution)/shard_map/ppermute | solution.py:67
  266.3 89.5 %collective-permute-start.21 = (bf16[152,2048]{1,0:T(8,128)(2,1)}, bf16[152,2048]{1,0:T(8,128)(2,1)S(1)}, u32[]{:S(2)}, u32[]{:S(2)}) collective-permute-start(bf16[152,2048]{1,0:T(8,128)(2,1)} %maximum_maximum_fusion.8), channel_id=1, source_target_pairs={{0,16},{8,24},{16,0},{24,8},{1,17},{9,25},{17,1},{25,9},{2,18},{10... | collective-permute-start | bytes 1867784 | tf_op jit(solution)/shard_map/ppermute | solution.py:67
  268.6 87.7 %collective-permute-start.14 = (bf16[152,2048]{1,0:T(8,128)(2,1)}, bf16[152,2048]{1,0:T(8,128)(2,1)S(1)}, u32[]{:S(2)}, u32[]{:S(2)}) collective-permute-start(bf16[152,2048]{1,0:T(8,128)(2,1)} %maximum_maximum_fusion.8), channel_id=1, source_target_pairs={{0,24},{8,16},{16,8},{24,0},{1,25},{9,17},{17,9},{25,1},{2,26},{10... | collective-permute-start | bytes 1867784 | tf_op jit(solution)/shard_map/ppermute | solution.py:67
  271.7 112.6 %collective-permute-start.12 = (bf16[304,2048]{1,0:T(8,128)(2,1)S(1)}, bf16[304,2048]{1,0:T(8,128)(2,1)S(1)}, u32[]{:S(2)}, u32[]{:S(2)}) collective-permute-start(bf16[304,2048]{1,0:T(8,128)(2,1)S(1)} %pad_maximum_fusion.11), channel_id=1, source_target_pairs={{0,2},{2,0},{4,6},{6,4},{1,3},{3,1},{5,7},{7,5},{8,10},{10,8},{12,... | collective-permute-start | bytes 3735560 | tf_op jit(solution)/shard_map/ppermute | solution.py:67
  313.7 46.6 %collective-permute-start.28 = (bf16[152,2048]{1,0:T(8,128)(2,1)S(1)}, bf16[152,2048]{1,0:T(8,128)(2,1)S(1)}, u32[]{:S(2)}, u32[]{:S(2)}) collective-permute-start(bf16[152,2048]{1,0:T(8,128)(2,1)S(1)} %collective-permute-done.27), channel_id=1, source_target_pairs={{0,4},{2,6},{4,0},{6,2},{1,5},{3,7},{5,1},{7,3},{8,12},{10,14},{12... | collective-permute-start | bytes 1867784 | tf_op jit(solution)/shard_map/ppermute | solution.py:67
  360.4 51.7 %collective-permute-start.13 = (bf16[4,256,1152]{2,1,0:T(8,128)(2,1)}, bf16[4,256,1152]{2,1,0:T(8,128)(2,1)}, u32[]{:S(2)}, u32[]{:S(2)}) collective-permute-start(bf16[4,256,1152]{2,1,0:T(8,128)(2,1)} %all-to-all-done), channel_id=1, source_target_pairs={{0,1},{1,0},{2,3},{3,2},{4,5},{5,4},{6,7},{7,6},{8,9},{9,8},{10,11... | collective-permute-start | bytes 7077896 | tf_op jit(solution)/shard_map/ppermute | solution.py:67
  372.8 52.7 %collective-permute-start.29 = (bf16[304,2048]{1,0:T(8,128)(2,1)}, bf16[304,2048]{1,0:T(8,128)(2,1)}, u32[]{:S(2)}, u32[]{:S(2)}) collective-permute-start(bf16[304,2048]{1,0:T(8,128)(2,1)} %pad_maximum_fusion.16), channel_id=1, source_target_pairs={{0,2},{2,0},{4,6},{6,4},{1,3},{3,1},{5,7},{7,5},{8,10},{10,8},{12,... | collective-permute-start | bytes 3735560 | tf_op jit(solution)/shard_map/ppermute | solution.py:67
  383.0 45.4 %collective-permute-start.23 = (bf16[304,2048]{1,0:T(8,128)(2,1)}, bf16[304,2048]{1,0:T(8,128)(2,1)}, u32[]{:S(2)}, u32[]{:S(2)}) collective-permute-start(bf16[304,2048]{1,0:T(8,128)(2,1)} %pad_maximum_fusion.14), channel_id=1, source_target_pairs={{0,2},{2,0},{4,6},{6,4},{1,3},{3,1},{5,7},{7,5},{8,10},{10,8},{12,... | collective-permute-start | bytes 3735560 | tf_op jit(solution)/shard_map/ppermute | solution.py:67
  384.3 47.1 %collective-permute-start.16 = (bf16[304,2048]{1,0:T(8,128)(2,1)}, bf16[304,2048]{1,0:T(8,128)(2,1)}, u32[]{:S(2)}, u32[]{:S(2)}) collective-permute-start(bf16[304,2048]{1,0:T(8,128)(2,1)} %pad_maximum_fusion.12), channel_id=1, source_target_pairs={{0,2},{2,0},{4,6},{6,4},{1,3},{3,1},{5,7},{7,5},{8,10},{10,8},{12,... | collective-permute-start | bytes 3735560 | tf_op jit(solution)/shard_map/ppermute | solution.py:67
  386.6 86.6 %all-to-all-start.2 = ((bf16[4,1152,256]{2,1,0:T(8,128)(2,1)}), bf16[4,1152,256]{2,1,0:T(8,128)(2,1)}, u32[]{:S(2)}, u32[]{:S(2)}) async-start(bf16[4,1152,256]{2,1,0:T(8,128)(2,1)} %maximum_maximum_fusion.6), calls=%async_computation.2 | async-start | bytes 4718592 | tf_op jit(solution)/shard_map/all_to_all | solution.py:261
  412.1 53.6 %collective-permute-start.17 = (bf16[4,256,1152]{2,1,0:T(8,128)(2,1)S(1)}, bf16[4,256,1152]{2,1,0:T(8,128)(2,1)S(1)}, u32[]{:S(2)}, u32[]{:S(2)}) collective-permute-start(bf16[4,256,1152]{2,1,0:T(8,128)(2,1)S(1)} %all-to-all-done.1), channel_id=1, source_target_pairs={{0,1},{1,0},{2,3},{3,2},{4,5},{5,4},{6,7},{7,6},{8,9},{9,8},{10,11... | collective-permute-start | bytes 7077896 | tf_op jit(solution)/shard_map/ppermute | solution.py:67
  475.1 92.3 %collective-permute-start.20 = (bf16[4,1152,256]{2,1,0:T(8,128)(2,1)}, bf16[4,1152,256]{2,1,0:T(8,128)(2,1)S(1)}, u32[]{:S(2)}, u32[]{:S(2)}) collective-permute-start(bf16[4,1152,256]{2,1,0:T(8,128)(2,1)} %all-to-all-done.2), channel_id=1, source_target_pairs={{0,1},{1,0},{2,3},{3,2},{4,5},{5,4},{6,7},{7,6},{8,9},{9,8},{10,11... | collective-permute-start | bytes 7077896 | tf_op jit(solution)/shard_map/ppermute | solution.py:67
  495.9 44.8 %collective-permute-start.30 = (bf16[152,2048]{1,0:T(8,128)(2,1)}, bf16[152,2048]{1,0:T(8,128)(2,1)S(1)}, u32[]{:S(2)}, u32[]{:S(2)}) collective-permute-start(bf16[152,2048]{1,0:T(8,128)(2,1)} %maximum_maximum_fusion.7), channel_id=1, source_target_pairs={{0,16},{8,24},{16,0},{24,8},{1,17},{9,25},{17,1},{25,9},{2,18},{10... | collective-permute-start | bytes 1867784 | tf_op jit(solution)/shard_map/ppermute | solution.py:67
  495.9 47.6 %collective-permute-start.34 = (bf16[152,2048]{1,0:T(8,128)(2,1)}, bf16[152,2048]{1,0:T(8,128)(2,1)S(1)}, u32[]{:S(2)}, u32[]{:S(2)}) collective-permute-start(bf16[152,2048]{1,0:T(8,128)(2,1)} %maximum_maximum_fusion.7), channel_id=1, source_target_pairs={{0,24},{8,16},{16,8},{24,0},{1,25},{9,17},{17,9},{25,1},{2,26},{10... | collective-permute-start | bytes 1867784 | tf_op jit(solution)/shard_map/ppermute | solution.py:67
  509.1 49.3 %collective-permute-start.19 = (bf16[304,2048]{1,0:T(8,128)(2,1)S(1)}, bf16[304,2048]{1,0:T(8,128)(2,1)S(1)}, u32[]{:S(2)}, u32[]{:S(2)}) collective-permute-start(bf16[304,2048]{1,0:T(8,128)(2,1)S(1)} %pad_maximum_fusion.13), channel_id=1, source_target_pairs={{0,2},{2,0},{4,6},{6,4},{1,3},{3,1},{5,7},{7,5},{8,10},{10,8},{12,... | collective-permute-start | bytes 3735560 | tf_op jit(solution)/shard_map/ppermute | solution.py:67
  545.5 38.4 %collective-permute-start.26 = (bf16[304,2048]{1,0:T(8,128)(2,1)S(1)}, bf16[304,2048]{1,0:T(8,128)(2,1)S(1)}, u32[]{:S(2)}, u32[]{:S(2)}) collective-permute-start(bf16[304,2048]{1,0:T(8,128)(2,1)S(1)} %pad_maximum_fusion.15), channel_id=1, source_target_pairs={{0,2},{2,0},{4,6},{6,4},{1,3},{3,1},{5,7},{7,5},{8,10},{10,8},{12,... | collective-permute-start | bytes 3735560 | tf_op jit(solution)/shard_map/ppermute | solution.py:67
  551.6 56.6 %collective-permute-start.32 = (bf16[304,2048]{1,0:T(8,128)(2,1)S(1)}, bf16[304,2048]{1,0:T(8,128)(2,1)S(1)}, u32[]{:S(2)}, u32[]{:S(2)}) collective-permute-start(bf16[304,2048]{1,0:T(8,128)(2,1)S(1)} %pad_maximum_fusion.17), channel_id=1, source_target_pairs={{0,2},{2,0},{4,6},{6,4},{1,3},{3,1},{5,7},{7,5},{8,10},{10,8},{12,... | collective-permute-start | bytes 3735560 | tf_op jit(solution)/shard_map/ppermute | solution.py:67
  558.3 59.6 %collective-permute-start.36 = (bf16[304,2048]{1,0:T(8,128)(2,1)S(1)}, bf16[304,2048]{1,0:T(8,128)(2,1)S(1)}, u32[]{:S(2)}, u32[]{:S(2)}) collective-permute-start(bf16[304,2048]{1,0:T(8,128)(2,1)S(1)} %pad_maximum_fusion.19), channel_id=1, source_target_pairs={{0,2},{2,0},{4,6},{6,4},{1,3},{3,1},{5,7},{7,5},{8,10},{10,8},{12,... | collective-permute-start | bytes 3735560 | tf_op jit(solution)/shard_map/ppermute | solution.py:67
  671.2 52.1 %collective-permute-start.41 = (bf16[152,2048]{1,0:T(8,128)(2,1)}, bf16[152,2048]{1,0:T(8,128)(2,1)}, u32[]{:S(2)}, u32[]{:S(2)}) collective-permute-start(bf16[152,2048]{1,0:T(8,128)(2,1)} %pad_maximum_fusion.36), channel_id=1, source_target_pairs={{0,4},{2,6},{4,0},{6,2},{1,5},{3,7},{5,1},{7,3},{8,12},{10,14},{12... | collective-permute-start | bytes 1867784 | tf_op jit(solution)/shard_map/ppermute | solution.py:67
  714.1 44.3 %collective-permute-start.44 = (bf16[152,2048]{1,0:T(8,128)(2,1)}, bf16[152,2048]{1,0:T(8,128)(2,1)}, u32[]{:S(2)}, u32[]{:S(2)}) collective-permute-start(bf16[152,2048]{1,0:T(8,128)(2,1)} %add_convert_fusion.11), channel_id=1, source_target_pairs={{0,8},{8,0},{16,24},{24,16},{1,9},{9,1},{17,25},{25,17},{2,10},{10... | collective-permute-start | bytes 1867784 | tf_op jit(solution)/shard_map/ppermute | solution.py:67
  721.7 110.1 %collective-permute-start.50 = (bf16[4,256,1152]{2,1,0:T(8,128)(2,1)}, bf16[4,256,1152]{2,1,0:T(8,128)(2,1)}, u32[]{:S(2)}, u32[]{:S(2)}) collective-permute-start(bf16[4,256,1152]{2,1,0:T(8,128)(2,1)} %get-tuple-element.367), channel_id=1, source_target_pairs={{0,1},{1,0},{2,3},{3,2},{4,5},{5,4},{6,7},{7,6},{8,9},{9,8},{10,11... | collective-permute-start | bytes 7077896 | tf_op jit(solution)/shard_map/ppermute | solution.py:67
  745.4 43.3 %collective-permute-start.45 = (bf16[152,2048]{1,0:T(8,128)(2,1)S(1)}, bf16[152,2048]{1,0:T(8,128)(2,1)S(1)}, u32[]{:S(2)}, u32[]{:S(2)}) collective-permute-start(bf16[152,2048]{1,0:T(8,128)(2,1)S(1)} %add_convert_fusion.10), channel_id=1, source_target_pairs={{0,16},{8,24},{16,0},{24,8},{1,17},{9,25},{17,1},{25,9},{2,18},{10... | collective-permute-start | bytes 1867784 | tf_op jit(solution)/shard_map/ppermute | solution.py:67
  749.1 39.6 %collective-permute-start.46 = (bf16[152,2048]{1,0:T(8,128)(2,1)}, bf16[152,2048]{1,0:T(8,128)(2,1)}, u32[]{:S(2)}, u32[]{:S(2)}) collective-permute-start(bf16[152,2048]{1,0:T(8,128)(2,1)} %add_convert_fusion.9), channel_id=1, source_target_pairs={{0,24},{8,16},{16,8},{24,0},{1,25},{9,17},{17,9},{25,1},{2,26},{10... | collective-permute-start | bytes 1867784 | tf_op jit(solution)/shard_map/ppermute | solution.py:67
  757.1 194.8 %collective-permute-start.54 = (bf16[4,256,1152]{2,1,0:T(8,128)(2,1)}, bf16[4,256,1152]{2,1,0:T(8,128)(2,1)}, u32[]{:S(2)}, u32[]{:S(2)}) collective-permute-start(bf16[4,256,1152]{2,1,0:T(8,128)(2,1)} %get-tuple-element.365), channel_id=1, source_target_pairs={{0,1},{1,0},{2,3},{3,2},{4,5},{5,4},{6,7},{7,6},{8,9},{9,8},{10,11... | collective-permute-start | bytes 7077896 | tf_op jit(solution)/shard_map/ppermute | solution.py:67
  830.1 295.0 %collective-permute-start.66 = (bf16[4,1152,256]{2,1,0:T(8,128)(2,1)}, bf16[4,1152,256]{2,1,0:T(8,128)(2,1)}, u32[]{:S(2)}, u32[]{:S(2)}) collective-permute-start(bf16[4,1152,256]{2,1,0:T(8,128)(2,1)} %get-tuple-element.360), channel_id=1, source_target_pairs={{0,1},{1,0},{2,3},{3,2},{4,5},{5,4},{6,7},{7,6},{8,9},{9,8},{10,11... | collective-permute-start | bytes 7077896 | tf_op jit(solution)/shard_map/ppermute | solution.py:67
  863.8 88.1 %collective-permute-start.55 = (bf16[4,152,2048]{2,1,0:T(8,128)(2,1)}, bf16[4,152,2048]{2,1,0:T(8,128)(2,1)}, u32[]{:S(2)}, u32[]{:S(2)}) collective-permute-start(bf16[4,152,2048]{2,1,0:T(8,128)(2,1)} %pad_maximum_fusion.2), channel_id=1, source_target_pairs={{0,4},{2,6},{4,0},{6,2},{1,5},{3,7},{5,1},{7,3},{8,12},{10,14},{12... | collective-permute-start | bytes 7471112 | tf_op jit(solution)/shard_map/ppermute | solution.py:67
  868.2 78.2 %all-to-all-start.3 = ((bf16[4,256,1152]{2,1,0:T(8,128)(2,1)}), bf16[4,256,1152]{2,1,0:T(8,128)(2,1)}, u32[]{:S(2)}, u32[]{:S(2)}) async-start(bf16[4,256,1152]{2,1,0:T(8,128)(2,1)} %add_convert_fusion.4), calls=%async_computation.3 | async-start | bytes 4718592 | tf_op jit(solution)/shard_map/all_to_all | solution.py:261
  892.0 52.8 %collective-permute-start.68 = (bf16[4,512,384]{2,1,0:T(8,128)(2,1)S(1)}, bf16[4,512,384]{2,1,0:T(8,128)(2,1)S(1)}, u32[]{:S(2)}, u32[]{:S(2)}) collective-permute-start(bf16[4,512,384]{2,1,0:T(8,128)(2,1)S(1)} %dynamic-slice_bitcast_fusion.2), channel_id=1, source_target_pairs={{0,1},{1,0},{2,3},{3,2},{4,5},{5,4},{6,7},{7,6},{8,9},{9,8},{10,11... | collective-permute-start | bytes 4718600 | tf_op jit(solution)/shard_map/ppermute | solution.py:67
  897.1 38.1 %collective-permute-start.52 = (bf16[2,288,256]{2,1,0:T(8,128)(2,1)S(1)}, bf16[2,288,256]{2,1,0:T(8,128)(2,1)S(1)}, u32[]{:S(2)}, u32[]{:S(2)}) collective-permute-start(bf16[2,288,256]{2,1,0:T(8,128)(2,1)S(1)} %fusion.140), channel_id=1, source_target_pairs={{0,1},{1,0},{2,3},{3,2},{4,5},{5,4},{6,7},{7,6},{8,9},{9,8},{10,11... | collective-permute-start | bytes 884744 | tf_op jit(solution)/shard_map/ppermute | solution.py:67
  946.4 42.7 %all-to-all-start.6 = ((bf16[4,512,384]{2,1,0:T(8,128)(2,1)}), bf16[4,512,384]{2,1,0:T(8,128)(2,1)S(1)}, u32[]{:S(2)}, u32[]{:S(2)}) async-start(bf16[4,512,384]{2,1,0:T(8,128)(2,1)} %fusion.23), calls=%async_computation.6 | async-start | bytes 3145728 | tf_op jit(solution)/shard_map/all_to_all | solution.py:261
  958.6 166.5 %collective-permute-start.65 = (bf16[4,384,768]{2,1,0:T(8,128)(2,1)}, bf16[4,384,768]{2,1,0:T(8,128)(2,1)}, u32[]{:S(2)}, u32[]{:S(2)}) collective-permute-start(bf16[4,384,768]{2,1,0:T(8,128)(2,1)} %get-tuple-element.362), channel_id=1, source_target_pairs={{0,1},{1,0},{2,3},{3,2},{4,5},{5,4},{6,7},{7,6},{8,9},{9,8},{10,11... | collective-permute-start | bytes 7077896 | tf_op jit(solution)/shard_map/ppermute | solution.py:67
  971.6 57.6 %collective-permute-start.57 = (bf16[152,2048]{1,0:T(8,128)(2,1)}, bf16[152,2048]{1,0:T(8,128)(2,1)}, u32[]{:S(2)}, u32[]{:S(2)}) collective-permute-start(bf16[152,2048]{1,0:T(8,128)(2,1)} %get-tuple-element.393), channel_id=1, source_target_pairs={{0,16},{8,24},{16,0},{24,8},{1,17},{9,25},{17,1},{25,9},{2,18},{10... | collective-permute-start | bytes 1867784 | tf_op jit(solution)/shard_map/ppermute | solution.py:67
  974.0 55.2 %collective-permute-start.58 = (bf16[152,2048]{1,0:T(8,128)(2,1)}, bf16[152,2048]{1,0:T(8,128)(2,1)}, u32[]{:S(2)}, u32[]{:S(2)}) collective-permute-start(bf16[152,2048]{1,0:T(8,128)(2,1)} %get-tuple-element.392), channel_id=1, source_target_pairs={{0,24},{8,16},{16,8},{24,0},{1,25},{9,17},{17,9},{25,1},{2,26},{10... | collective-permute-start | bytes 1867784 | tf_op jit(solution)/shard_map/ppermute | solution.py:67
  1083.6 59.1 %all-to-all-start.4 = ((bf16[4,256,1152]{2,1,0:T(8,128)(2,1)}), bf16[4,256,1152]{2,1,0:T(8,128)(2,1)}, u32[]{:S(2)}, u32[]{:S(2)}) async-start(bf16[4,256,1152]{2,1,0:T(8,128)(2,1)} %add_convert_fusion.2), calls=%async_computation.4 | async-start | bytes 4718592 | tf_op jit(solution)/shard_map/all_to_all | solution.py:261
  1109.7 53.3 %collective-permute-start.64 = (bf16[2,152,2048]{2,1,0:T(8,128)(2,1)}, bf16[2,152,2048]{2,1,0:T(8,128)(2,1)}, u32[]{:S(2)}, u32[]{:S(2)}) collective-permute-start(bf16[2,152,2048]{2,1,0:T(8,128)(2,1)} %pad_maximum_fusion.32), channel_id=1, source_target_pairs={{0,2},{2,0},{4,6},{6,4},{1,3},{3,1},{5,7},{7,5},{8,10},{10,8},{12,... | collective-permute-start | bytes 3735560 | tf_op jit(solution)/shard_map/ppermute | solution.py:67
  1122.9 42.0 %collective-permute-start.60 = (bf16[2,152,2048]{2,1,0:T(8,128)(2,1)}, bf16[2,152,2048]{2,1,0:T(8,128)(2,1)}, u32[]{:S(2)}, u32[]{:S(2)}) collective-permute-start(bf16[2,152,2048]{2,1,0:T(8,128)(2,1)} %pad_maximum_fusion.30), channel_id=1, source_target_pairs={{0,2},{2,0},{4,6},{6,4},{1,3},{3,1},{5,7},{7,5},{8,10},{10,8},{12,... | collective-permute-start | bytes 3735560 | tf_op jit(solution)/shard_map/ppermute | solution.py:67
  1150.1 58.0 %all-to-all-start.5 = ((bf16[4,384,768]{2,1,0:T(8,128)(2,1)}), bf16[4,384,768]{2,1,0:T(8,128)(2,1)}, u32[]{:S(2)}, u32[]{:S(2)}) async-start(bf16[4,384,768]{2,1,0:T(8,128)(2,1)} %add_convert_fusion.1), calls=%async_computation.5 | async-start | bytes 4718592 | tf_op jit(solution)/shard_map/all_to_all | solution.py:261
  1208.1 57.9 %all-to-all-start.7 = ((bf16[4,1152,256]{2,1,0:T(8,128)(2,1)}), bf16[4,1152,256]{2,1,0:T(8,128)(2,1)}, u32[]{:S(2)}, u32[]{:S(2)}) async-start(bf16[4,1152,256]{2,1,0:T(8,128)(2,1)} %add_convert_fusion), calls=%async_computation.7 | async-start | bytes 4718592 | tf_op jit(solution)/shard_map/all_to_all | solution.py:261
  1222.7 49.4 %collective-permute-start.67 = (bf16[384,256]{1,0:T(8,128)(2,1)S(1)}, bf16[384,256]{1,0:T(8,128)(2,1)S(1)}, u32[]{:S(2)}, u32[]{:S(2)}) collective-permute-start(bf16[384,256]{1,0:T(8,128)(2,1)S(1)} %slice.3484), channel_id=1, source_target_pairs={{0,2},{2,0},{4,6},{6,4},{1,3},{3,1},{5,7},{7,5},{8,10},{10,8},{12,... | collective-permute-start | bytes 589832 | tf_op jit(solution)/shard_map/ppermute | solution.py:67
  (254 other events, 2835.2 us)
Sparse Core Ops, SparseCore 0:
  61.8 85.1 all-gather.2

commit v2 on v1

v2 whole, which is shorter than its diff:
```python
import functools

import jax
import jax.numpy as jnp
from jax import lax
from jax.experimental import pallas as pl
from jax.experimental.pallas import tpu as pltpu
from jax.sharding import PartitionSpec as P

HD = 256
EPSILON = 1e-06
PAD = 64
F32 = jnp.float32
BF16 = jnp.bfloat16


def rms_scale(values, gain):
    return values * lax.rsqrt(jnp.mean(values * values, axis=-1, keepdims=True) + EPSILON) * gain


def gelu_tanh(values):
    return jax.nn.gelu(values, approximate=True)


def geglu(gate, upward):
    return gelu_tanh(gate) * upward


def project(left, right):
    return jnp.dot(left, right, preferred_element_type=F32)


def project_back(left, right):
    return lax.dot_general(left, right, (((1,), (1,)), ((), ())), preferred_element_type=F32)


def outer_sum(left, right):
    return lax.dot_general(left, right, (((0,), (0,)), ((), ())), preferred_element_type=F32)


def norm_back(values, gain, cotangent):
    return jax.vjp(rms_scale, values, gain.astype(F32))[1](cotangent)


MIB = 1024 * 1024


def key_mask(shape, start, length, group, half_rows):
    place = lax.broadcasted_iota(jnp.int32, shape, 1)
    own = jnp.where(place < half_rows, group, 1 - group) * half_rows
    place = jnp.where(place < half_rows, place, place - half_rows) + own
    return place < length


def softmax_parts(scores):
    top = functools.reduce(jnp.maximum, [jnp.max(s, axis=1, keepdims=True) for s in scores])
    expo = [jnp.exp(s - top) for s in scores]
    denom = sum(jnp.sum(e, axis=1, keepdims=True) for e in expo)
    return [e / denom for e in expo]


def suffix_scores(q, keys, own_keys, live, later, scale):
    first = jnp.where(live, project_back(q, keys) * scale, -1e30)
    second = jnp.where(later, project_back(q, own_keys) * scale, -1e30)
    return softmax_parts([first, second])


def suffix_masks(suf_len, full, length, group, half_rows):
    live = key_mask((PAD, full), 0, length, group, half_rows)
    row = lax.broadcasted_iota(jnp.int32, (PAD, PAD), 0)
    column = lax.broadcasted_iota(jnp.int32, (PAD, PAD), 1)
    later = ((column == 0) | (row > 0)) & (column < suf_len)
    return live, later


def attend_kernel(items, heads, suf_len, info, q, qs, k, v, att, att_suf):
    scale = HD ** (-0.5)
    rows = q.shape[0] // items
    full = (k.shape[0] - PAD) // items
    group = info[0]
    for i in range(items):
        live = key_mask((rows, full), 0, info[1 + i], group, rows)
        for h in range(heads):
            at, keys = (slice(i * rows, (i + 1) * rows), slice(h * HD, (h + 1) * HD)), slice(i * full, (i + 1) * full)
            scores = jnp.where(live, project_back(q[at], k[keys]) * scale, -1e30)
            (probs,) = softmax_parts([scores])
            att[at] = project(probs.astype(BF16), v[keys]).astype(BF16)
    live, later = suffix_masks(suf_len, full, info[1 + items], group, rows)
    start = pl.multiple_of(group * full, full)
    keys, values = k[pl.ds(start, full)], v[pl.ds(start, full)]
    own_keys, own_values = k[items * full :], v[items * full :]
    for h in range(heads):
        at = (slice(None), slice(h * HD, (h + 1) * HD))
        first, second = suffix_scores(qs[at], keys, own_keys, live, later, scale)
        total = project(first.astype(BF16), values) + project(second.astype(BF16), own_values)
        att_suf[at] = total.astype(BF16)


def attend_back_kernel(items, heads, suf_len, info, q, qs, k, v, cot, cot_suf, qcot, qcot_suf, kcot, vcot):
    scale = HD ** (-0.5)
    rows = q.shape[0] // items
    full = (k.shape[0] - PAD) // items
    group = info[0]
    for i in range(items):
        live = key_mask((rows, full), 0, info[1 + i], group, rows)
        for h in range(heads):
            at, keys = (slice(i * rows, (i + 1) * rows), slice(h * HD, (h + 1) * HD)), slice(i * full, (i + 1) * full)
            scores = jnp.where(live, project_back(q[at], k[keys]) * scale, -1e30)
            (probs,) = softmax_parts([scores])
            grad = project_back(cot[at], v[keys])
            delta = jnp.sum(probs * grad, axis=1, keepdims=True)
            inner = (probs * (grad - delta)).astype(BF16)
            qcot[at] = (project(inner, k[keys]) * scale).astype(BF16)
            kterm = outer_sum(inner, q[at]) * scale
            vterm = outer_sum(probs.astype(BF16), cot[at])
            if h == 0:
                kcot[keys], vcot[keys] = kterm, vterm
            else:
                kcot[keys] += kterm
                vcot[keys] += vterm
    live, later = suffix_masks(suf_len, full, info[1 + items], group, rows)
    start = pl.multiple_of(group * full, full)
    own = slice(items * full, items * full + PAD)
    place = pl.ds(start, full)
    for h in range(heads):
        at = (slice(None), slice(h * HD, (h + 1) * HD))
        first, second = suffix_scores(qs[at], k[place], k[own], live, later, scale)
        grads = project_back(cot_suf[at], v[place]), project_back(cot_suf[at], v[own])
        delta = sum(jnp.sum(p * g, axis=1, keepdims=True) for p, g in zip((first, second), grads))
        inners = [(p * (g - delta)).astype(BF16) for p, g in zip((first, second), grads)]
        total = project(inners[0], k[place]) + project(inners[1], k[own])
        qcot_suf[at] = (total * scale).astype(BF16)
        kcot[place] += outer_sum(inners[0], qs[at]) * scale
        vcot[place] += outer_sum(first.astype(BF16), cot_suf[at])
        kterm = outer_sum(inners[1], qs[at]) * scale
        vterm = outer_sum(second.astype(BF16), cot_suf[at])
        if h == 0:
            kcot[own], vcot[own] = kterm, vterm
        else:
            kcot[own] += kterm
            vcot[own] += vterm


def attention_call(kernel, name, out_shape, items, heads, suf_len, info, *arrays):
    spec = pl.BlockSpec(memory_space=pltpu.VMEM)
    return pl.pallas_call(
        functools.partial(kernel, items, heads, suf_len),
        in_specs=[pl.BlockSpec(memory_space=pltpu.SMEM)] + [spec] * len(arrays),
        out_specs=[spec] * len(out_shape),
        out_shape=out_shape,
        compiler_params=pltpu.CompilerParams(vmem_limit_bytes=32 * MIB),
        name=name,
    )(info, *arrays)


def attend(info, q, qs, k, v, items, suf_len):
    shape = [jax.ShapeDtypeStruct(q.shape, BF16), jax.ShapeDtypeStruct(qs.shape, BF16)]
    heads = q.shape[1] // HD
    return attention_call(attend_kernel, "attend", shape, items, heads, suf_len, info, q, qs, k, v)


def attend_back(info, q, qs, k, v, cot, cot_suf, items, suf_len):
    shape = [jax.ShapeDtypeStruct(a.shape, t) for a, t in ((q, BF16), (qs, BF16), (k, F32), (v, F32))]
    heads = q.shape[1] // HD
    return attention_call(
        attend_back_kernel, "attend_back", shape, items, heads, suf_len, info, q, qs, k, v, cot, cot_suf
    )


def swap(value, axis, size, mask):
    return lax.ppermute(value, axis, [(i, i ^ mask) for i in range(size)])


def column_blocks(value, count):
    width = value.shape[1] // count
    return [value[:, i * width : (i + 1) * width] for i in range(count)]


def halves_down(value, axis):
    other = value.ndim - 1 if axis == value.ndim - 2 else value.ndim - 2
    size = value.shape[axis] // 2
    first = lax.slice_in_dim(value, 0, size, axis=axis)
    second = lax.slice_in_dim(value, size, 2 * size, axis=axis)
    return jnp.concatenate([first, second], axis=other)


def after(*values):
    return lax.optimization_barrier(values)


def own_first(value, dp, group):
    width = value.shape[1] // (2 * dp)
    zero = jnp.zeros((), value.dtype)
    right = lax.pad(value, zero, ((0, 0, 0), (-width, width, 0)))
    left = lax.pad(value, zero, ((0, 0, 0), (width, -width, 0)))
    block = lax.broadcasted_iota(jnp.int32, value.shape, 1) // width
    return jnp.where(group == 0, value, jnp.where(block % 2 == 0, right, left))


class Rows:
    def __init__(self, part, suf_part, width, act_width, core, x_index):
        self.part, self.suf_part, self.core, self.x_index = part, suf_part, core, x_index
        self.width, self.act_width = width, act_width

    def join(self, pre, suf):
        zero = jnp.zeros((), suf.dtype)
        suf = lax.pad(suf, zero, ((0, 0, 0), (0, self.width - self.act_width, 0)))
        pre = pre.reshape(-1, self.part, self.width)
        return jnp.concatenate([pre, suf.reshape(-1, self.suf_part, self.width)], axis=1)

    def split(self, blocks):
        pre = blocks[:, : self.part].reshape(-1, self.width)
        return pre, blocks[:, self.part :, : self.act_width].reshape(-1, self.act_width)

    def tp_sum(self, pre, suf):
        whole = self.join(pre.astype(BF16), suf.astype(BF16))
        whole = whole.reshape(2, 2, -1, self.width)

        def pick(value, index, axis):
            return lax.dynamic_index_in_dim(value, index, axis, keepdims=False)

        got = swap(pick(whole, 1 - self.core, 1), "tp", 4, 1)
        pair = pick(whole, self.core, 1).astype(F32) + got.astype(F32)
        got = swap(pick(pair, 1 - self.x_index, 0).astype(BF16), "tp", 4, 2)
        return self.split((pick(pair, self.x_index, 0) + got.astype(F32))[None])

    def tp_gather(self, block):
        other = swap(block, "tp", 4, 2)
        low = jnp.where(self.x_index == 0, block, other)
        high = jnp.where(self.x_index == 0, other, block)
        pair = jnp.concatenate([low, high], axis=0)
        got = swap(pair, "tp", 4, 1)
        even = jnp.where(self.core == 0, pair, got)
        odd = jnp.where(self.core == 0, got, pair)
        return self.split(jnp.stack([even, odd], axis=1).reshape(4, -1, self.width))

    def spread(self, block, far):
        pair = jnp.concatenate([block, far], axis=0)
        return self.split(jnp.concatenate([pair, swap(pair, "tp", 4, 1)], axis=0))

    def first(self, pre, suf):
        whole = self.join(pre, suf).reshape(-1, 4, self.part + self.suf_part, self.width)
        return whole[:, :2], whole[:, 2:]

    def second(self, keep, got):
        pair = keep.astype(F32) + got.astype(F32)
        return pair[:, 0], pair[:, 1].astype(BF16)

    def third(self, keep, got):
        return keep + got.astype(F32)


def local(
    dp,
    prefix_in,
    suffix_in,
    noisy_actions,
    prefix_len,
    action_live,
    pre_query,
    pre_keyval,
    pre_output,
    pre_gate,
    pre_up,
    pre_down,
    pre_norm_attn,
    pre_norm_ffn,
    act_query,
    act_keyval,
    act_output,
    act_gate,
    act_up,
    act_down,
    act_norm_attn,
    act_norm_ffn,
    action_embed,
    prefix_cot,
    suffix_cot,
):
    shards = 2 * dp
    both = ("dp", "expert")
    group = lax.axis_index("expert")
    t_index = lax.axis_index("tp")
    core, x_index = lax.rem(t_index, 2), t_index // 2
    pre_items, half_rows, width = prefix_in.shape
    _, suf_len, act_width = suffix_in.shape
    rows = pre_items * half_rows
    part = rows // 4
    suf_part = PAD // 4
    pack = Rows(part, suf_part, width, act_width, core, x_index)
    d_slice, q_cols = pre_query.shape
    a_slice = act_query.shape[0]
    hid = pre_gate.shape[1] // dp
    hid_act = act_gate.shape[1] // dp

    def half_cols(value):
        return lax.dynamic_slice_in_dim(value, core * HD, HD, 1)

    w1 = q_cols + HD
    small = [pre_norm_attn, pre_norm_ffn, act_norm_attn, act_norm_ffn, action_embed.reshape(-1)]
    small = jnp.concatenate(small)
    small_rows = -(-small.shape[0] // (16 * w1)) * 16
    small = jnp.pad(small, (0, small_rows * w1 - small.shape[0])).reshape(small_rows, w1)
    packed_in = jnp.concatenate(
        [
            jnp.concatenate([pre_query, half_cols(pre_keyval)], axis=1),
            jnp.concatenate([act_query, half_cols(act_keyval)], axis=1),
            small,
        ],
        axis=0,
    )
    z_index = lax.axis_index("dp")
    in_z = [packed_in] + [swap(packed_in, "dp", dp, d) for d in range(1, dp)]
    in_far = [swap(packed_in, "expert", 2, 1)]

    def columns_out(pre, act):
        act_blocks = halves_down(jnp.stack(column_blocks(act, dp)), 2)
        return jnp.concatenate([jnp.stack(column_blocks(pre, dp)), act_blocks], axis=2)

    def columns_in(moved, pre, act):
        halves = jnp.stack(moved, axis=1)
        w_pre = halves[..., :hid].reshape(width, hid)
        w_act = halves_down(halves[..., hid:], 2).reshape(act_width, hid_act)
        return w_pre, w_act

    def dp_move(value):
        return lax.all_to_all(value, "dp", 0, 0, tiled=True)

    gate_out = columns_out(pre_gate, act_gate)
    up_out = columns_out(pre_up, act_up)
    down_out = jnp.concatenate(
        [
            pre_down.reshape(dp, hid, d_slice),
            halves_down(act_down.reshape(dp, hid_act, a_slice), 1),
        ],
        axis=1,
    )
    packed_out = jnp.concatenate([pre_output, act_output], axis=1)

    def own_rows(value):
        return lax.dynamic_slice_in_dim(value, t_index * part, part, 0)

    def own_suffix(value):
        return lax.dynamic_slice_in_dim(value, t_index * suf_part, suf_part, 0)

    def pad_suffix(value):
        return jnp.pad(value, ((0, PAD - suf_len), (0, 0)))

    def own_block(pre, suf):
        return pack.join(own_first(pre, dp, group), own_first(suf, dp, group))

    def undo_block(block):
        pre, suf = pack.split(block)
        return own_first(pre, dp, group), own_first(suf, dp, group)

    cot_mine = own_rows(prefix_cot.reshape(rows, width))
    cot_suf_mine = own_suffix(pad_suffix(suffix_cot[0]))
    cot_block = own_block(cot_mine, cot_suf_mine)

    gate_own = dp_move(gate_out)
    *in_z, gate_own, packed_out = after(*in_z, gate_own, packed_out)
    in_far += [swap(block, "expert", 2, 1) for block in in_z[1:]]
    full_out = lax.all_gather(packed_out, both, axis=0)
    *in_far, up_out = after(*in_far, up_out)
    up_own = dp_move(up_out)
    full_in = jnp.zeros((dp, 2) + packed_in.shape, BF16)
    for d in range(dp):
        z = jnp.bitwise_xor(z_index, d)
        full_in = lax.dynamic_update_slice(full_in, in_z[d][None, None], (z, group, 0, 0))
        full_in = lax.dynamic_update_slice(full_in, in_far[d][None, None], (z, 1 - group, 0, 0))
    full_in = full_in.reshape((shards,) + packed_in.shape)

    w_pq = full_in[:, :d_slice, :q_cols].reshape(width, q_cols)
    w_pkv = full_in[:, :d_slice, q_cols:].reshape(width, HD)
    w_aq = full_in[:, d_slice : d_slice + a_slice, :q_cols].reshape(act_width, q_cols)
    w_akv = full_in[:, d_slice : d_slice + a_slice, q_cols:].reshape(act_width, HD)
    rest = full_in[:, d_slice + a_slice :].reshape(shards, small_rows * w1)
    gains, at = [], 0
    for size in (d_slice, d_slice, a_slice, a_slice):
        gains.append(rest[:, at : at + size].reshape(1, shards * size).astype(F32))
        at += size
    gain_pa, gain_pf, gain_aa, gain_af = gains
    embed = rest[:, at : at + action_embed.size].reshape(-1, act_width)
    prefix_x = prefix_in.astype(F32).reshape(rows, width)
    chosen = jnp.where(
        action_live[0][None, :] == 1, noisy_actions[0], jnp.zeros_like(noisy_actions[0])
    )
    chosen = jnp.pad(chosen, ((1, PAD - suf_len), (0, 0)))
    suffix_x = pad_suffix(suffix_in[0].astype(F32)) + project(chosen, embed)
    normed_pre = rms_scale(prefix_x, gain_pa).astype(BF16)
    normed_suf = rms_scale(suffix_x, gain_aa).astype(BF16)
    kv_pre = project(normed_pre, w_pkv).astype(BF16)
    kv_pre = kv_pre.reshape(pre_items, half_rows, HD)
    kv_got = swap(kv_pre, "expert", 2, 1)
    kv_suf = project(normed_suf, w_akv).astype(BF16)
    queries_pre = project(normed_pre, w_pq).astype(BF16)
    queries_suf = project(normed_suf, w_aq).astype(BF16)
    queries_pre, queries_suf, kv_suf, kv_got, gate_own = after(
        queries_pre, queries_suf, kv_suf, kv_got, gate_own
    )
    gate_got = swap(gate_own, "expert", 2, 1)
    kv_pre = jnp.concatenate([kv_pre, kv_got], axis=1)
    full_len = kv_pre.shape[1]
    kv_mine = jnp.concatenate([kv_pre.reshape(pre_items * full_len, HD), kv_suf], axis=0)
    kv_other = swap(kv_mine, "tp", 4, 1)
    keys = jnp.where(core == 0, kv_mine, kv_other)
    values = jnp.where(core == 0, kv_other, kv_mine)

    own_len = lax.dynamic_slice_in_dim(prefix_len, group, 1)
    info = jnp.concatenate([group.reshape(1).astype(jnp.int32), prefix_len, own_len])
    att_pre, att_suf = attend(info, queries_pre, queries_suf, keys, values, pre_items, suf_len)
    att_pre, att_suf, full_out = after(att_pre, att_suf, full_out)
    w_po = jnp.concatenate([full_out[i, :, :d_slice] for i in range(shards)], axis=1)
    w_ao = jnp.concatenate([full_out[i, :, d_slice:] for i in range(shards)], axis=1)
    x_mine = own_rows(prefix_in.reshape(rows, width)).astype(F32)
    xs_mine = own_suffix(suffix_x)
    branch = pack.tp_sum(project(att_pre, w_po), project(att_suf, w_ao))
    branch, branch_suf = branch
    resid = x_mine + branch
    resid_suf = xs_mine + branch_suf
    normed_block = own_block(
        rms_scale(resid, gain_pf).astype(BF16), rms_scale(resid_suf, gain_af).astype(BF16)
    )

    normed_far = swap(normed_block, "tp", 4, 2)
    normed_z = [normed_block] + [swap(normed_block, "dp", dp, d) for d in range(1, dp)]
    normed_far, up_own, gate_got = after(normed_far, up_own, gate_got)
    up_got = swap(up_own, "expert", 2, 1)
    *normed_z, down_out = after(*normed_z, down_out)
    down_own = dp_move(down_out)
    w_pg, w_ag = columns_in((gate_own, gate_got), pre_gate, act_gate)
    normed_chunks, gates, inner_terms = [], [], []

    def gelu_terms(gate):
        value, pull = jax.vjp(gelu_tanh, gate)
        return value, pull(jnp.ones_like(gate))[0]

    def scale_terms(gate, upward):
        value, slope = gate
        return (value * upward).astype(BF16), upward * slope, value

    for d in range(dp):
        far = normed_far if d == 0 else swap(normed_z[d], "tp", 4, 2)
        pre, suf = pack.spread(normed_z[d], far)
        if d > 0:
            pre, suf, *gates[-1] = after(pre, suf, *gates[-1])
        normed_chunks.append((pre, suf))
        gates.append((gelu_terms(project(pre, w_pg)), gelu_terms(project(suf, w_ag))))
    gates[-1], up_got = after(gates[-1], up_got)
    w_pu, w_au = columns_in((up_own, up_got), pre_up, act_up)
    for d in range(dp):
        pre, suf = normed_chunks[d]
        terms = scale_terms(gates[d][0], project(pre, w_pu))
        terms += scale_terms(gates[d][1], project(suf, w_au))
        inner_terms.append(after(*terms))
    cot_far = swap(cot_block, "tp", 4, 2)
    inner_terms[0], cot_far = after(inner_terms[0], cot_far)
    cot_chunks = [pack.spread(cot_block, cot_far)]
    inner_terms[0], cot_block, down_own = after(inner_terms[0], cot_block, down_own)
    down_got = swap(down_own, "expert", 2, 1)
    cot_z = [swap(cot_block, "dp", dp, d) for d in range(1, dp)]
    cot_chunks += [pack.spread(z, swap(z, "tp", 4, 2)) for z in cot_z]
    down = jnp.stack([down_own, down_got], axis=1).reshape(shards, hid + hid_act // 2, d_slice)
    w_pd = jnp.concatenate([down[i, :hid] for i in range(shards)], axis=1)
    act_down_blocks = halves_down(down[:, hid:], 2)
    w_ad = jnp.concatenate([act_down_blocks[i] for i in range(shards)], axis=1)

    def inner(terms, cot, w_d):
        hidden, gate_term, up_term = terms
        grad = project_back(cot, w_d)
        return hidden, (grad * gate_term).astype(BF16), (grad * up_term).astype(BF16)

    def back(gate_cot, up_cot, w_g, w_u):
        return (project_back(gate_cot, w_g) + project_back(up_cot, w_u)).astype(BF16)

    inners, inners_suf, pairs, sent, homes = {}, {}, {}, {}, {}

    def partial_of(d):
        pre = back(*inners[d][1:], w_pg, w_pu)
        suf = back(*inners_suf[d][1:], w_ag, w_au)
        return pre, suf

    def inner_of(d, *ties):
        cot, cot_suf = cot_chunks[d]
        terms, cot, *ties = after(inner_terms[d], cot, *ties)
        inners[d] = inner(terms[:3], cot, w_pd)
        inners_suf[d] = inner(terms[3:], cot_suf, w_ad)
        return ties

    order = list(range(1, dp)) + [0]
    inner_of(0)
    last = inners[0][0]
    for i, d in enumerate(order):
        if d > 0:
            inner_of(d, last)
        if i > 0:
            e = order[i - 1]
            *inners[d], pairs[e] = after(*inners[d], pairs[e])
            keep, got = pairs[e][0], pairs[e][1]
            keep, send = pack.second(keep, got)
            *inners[d], send = after(*inners[d], send)
            pairs[e] = keep, swap(send, "tp", 4, 2)
        pre, suf = partial_of(d)
        last = pre
        keep, send = pack.first(pre, suf)
        pairs[d] = keep, swap(send, "tp", 4, 1)
        if i > 1:
            e = order[i - 2]
            *pairs[d], keep, got = after(*pairs[d], *pairs[e])
            homes[e] = swap(pack.third(keep, got).astype(BF16), "dp", dp, e)
    def joined(values):
        return values if dp > 4 else [jnp.concatenate(values, axis=0)]

    def outer_chunks(left, right):
        return sum(outer_sum(a, b) for a, b in zip(joined(left), joined(right)))

    def columns_back(i):
        pre = outer_chunks([n[0] for n in normed_late], [inners[d][i] for d in range(dp)])
        act = outer_chunks([n[1] for n in normed_late], [inners_suf[d][i] for d in range(dp)])
        pre = pre.astype(BF16).reshape(shards, d_slice, hid)
        act = halves_down(act.astype(BF16).reshape(shards, a_slice, hid_act), 2)
        whole = jnp.concatenate([pre, act], axis=2).reshape(dp, 2, d_slice, -1)
        return whole[:, 0], whole[:, 1]

    def both_sum(own, got):
        return (own.astype(F32) + got.astype(F32)).astype(BF16)

    def columns_end(whole):
        pre = jnp.concatenate([whole[i, :, :hid] for i in range(dp)], axis=1)
        act = halves_down(whole[:, :, hid:], 1)
        act = jnp.concatenate([act[i] for i in range(dp)], axis=1)
        return pre.astype(F32), act.astype(F32)

    hiddens = [inners[d][0] for d in range(dp)]
    hid_suf = [inners_suf[d][0] for d in range(dp)]
    last, normed_late, cot_late, pairs[0] = after(last, normed_chunks, cot_chunks, pairs[0])
    keep, send = pack.second(*pairs[0])
    pairs[0] = keep, swap(send, "tp", 4, 2)
    normed_late, send = after(normed_late, send)
    gate_own, gate_send = columns_back(1)
    gate_got = swap(gate_send, "expert", 2, 1)
    for e in order[-2:-1]:
        gate_send, keep, got = after(gate_send, *pairs[e])
        homes[e] = swap(pack.third(keep, got).astype(BF16), "dp", dp, e)
    hiddens, gate_send = after(hiddens, gate_send)
    outs = jnp.concatenate([project(h, w_pd).astype(BF16) for h in hiddens], axis=0)
    outs_suf = project(jnp.concatenate(hid_suf, axis=0), w_ad).astype(BF16)
    outs_keep, outs_send = pack.first(outs, outs_suf)
    outs_got = swap(outs_send, "tp", 4, 1)
    outs_got, keep, got, normed_late = after(outs_got, *pairs[0], normed_late)
    home = pack.third(keep, got)
    outs_keep, outs_send = pack.second(outs_keep, outs_got)
    outs_got = swap(outs_send, "tp", 4, 2)
    up_own, up_send = columns_back(2)

    for d in range(1, dp):
        home = home + homes[d].astype(F32)
    mcot, mcot_suf = undo_block(home)
    mid_part, ffn_gain = norm_back(resid, gain_pf, mcot)
    mid_part_suf, ffn_gain_suf = norm_back(resid_suf, gain_af, mcot_suf)
    mid = cot_mine.astype(F32) + mid_part
    mid_suf = cot_suf_mine.astype(F32) + mid_part_suf
    mid_block, hiddens = after(pack.join(mid, mid_suf).astype(BF16), hiddens)
    bcot, bcot_suf = pack.tp_gather(mid_block)
    down_pre = outer_chunks(hiddens, [c[0] for c in cot_late]).astype(BF16)
    down_act = outer_chunks(hid_suf, [c[1] for c in cot_late]).astype(BF16)
    pre_blocks, act_blocks = column_blocks(down_pre, shards), column_blocks(down_act, shards)

    def down_half(i):
        act = halves_down(jnp.stack(act_blocks[i::2]), 1)
        return jnp.concatenate([jnp.stack(pre_blocks[i::2]), act], axis=1)

    down_own, down_send = down_half(0), down_half(1)
    bcot, bcot_suf, gate_got, up_send = after(bcot, bcot_suf, gate_got, up_send)
    gate_grad = dp_move(both_sum(gate_own, gate_got))
    up_got = swap(up_send, "expert", 2, 1)
    bcot, outs_got = after(bcot, outs_got)
    outs = pack.third(outs_keep, outs_got)
    outs = [outs[:1]] + [
        swap(outs[d : d + 1].astype(BF16), "dp", dp, d).astype(F32) for d in range(1, dp)
    ]
    acot_pre = project_back(bcot, w_po).astype(BF16)
    acot_suf = project_back(bcot_suf, w_ao).astype(BF16)
    qcot_pre, qcot_suf, kcot, vcot = attend_back(
        info, queries_pre, queries_suf, keys, values, acot_pre, acot_suf, pre_items, suf_len
    )
    got = swap(jnp.where(core == 0, vcot, kcot).astype(BF16), "tp", 4, 1)
    kvcot = jnp.where(core == 0, kcot, vcot) + got.astype(F32)
    kv_pre_cot = kvcot[: pre_items * full_len].reshape(pre_items, 2, half_rows, HD)
    got = swap(kv_pre_cot[:, 1].astype(BF16), "expert", 2, 1)
    kv_pre_cot = kv_pre_cot[:, 0] + got.astype(F32)
    kvcot = jnp.concatenate(
        [kv_pre_cot.reshape(rows, HD), kvcot[pre_items * full_len :]], axis=0
    )
    kvcot, att_pre, att_suf = after(kvcot, att_pre, att_suf)
    got = swap(kvcot.astype(BF16), "tp", 4, 2)
    kvcot = (kvcot + got.astype(F32)).astype(BF16)
    kvcot, gate_grad, up_got, down_send = after(kvcot, gate_grad, up_got, down_send)
    up_grad = dp_move(both_sum(up_own, up_got))
    down_got = swap(down_send, "expert", 2, 1)
    key_half, key_own = kvcot[:rows], kvcot[rows:]
    ncot = project_back(qcot_pre, w_pq) + 0.5 * project_back(key_half, w_pkv)
    ncot_suf = project_back(qcot_suf, w_aq) + 0.5 * project_back(key_own, w_akv)
    ncot, ncot_suf = pack.tp_sum(ncot, ncot_suf)
    in_part, attn_gain = norm_back(x_mine, gain_pa, ncot)
    in_part_suf, attn_gain_suf = norm_back(xs_mine, gain_aa, ncot_suf)
    grad_mine = mid + in_part
    grad_suf_mine = mid_suf + in_part_suf
    embed_w = lax.dot_general(
        own_suffix(chosen).astype(F32),
        grad_suf_mine,
        (((0,), (0,)), ((), ())),
        precision=lax.Precision.HIGHEST,
    )
    tail = jnp.concatenate(
        [
            attn_gain.reshape(shards, -1),
            ffn_gain.reshape(shards, -1),
            attn_gain_suf.reshape(shards, -1),
            ffn_gain_suf.reshape(shards, -1),
            embed_w.reshape(shards, -1),
        ],
        axis=1,
    )

    out_w = jnp.concatenate(
        [
            jnp.stack(column_blocks(outer_sum(att_pre, bcot).astype(BF16), shards)),
            jnp.stack(column_blocks(outer_sum(att_suf, bcot_suf).astype(BF16), shards)),
        ],
        axis=2,
    )
    in_w = jnp.concatenate(
        [
            jnp.concatenate(
                [
                    outer_sum(normed_pre, qcot_pre).astype(BF16).reshape(shards, d_slice, q_cols),
                    outer_sum(normed_pre, key_half).astype(BF16).reshape(shards, d_slice, HD),
                ],
                axis=2,
            ),
            jnp.concatenate(
                [
                    outer_sum(normed_suf, qcot_suf).astype(BF16).reshape(shards, a_slice, q_cols),
                    outer_sum(normed_suf, key_own).astype(BF16).reshape(shards, a_slice, HD),
                ],
                axis=2,
            ),
        ],
        axis=1,
    )

    def scatter_y(value):
        value = value.reshape((dp, 2) + value.shape[1:])
        send = lax.dynamic_index_in_dim(value, 1 - group, 1, keepdims=False)
        keep = lax.dynamic_index_in_dim(value, group, 1, keepdims=False)
        return keep, swap(send, "expert", 2, 1)

    def scatter_z(moved):
        return jnp.sum(dp_move(both_sum(*moved)).astype(F32), axis=0)

    out_w = scatter_y(out_w)
    in_w = scatter_y(in_w)
    in_w, up_grad, down_got = after(in_w, up_grad, down_got)
    down_grad = dp_move(both_sum(down_own, down_got))
    tail = tail + swap(tail, "tp", 4, 1)
    tail = tail + swap(tail, "tp", 4, 2)
    tail_own, tail_got = scatter_y(tail)
    tail_size = tail.shape[1]
    tail_rows = -(-tail_size // (16 * w1)) * 16
    tail = jnp.pad(tail_own + tail_got, ((0, 0), (0, tail_rows * w1 - tail_size)))
    out_w = scatter_z(out_w)
    in_w = both_sum(*in_w)
    in_rows = in_w.shape[1]
    in_w = jnp.concatenate([in_w, tail.reshape(dp, tail_rows, w1).astype(BF16)], axis=1)
    in_w = jnp.sum(dp_move(in_w).astype(F32), axis=0)
    tail = in_w[in_rows:].reshape(-1)[:tail_size]
    in_w = in_w[:in_rows]
    g_po, g_ao = out_w[:, :d_slice], out_w[:, d_slice:]
    g_pq, g_aq = in_w[:d_slice, :q_cols], in_w[d_slice:, :q_cols]
    kv_w = in_w[:, q_cols:].astype(BF16)
    kv_other = swap(kv_w, "tp", 4, 1).astype(F32)
    kv_w = kv_w.astype(F32)
    kv_w = jnp.concatenate(
        [jnp.where(core == 0, kv_w, kv_other), jnp.where(core == 0, kv_other, kv_w)], axis=1
    )
    g_pkv, g_akv = kv_w[:d_slice], kv_w[d_slice:]

    out_pre, out_suf = undo_block(sum(outs))
    out_block = pack.join(resid + out_pre, resid_suf + out_suf).astype(BF16)
    out_pre, out_suf = pack.tp_gather(out_block)
    prefix_out = out_pre.reshape(pre_items, half_rows, width)
    suffix_out = out_suf[None, :suf_len]
    grad_pre, grad_suf = pack.tp_gather(pack.join(grad_mine, grad_suf_mine).astype(BF16))
    prefix_grad = grad_pre.astype(F32).reshape(pre_items, half_rows, width)
    suffix_grad = grad_suf.astype(F32)[None, :suf_len]
    g_pg, g_ag = columns_end(gate_grad)
    g_pu, g_au = columns_end(up_grad)
    g_pd = down_grad[:, :hid].reshape(dp * hid, d_slice).astype(F32)
    g_ad = halves_down(down_grad[:, hid:], 2).reshape(dp * hid_act, a_slice).astype(F32)
    tails, at = [], 0
    for size in (d_slice, d_slice, a_slice, a_slice, action_embed.size):
        tails.append(tail[at : at + size])
        at += size
    g_gpa, g_gpf, g_gaa, g_gaf, g_embed = tails
    g_embed = g_embed.reshape(action_embed.shape)
    return (
        prefix_out,
        suffix_out,
        prefix_grad,
        suffix_grad,
        g_pq,
        g_pkv,
        g_po,
        g_pg,
        g_pu,
        g_pd,
        g_gpa,
        g_gpf,
        g_aq,
        g_akv,
        g_ao,
        g_ag,
        g_au,
        g_ad,
        g_gaa,
        g_gaf,
        g_embed,
    )


def solution(mesh):
    return jax.shard_map(
        functools.partial(local, mesh.shape["dp"]),
        mesh=mesh,
        in_specs=(
            P("dp", "expert", None),
            P(("dp", "expert"), None, None),
            P(("dp", "expert"), None, None),
            P("dp"),
            P(("dp", "expert"), None),
            P(("dp", "expert"), "tp"),
            P(("dp", "expert"), None),
            P("tp", ("dp", "expert")),
            P(("dp", "expert"), "tp"),
            P(("dp", "expert"), "tp"),
            P("tp", ("dp", "expert")),
            P(("dp", "expert")),
            P(("dp", "expert")),
            P(("dp", "expert"), "tp"),
            P(("dp", "expert"), None),
            P("tp", ("dp", "expert")),
            P(("dp", "expert"), "tp"),
            P(("dp", "expert"), "tp"),
            P("tp", ("dp", "expert")),
            P(("dp", "expert")),
            P(("dp", "expert")),
            P(("dp", "expert"), None),
            P("dp", "expert", None),
            P(("dp", "expert"), None, None),
        ),
        out_specs=(
            P("dp", "expert", None),
            P(("dp", "expert"), None, None),
            P("dp", "expert", None),
            P(("dp", "expert"), None, None),
            P(("dp", "expert"), "tp"),
            P(("dp", "expert"), None),
            P("tp", ("dp", "expert")),
            P(("dp", "expert"), "tp"),
            P(("dp", "expert"), "tp"),
            P("tp", ("dp", "expert")),
            P(("dp", "expert")),
            P(("dp", "expert")),
            P(("dp", "expert"), "tp"),
            P(("dp", "expert"), None),
            P("tp", ("dp", "expert")),
            P(("dp", "expert"), "tp"),
            P(("dp", "expert"), "tp"),
            P("tp", ("dp", "expert")),
            P(("dp", "expert")),
            P(("dp", "expert")),
            P(("dp", "expert"), None),
        ),
        check_vma=False,
    )
```

time: 1290 us -> 1180 us (0.915)
  local copies, waits for them, and re-layouts: 201 us -> 144 us
  waiting for transfers between devices: 539 us -> 504 us
  matrix products: 213 us -> 181 us
    all_to_all x8, waiting for transfers between devices: 136 us -> 72.6 us  [dp_move(): return lax.all_to_all(value, 'dp', 0, 0, tiled=True)]
    unnamed x613 -> x550, local copies, waits for them, and re-layouts: 124 us -> 72.4 us
    ppermute x69 -> x72, waiting for transfers between devices: 387 us -> 425 us  [swap(): return lax.ppermute(value, axis, [(i, i ^ mask) for i in range(size)])]
    dot_general x30, matrix products: 81.1 us -> 58.8 us  [project_back(): lax.dot_general(left, right, (((1,), (1,)), ((), ())), preferred_element_...]
    unnamed x73 -> x9, other arithmetic: 16.3 us -> 0.13 us
    all_to_all x8, starting transfers between devices: 71.6 us -> 87.1 us  [dp_move(): return lax.all_to_all(value, 'dp', 0, 0, tiled=True)]
    all_to_all x1 -> x0, waiting for transfers between devices: 15.1 us -> none  [local(): tail = lax.all_to_all(tail, ('dp', 'expert', 'tp'), 0, 0, tiled=True)]
    all_to_all x1 -> x0, starting transfers between devices: 14.3 us -> none  [local(): tail = lax.all_to_all(tail, ('dp', 'expert', 'tp'), 0, 0, tiled=True)]
  transfers between devices with their start and end apart: 79 -> 81, of which waited for: 31 -> 26; matrix products, arithmetic and copies ran while one was open for 40% -> 35% of each run, Pallas kernels for 0% -> 1%
where the time goes in v2:
time: 1180 us; the launch traced here: 1170 us
  waiting for transfers between devices  504 us (43%)
  matrix products  181 us (15%)
  starting transfers between devices  157 us (13%)
  other arithmetic  154 us (13%)
  local copies, waits for them, and re-layouts  144 us (12%)
  between operations  19 us (2%)
    ppermute x72, waiting for transfers between devices, swap(): return lax.ppermute(value, axis, [(i, i ^ mask) for i in range(size)])  425 us
    all_to_all x8, starting transfers between devices, dp_move(): return lax.all_to_all(value, 'dp', 0, 0, tiled=True)  87.1 us
    all_to_all x8, waiting for transfers between devices, dp_move(): return lax.all_to_all(value, 'dp', 0, 0, tiled=True)  72.6 us
    unnamed x550, local copies, waits for them, and re-layouts  72.4 us
    ppermute x72, starting transfers between devices, swap(): return lax.ppermute(value, axis, [(i, i ^ mask) for i in range(size)])  69.5 us
    dot_general x28, matrix products, project(): return jnp.dot(left, right, preferred_element_type=F32)  64.9 us
    dot_general x30, matrix products, project_back(): lax.dot_general(left, right, (((1,), (1,)), ((), ())), preferred_element_...  58.8 us
    dot_general x12, matrix products, outer_sum(): lax.dot_general(left, right, (((0,), (0,)), ((), ())), preferred_element_...  57.2 us
  transfers between devices with their start and end apart: 81, of which 26 were waited for; matrix products, arithmetic and copies ran while one was open for 35% of the time, Pallas kernels for 1%

profile of v2, /device:TPU:0, one launch (start us, length us, event | category | flops | bytes accessed | tf_op | source)
XLA Modules:
  0.0 1167.5 jit_solution(17362347194908030856)
XLA Ops:
  12.6 6.5 all-to-all-start
  35.0 36.6 %collective-permute-done = bf16[400,768]{1,0:T(8,128)(2,1)} collective-permute-done((bf16[400,768]{1,0:T(8,128)(2,1)}, bf16[400,768]{1,0:T(8,128)(2,1)}, u32[]{:S(2)}, u32[]{:S(2)}) %collective-permute-start) | collective-permute-done | bytes 614432 | tf_op jit(solution)/shard_map/ppermute | solution.py:171
  71.6 41.9 %collective-permute-done.1 = bf16[400,768]{1,0:T(8,128)(2,1)} collective-permute-done((bf16[400,768]{1,0:T(8,128)(2,1)}, bf16[400,768]{1,0:T(8,128)(2,1)}, u32[]{:S(2)}, u32[]{:S(2)}) %collective-permute-start.1) | collective-permute-done | bytes 614432 | tf_op jit(solution)/shard_map/ppermute | solution.py:171
  118.8 12.0 %collective-permute-done.4 = bf16[400,768]{1,0:T(8,128)(2,1)} collective-permute-done((bf16[400,768]{1,0:T(8,128)(2,1)}, bf16[400,768]{1,0:T(8,128)(2,1)}, u32[]{:S(2)}, u32[]{:S(2)}) %collective-permute-start.4) | collective-permute-done | bytes 614432 | tf_op jit(solution)/shard_map/ppermute | solution.py:171
  130.7 17.4 %collective-permute-done.5 = bf16[400,768]{1,0:T(8,128)(2,1)} collective-permute-done((bf16[400,768]{1,0:T(8,128)(2,1)}, bf16[400,768]{1,0:T(8,128)(2,1)}, u32[]{:S(2)}, u32[]{:S(2)}) %collective-permute-start.5) | collective-permute-done | bytes 614432 | tf_op jit(solution)/shard_map/ppermute | solution.py:171
  148.1 10.1 collective-permute-done.6
  192.5 6.4 all-gather.3.cloned.1.call-done
  219.0 17.6 %all-to-all-start.1 = ((bf16[4,256,1152]{2,1,0:T(8,128)(2,1)}), bf16[4,256,1152]{2,1,0:T(8,128)(2,1)}, u32[]{:S(2)}, u32[]{:S(2)}) async-start(bf16[4,256,1152]{2,1,0:T(8,128)(2,1)} %maximum_maximum_fusion.2), calls=%async_computation.1 | async-start | bytes 4718592 | tf_op jit(solution)/shard_map/all_to_all | solution.py:327
  248.0 11.4 collective-permute-start.11
  263.8 31.4 %collective-permute-done.11 = bf16[1,160,2048]{2,1,0:T(8,128)(2,1)} collective-permute-done((bf16[1,160,2048]{2,1,0:T(8,128)(2,1)}, bf16[1,160,2048]{2,1,0:T(8,128)(2,1)}, u32[]{:S(2)}, u32[]{:S(2)}) %collective-permute-start.11) | collective-permute-done | bytes 655392 | tf_op jit(solution)/shard_map/ppermute | solution.py:171
  295.7 38.0 %collective-permute-done.12 = bf16[1,160,2048]{2,1,0:T(8,128)(2,1)} collective-permute-done((bf16[1,160,2048]{2,1,0:T(8,128)(2,1)}, bf16[1,160,2048]{2,1,0:T(8,128)(2,1)}, u32[]{:S(2)}, u32[]{:S(2)}) %collective-permute-start.12) | collective-permute-done | bytes 655392 | tf_op jit(solution)/shard_map/ppermute | solution.py:171
  353.8 16.9 %all-to-all-start.2 = ((bf16[4,1152,256]{2,1,0:T(8,128)(2,1)}), bf16[4,1152,256]{2,1,0:T(8,128)(2,1)}, u32[]{:S(2)}, u32[]{:S(2)}) async-start(bf16[4,1152,256]{2,1,0:T(8,128)(2,1)} %maximum_maximum_fusion.3), calls=%async_computation.2 | async-start | bytes 4718592 | tf_op jit(solution)/shard_map/all_to_all | solution.py:327
  406.3 19.3 %collective-permute-done.23 = bf16[4,256,1152]{2,1,0:T(8,128)(2,1)S(1)} collective-permute-done((bf16[4,256,1152]{2,1,0:T(8,128)(2,1)}, bf16[4,256,1152]{2,1,0:T(8,128)(2,1)S(1)}, u32[]{:S(2)}, u32[]{:S(2)}) %collective-permute-start.23) | collective-permute-done | bytes 2359328 | tf_op jit(solution)/shard_map/ppermute | solution.py:171
  430.5 4.4 fusion.321
  438.1 4.5 fusion.319
  443.5 4.5 fusion.320
  464.9 20.5 %collective-permute-done.33 = bf16[1,160,2048]{2,1,0:T(8,128)(2,1)S(1)} collective-permute-done((bf16[1,160,2048]{2,1,0:T(8,128)(2,1)}, bf16[1,160,2048]{2,1,0:T(8,128)(2,1)S(1)}, u32[]{:S(2)}, u32[]{:S(2)}) %collective-permute-start.33) | collective-permute-done | bytes 655392 | tf_op jit(solution)/shard_map/ppermute | solution.py:171
  486.9 15.7 %collective-permute-done.30 = bf16[1,160,2048]{2,1,0:T(8,128)(2,1)S(1)} collective-permute-done((bf16[1,160,2048]{2,1,0:T(8,128)(2,1)}, bf16[1,160,2048]{2,1,0:T(8,128)(2,1)S(1)}, u32[]{:S(2)}, u32[]{:S(2)}) %collective-permute-start.30) | collective-permute-done | bytes 655392 | tf_op jit(solution)/shard_map/ppermute | solution.py:171
  506.0 14.3 %collective-permute-done.31 = bf16[1,160,2048]{2,1,0:T(8,128)(2,1)S(1)} collective-permute-done((bf16[1,160,2048]{2,1,0:T(8,128)(2,1)S(1)}, bf16[1,160,2048]{2,1,0:T(8,128)(2,1)S(1)}, u32[]{:S(2)}, u32[]{:S(2)}) %collective-permute-start.31) | collective-permute-done | bytes 655392 | tf_op jit(solution)/shard_map/ppermute | solution.py:171
  520.5 9.5 collective-permute-done.28
  541.0 6.3 multiply_convert_fusion.10
  553.3 5.1 multiply_convert_fusion.5
  571.1 5.9 multiply_convert_fusion.3
  587.2 5.0 multiply_convert_fusion.1
  597.5 4.8 add_convert_fusion.4
  614.5 5.0 convolution_convert_fusion.4
  619.5 5.1 convolution_convert_fusion.3
  624.6 5.1 convolution_convert_fusion.2
  629.8 5.0 convolution_convert_fusion.1
  636.8 7.3 fusion.24
  661.6 15.5 %fusion.63 = bf16[2048,1024]{1,0:T(8,128)(2,1)} fusion(bf16[576,1024]{1,0:T(8,128)(2,1)} %copy-done.240, bf16[576,1024]{1,0:T(8,128)(2,1)} %copy-done.239, bf16[576,1024]{1,0:T(8,128)(2,1)} %copy-done.238, bf16[576,1024]{1,0:T(8,128)(2,1)} %get-tuple-element.390, bf16[576,2048]{1,0:T(8,128)(2,1)} %bitcast.831, bf16[576,2048]{1,0:T(8,128)(2,1)} %bitcast.827, ...), kind=kOutput, calls=%fused_computation.89 | convolution fusion | flops 9722396672 | bytes 18350080 | tf_op jit(solution)/shard_map/dot_general | solution.py:38
  685.7 18.7 %collective-permute-done.45 = bf16[1,160,2048]{2,1,0:T(8,128)(2,1)} collective-permute-done((bf16[1,160,2048]{2,1,0:T(8,128)(2,1)}, bf16[1,160,2048]{2,1,0:T(8,128)(2,1)}, u32[]{:S(2)}, u32[]{:S(2)}) %collective-permute-start.45) | collective-permute-done | bytes 655392 | tf_op jit(solution)/shard_map/ppermute | solution.py:171
  711.9 6.5 convert_add_fusion
  725.2 15.4 %fusion.58 = bf16[2048,1024]{1,0:T(8,128)(2,1)} fusion(bf16[576,1024]{1,0:T(8,128)(2,1)} %copy-done.236, bf16[576,1024]{1,0:T(8,128)(2,1)} %copy-done.235, bf16[576,1024]{1,0:T(8,128)(2,1)} %copy-done.234, bf16[576,1024]{1,0:T(8,128)(2,1)} %get-tuple-element.391, bf16[576,2048]{1,0:T(8,128)(2,1)} %bitcast.832, bf16[576,2048]{1,0:T(8,128)(2,1)} %bitcast.828, ...), kind=kOutput, calls=%fused_computation.88 | convolution fusion | flops 9722396672 | bytes 18350080 | tf_op jit(solution)/shard_map/dot_general | solution.py:38
  740.6 15.3 %fusion.53 = bf16[1024,2048]{1,0:T(8,128)(2,1)} fusion(bf16[576,2048]{1,0:T(8,128)(2,1)} %bitcast.840, bf16[576,2048]{1,0:T(8,128)(2,1)} %bitcast.838, bf16[576,2048]{1,0:T(8,128)(2,1)} %bitcast.836, bf16[576,2048]{1,0:T(8,128)(2,1)} %bitcast.834, bf16[576,1024]{1,0:T(8,128)(2,1)S(1)} %copy-done.102, bf16[576,1024]{1,0:T(8,128)(2,1)} %get-tuple-element.446, ...), kind=kOutput, calls=%fused_computation.87 | convolution fusion | flops 9722396672 | bytes 18350080 | tf_op jit(solution)/shard_map/dot_general | solution.py:38
  776.5 16.2 %all-to-all-start.3 = ((bf16[4,256,1152]{2,1,0:T(8,128)(2,1)}), bf16[4,256,1152]{2,1,0:T(8,128)(2,1)}, u32[]{:S(2)}, u32[]{:S(2)}) async-start(bf16[4,256,1152]{2,1,0:T(8,128)(2,1)} %fusion.48), calls=%async_computation.3 | async-start | bytes 4718592 | tf_op jit(solution)/shard_map/all_to_all | solution.py:327
  797.4 6.5 attend_back.1
  819.1 33.6 %collective-permute-done.58 = bf16[2,288,256]{2,1,0:T(8,128)(2,1)S(1)} collective-permute-done((bf16[2,288,256]{2,1,0:T(8,128)(2,1)S(1)}, bf16[2,288,256]{2,1,0:T(8,128)(2,1)S(1)}, u32[]{:S(2)}, u32[]{:S(2)}) %collective-permute-start.58) | collective-permute-done | bytes 294944 | tf_op jit(solution)/shard_map/ppermute | solution.py:171
  858.4 31.6 %collective-permute-done.53 = bf16[1,160,2048]{2,1,0:T(8,128)(2,1)S(1)} collective-permute-done((bf16[1,160,2048]{2,1,0:T(8,128)(2,1)S(1)}, bf16[1,160,2048]{2,1,0:T(8,128)(2,1)S(1)}, u32[]{:S(2)}, u32[]{:S(2)}) %collective-permute-start.53) | collective-permute-done | bytes 655392 | tf_op jit(solution)/shard_map/ppermute | solution.py:171
  892.4 7.6 collective-permute-done.59
  901.6 15.9 %all-to-all-start.6 = ((bf16[4,512,384]{2,1,0:T(8,128)(2,1)}), bf16[4,512,384]{2,1,0:T(8,128)(2,1)}, u32[]{:S(2)}, u32[]{:S(2)}) async-start(bf16[4,512,384]{2,1,0:T(8,128)(2,1)} %fusion.68), calls=%async_computation.6 | async-start | bytes 3145728 | tf_op jit(solution)/shard_map/all_to_all | solution.py:327
  941.1 10.2 collective-permute-done.62
  956.7 5.3 all-to-all-start.4
  977.6 26.7 %collective-permute-done.68 = f32[8,4864]{1,0:T(8,128)S(1)} collective-permute-done((f32[8,4864]{1,0:T(8,128)S(1)}, f32[8,4864]{1,0:T(8,128)S(1)}, u32[]{:S(2)}, u32[]{:S(2)}) %collective-permute-start.68) | collective-permute-done | bytes 155680 | tf_op jit(solution)/shard_map/ppermute | solution.py:171
  1007.8 25.1 %collective-permute-done.66 = bf16[4,1152,256]{2,1,0:T(8,128)(2,1)} collective-permute-done((bf16[4,1152,256]{2,1,0:T(8,128)(2,1)}, bf16[4,1152,256]{2,1,0:T(8,128)(2,1)}, u32[]{:S(2)}, u32[]{:S(2)}) %collective-permute-start.66) | collective-permute-done | bytes 2359328 | tf_op jit(solution)/shard_map/ppermute | solution.py:171
  1036.5 5.1 all-to-all-start.7
  1060.7 32.6 %all-to-all-done.7 = bf16[4,1152,256]{2,1,0:T(8,128)(2,1)S(1)} async-done(((bf16[4,1152,256]{2,1,0:T(8,128)(2,1)}), bf16[4,1152,256]{2,1,0:T(8,128)(2,1)S(1)}, u32[]{:S(2)}, u32[]{:S(2)}) %all-to-all-start.7) | async-done | bytes 2359328 | tf_op jit(solution)/shard_map/all_to_all | solution.py:327
  1113.8 40.0 %all-to-all-done.5 = bf16[4,400,768]{2,1,0:T(8,128)(2,1)S(1)} async-done(((bf16[4,400,768]{2,1,0:T(8,128)(2,1)}), bf16[4,400,768]{2,1,0:T(8,128)(2,1)S(1)}, u32[]{:S(2)}, u32[]{:S(2)}) %all-to-all-start.5) | async-done | bytes 2457632 | tf_op jit(solution)/shard_map/all_to_all | solution.py:327
  (1031 shorter events, 427.1 us)
Async XLA Ops:
  12.6 100.9 %all-to-all-start = ((bf16[4,256,1152]{2,1,0:T(8,128)(2,1)}), bf16[4,256,1152]{2,1,0:T(8,128)(2,1)S(1)}, u32[]{:S(2)}, u32[]{:S(2)}) async-start(bf16[4,256,1152]{2,1,0:T(8,128)(2,1)} %maximum_maximum_fusion.1), calls=%async_computation | async-start | bytes 4718592 | tf_op jit(solution)/shard_map/all_to_all | solution.py:327
  19.1 179.8 %all-gather.3.cloned.1.call-start = ((), (), s32[]{:S(2)}) async-start(), calls=%async_computation.8 | async-start | bytes 3538944 | tf_op jit(solution)/shard_map/all_gather | solution.py:363
  22.3 49.4 %collective-permute-start = (bf16[400,768]{1,0:T(8,128)(2,1)}, bf16[400,768]{1,0:T(8,128)(2,1)}, u32[]{:S(2)}, u32[]{:S(2)}) collective-permute-start(bf16[400,768]{1,0:T(8,128)(2,1)} %pad_maximum_fusion.29), channel_id=1, source_target_pairs={{0,8},{8,0},{16,24},{24,16},{1,9},{9,1},{17,25},{25,17},{2,10},{10... | collective-permute-start | bytes 1843208 | tf_op jit(solution)/shard_map/ppermute | solution.py:171
  24.3 89.3 %collective-permute-start.1 = (bf16[400,768]{1,0:T(8,128)(2,1)}, bf16[400,768]{1,0:T(8,128)(2,1)}, u32[]{:S(2)}, u32[]{:S(2)}) collective-permute-start(bf16[400,768]{1,0:T(8,128)(2,1)} %pad_maximum_fusion.29), channel_id=1, source_target_pairs={{0,16},{8,24},{16,0},{24,8},{1,17},{9,25},{17,1},{25,9},{2,18},{10... | collective-permute-start | bytes 1843208 | tf_op jit(solution)/shard_map/ppermute | solution.py:171
  26.6 86.9 %collective-permute-start.2 = (bf16[400,768]{1,0:T(8,128)(2,1)}, bf16[400,768]{1,0:T(8,128)(2,1)}, u32[]{:S(2)}, u32[]{:S(2)}) collective-permute-start(bf16[400,768]{1,0:T(8,128)(2,1)} %pad_maximum_fusion.29), channel_id=1, source_target_pairs={{0,24},{8,16},{16,8},{24,0},{1,25},{9,17},{17,9},{25,1},{2,26},{10... | collective-permute-start | bytes 1843208 | tf_op jit(solution)/shard_map/ppermute | solution.py:171
  26.6 92.1 %collective-permute-start.3 = (bf16[400,768]{1,0:T(8,128)(2,1)}, bf16[400,768]{1,0:T(8,128)(2,1)}, u32[]{:S(2)}, u32[]{:S(2)}) collective-permute-start(bf16[400,768]{1,0:T(8,128)(2,1)} %pad_maximum_fusion.29), channel_id=1, source_target_pairs={{0,1},{1,0},{2,3},{3,2},{4,5},{5,4},{6,7},{7,6},{8,9},{9,8},{10,11... | collective-permute-start | bytes 1843208 | tf_op jit(solution)/shard_map/ppermute | solution.py:171
  115.7 42.6 %collective-permute-start.6 = (bf16[400,768]{1,0:T(8,128)(2,1)}, bf16[400,768]{1,0:T(8,128)(2,1)}, u32[]{:S(2)}, u32[]{:S(2)}) collective-permute-start(bf16[400,768]{1,0:T(8,128)(2,1)} %collective-permute-done.2), channel_id=1, source_target_pairs={{0,1},{1,0},{2,3},{3,2},{4,5},{5,4},{6,7},{7,6},{8,9},{9,8},{10,11... | collective-permute-start | bytes 1843208 | tf_op jit(solution)/shard_map/ppermute | solution.py:171
  219.0 120.8 %all-to-all-start.1 = ((bf16[4,256,1152]{2,1,0:T(8,128)(2,1)}), bf16[4,256,1152]{2,1,0:T(8,128)(2,1)}, u32[]{:S(2)}, u32[]{:S(2)}) async-start(bf16[4,256,1152]{2,1,0:T(8,128)(2,1)} %maximum_maximum_fusion.2), calls=%async_computation.1 | async-start | bytes 4718592 | tf_op jit(solution)/shard_map/all_to_all | solution.py:327
  240.4 99.3 %collective-permute-start.17 = (bf16[4,256,1152]{2,1,0:T(8,128)(2,1)S(1)}, bf16[4,256,1152]{2,1,0:T(8,128)(2,1)}, u32[]{:S(2)}, u32[]{:S(2)}) collective-permute-start(bf16[4,256,1152]{2,1,0:T(8,128)(2,1)S(1)} %copy-done.15), channel_id=1, source_target_pairs={{0,1},{1,0},{2,3},{3,2},{4,5},{5,4},{6,7},{7,6},{8,9},{9,8},{10,11... | collective-permute-start | bytes 7077896 | tf_op jit(solution)/shard_map/ppermute | solution.py:171
  247.4 92.3 %collective-permute-start.16 = (bf16[1,160,2048]{2,1,0:T(8,128)(2,1)}, bf16[1,160,2048]{2,1,0:T(8,128)(2,1)}, u32[]{:S(2)}, u32[]{:S(2)}) collective-permute-start(bf16[1,160,2048]{2,1,0:T(8,128)(2,1)} %pad_maximum_fusion.22), channel_id=1, source_target_pairs={{0,4},{2,6},{4,0},{6,2},{1,5},{3,7},{5,1},{7,3},{8,12},{10,14},{12... | collective-permute-start | bytes 1966088 | tf_op jit(solution)/shard_map/ppermute | solution.py:171
  248.0 47.2 %collective-permute-start.11 = (bf16[1,160,2048]{2,1,0:T(8,128)(2,1)}, bf16[1,160,2048]{2,1,0:T(8,128)(2,1)}, u32[]{:S(2)}, u32[]{:S(2)}) collective-permute-start(bf16[1,160,2048]{2,1,0:T(8,128)(2,1)} %pad_maximum_fusion.22), channel_id=1, source_target_pairs={{0,8},{8,0},{16,24},{24,16},{1,9},{9,1},{17,25},{25,17},{2,10},{10... | collective-permute-start | bytes 1966088 | tf_op jit(solution)/shard_map/ppermute | solution.py:171
  259.4 74.4 %collective-permute-start.12 = (bf16[1,160,2048]{2,1,0:T(8,128)(2,1)}, bf16[1,160,2048]{2,1,0:T(8,128)(2,1)}, u32[]{:S(2)}, u32[]{:S(2)}) collective-permute-start(bf16[1,160,2048]{2,1,0:T(8,128)(2,1)} %pad_maximum_fusion.22), channel_id=1, source_target_pairs={{0,16},{8,24},{16,0},{24,8},{1,17},{9,25},{17,1},{25,9},{2,18},{10... | collective-permute-start | bytes 1966088 | tf_op jit(solution)/shard_map/ppermute | solution.py:171
  259.4 74.4 %collective-permute-start.13 = (bf16[1,160,2048]{2,1,0:T(8,128)(2,1)}, bf16[1,160,2048]{2,1,0:T(8,128)(2,1)}, u32[]{:S(2)}, u32[]{:S(2)}) collective-permute-start(bf16[1,160,2048]{2,1,0:T(8,128)(2,1)} %pad_maximum_fusion.22), channel_id=1, source_target_pairs={{0,24},{8,16},{16,8},{24,0},{1,25},{9,17},{17,9},{25,1},{2,26},{10... | collective-permute-start | bytes 1966088 | tf_op jit(solution)/shard_map/ppermute | solution.py:171
  295.2 139.7 %collective-permute-start.24 = (bf16[1,160,2048]{2,1,0:T(8,128)(2,1)}, bf16[1,160,2048]{2,1,0:T(8,128)(2,1)}, u32[]{:S(2)}, u32[]{:S(2)}) collective-permute-start(bf16[1,160,2048]{2,1,0:T(8,128)(2,1)} %pad_maximum_fusion.23), channel_id=1, source_target_pairs={{0,4},{2,6},{4,0},{6,2},{1,5},{3,7},{5,1},{7,3},{8,12},{10,14},{12... | collective-permute-start | bytes 1966088 | tf_op jit(solution)/shard_map/ppermute | solution.py:171
  333.8 38.2 %collective-permute-start.14 = (bf16[1,160,2048]{2,1,0:T(8,128)(2,1)}, bf16[1,160,2048]{2,1,0:T(8,128)(2,1)}, u32[]{:S(2)}, u32[]{:S(2)}) collective-permute-start(bf16[1,160,2048]{2,1,0:T(8,128)(2,1)} %collective-permute-done.11), channel_id=1, source_target_pairs={{0,4},{2,6},{4,0},{6,2},{1,5},{3,7},{5,1},{7,3},{8,12},{10,14},{12... | collective-permute-start | bytes 1966088 | tf_op jit(solution)/shard_map/ppermute | solution.py:171
  334.3 40.7 %collective-permute-start.21 = (bf16[1,160,2048]{2,1,0:T(8,128)(2,1)}, bf16[1,160,2048]{2,1,0:T(8,128)(2,1)}, u32[]{:S(2)}, u32[]{:S(2)}) collective-permute-start(bf16[1,160,2048]{2,1,0:T(8,128)(2,1)} %collective-permute-done.12), channel_id=1, source_target_pairs={{0,4},{2,6},{4,0},{6,2},{1,5},{3,7},{5,1},{7,3},{8,12},{10,14},{12... | collective-permute-start | bytes 1966088 | tf_op jit(solution)/shard_map/ppermute | solution.py:171
  353.8 100.1 %all-to-all-start.2 = ((bf16[4,1152,256]{2,1,0:T(8,128)(2,1)}), bf16[4,1152,256]{2,1,0:T(8,128)(2,1)}, u32[]{:S(2)}, u32[]{:S(2)}) async-start(bf16[4,1152,256]{2,1,0:T(8,128)(2,1)} %maximum_maximum_fusion.3), calls=%async_computation.2 | async-start | bytes 4718592 | tf_op jit(solution)/shard_map/all_to_all | solution.py:327
  372.0 53.7 %collective-permute-start.23 = (bf16[4,256,1152]{2,1,0:T(8,128)(2,1)}, bf16[4,256,1152]{2,1,0:T(8,128)(2,1)S(1)}, u32[]{:S(2)}, u32[]{:S(2)}) collective-permute-start(bf16[4,256,1152]{2,1,0:T(8,128)(2,1)} %all-to-all-done.1), channel_id=1, source_target_pairs={{0,1},{1,0},{2,3},{3,2},{4,5},{5,4},{6,7},{7,6},{8,9},{9,8},{10,11... | collective-permute-start | bytes 7077896 | tf_op jit(solution)/shard_map/ppermute | solution.py:171
  455.8 46.8 %collective-permute-start.30 = (bf16[1,160,2048]{2,1,0:T(8,128)(2,1)}, bf16[1,160,2048]{2,1,0:T(8,128)(2,1)S(1)}, u32[]{:S(2)}, u32[]{:S(2)}) collective-permute-start(bf16[1,160,2048]{2,1,0:T(8,128)(2,1)} %pad_maximum_fusion.23), channel_id=1, source_target_pairs={{0,16},{8,24},{16,0},{24,8},{1,17},{9,25},{17,1},{25,9},{2,18},{10... | collective-permute-start | bytes 1966088 | tf_op jit(solution)/shard_map/ppermute | solution.py:171
  458.1 46.1 %collective-permute-start.27 = (bf16[1,160,2048]{2,1,0:T(8,128)(2,1)}, bf16[1,160,2048]{2,1,0:T(8,128)(2,1)S(1)}, u32[]{:S(2)}, u32[]{:S(2)}) collective-permute-start(bf16[1,160,2048]{2,1,0:T(8,128)(2,1)} %pad_maximum_fusion.23), channel_id=1, source_target_pairs={{0,24},{8,16},{16,8},{24,0},{1,25},{9,17},{17,9},{25,1},{2,26},{10... | collective-permute-start | bytes 1966088 | tf_op jit(solution)/shard_map/ppermute | solution.py:171
  460.5 69.8 %collective-permute-start.26 = (bf16[4,1152,256]{2,1,0:T(8,128)(2,1)}, bf16[4,1152,256]{2,1,0:T(8,128)(2,1)S(1)}, u32[]{:S(2)}, u32[]{:S(2)}) collective-permute-start(bf16[4,1152,256]{2,1,0:T(8,128)(2,1)} %all-to-all-done.2), channel_id=1, source_target_pairs={{0,1},{1,0},{2,3},{3,2},{4,5},{5,4},{6,7},{7,6},{8,9},{9,8},{10,11... | collective-permute-start | bytes 7077896 | tf_op jit(solution)/shard_map/ppermute | solution.py:171
  506.0 41.4 %collective-permute-start.35 = (bf16[2,160,2048]{2,1,0:T(8,128)(2,1)}, bf16[2,160,2048]{2,1,0:T(8,128)(2,1)}, u32[]{:S(2)}, u32[]{:S(2)}) collective-permute-start(bf16[2,160,2048]{2,1,0:T(8,128)(2,1)} %pad_maximum_fusion.18), channel_id=1, source_target_pairs={{0,2},{2,0},{4,6},{6,4},{1,3},{3,1},{5,7},{7,5},{8,10},{10,8},{12,... | collective-permute-start | bytes 3932168 | tf_op jit(solution)/shard_map/ppermute | solution.py:171
  530.1 36.6 %collective-permute-start.29 = (bf16[2,160,2048]{2,1,0:T(8,128)(2,1)S(1)}, bf16[2,160,2048]{2,1,0:T(8,128)(2,1)}, u32[]{:S(2)}, u32[]{:S(2)}) collective-permute-start(bf16[2,160,2048]{2,1,0:T(8,128)(2,1)S(1)} %pad_maximum_fusion.16), channel_id=1, source_target_pairs={{0,2},{2,0},{4,6},{6,4},{1,3},{3,1},{5,7},{7,5},{8,10},{10,8},{12,... | collective-permute-start | bytes 3932168 | tf_op jit(solution)/shard_map/ppermute | solution.py:171
  604.3 48.5 %collective-permute-start.42 = (bf16[1,160,2048]{2,1,0:T(8,128)(2,1)S(1)}, bf16[1,160,2048]{2,1,0:T(8,128)(2,1)S(1)}, u32[]{:S(2)}, u32[]{:S(2)}) collective-permute-start(bf16[1,160,2048]{2,1,0:T(8,128)(2,1)S(1)} %fusion.140), channel_id=1, source_target_pairs={{0,4},{2,6},{4,0},{6,2},{1,5},{3,7},{5,1},{7,3},{8,12},{10,14},{12... | collective-permute-start | bytes 1966088 | tf_op jit(solution)/shard_map/ppermute | solution.py:171
  613.4 39.4 %collective-permute-start.41 = (bf16[1,2,160,2048]{3,2,1,0:T(8,128)(2,1)S(1)}, bf16[1,2,160,2048]{3,2,1,0:T(8,128)(2,1)S(1)}, u32[]{:S(2)}, u32[]{:S(2)}) collective-permute-start(bf16[1,2,160,2048]{3,2,1,0:T(8,128)(2,1)S(1)} %get-tuple-element.508), channel_id=1, source_target_pairs={{0,2},{2,0},{4,6},{6,4},{1,3},{3,1},{5,7},{7,5},{8,10},{10,8},{12,... | collective-permute-start | bytes 3932168 | tf_op jit(solution)/shard_map/ppermute | solution.py:171
  646.9 38.8 %collective-permute-start.40 = (bf16[4,2,160,2048]{3,2,0,1:T(8,128)(2,1)}, bf16[4,2,160,2048]{3,2,0,1:T(8,128)(2,1)}, u32[]{:S(2)}, u32[]{:S(2)}) collective-permute-start(bf16[4,2,160,2048]{3,2,0,1:T(8,128)(2,1)} %copy.75), channel_id=1, source_target_pairs={{0,2},{2,0},{4,6},{6,4},{1,3},{3,1},{5,7},{7,5},{8,10},{10,8},{12,... | collective-permute-start | bytes 15728648 | tf_op jit(solution)/shard_map/ppermute | solution.py:171
  648.1 37.6 %collective-permute-start.44 = (bf16[1,160,2048]{2,1,0:T(8,128)(2,1)}, bf16[1,160,2048]{2,1,0:T(8,128)(2,1)}, u32[]{:S(2)}, u32[]{:S(2)}) collective-permute-start(bf16[1,160,2048]{2,1,0:T(8,128)(2,1)} %add_convert_fusion.9), channel_id=1, source_target_pairs={{0,8},{8,0},{16,24},{24,16},{1,9},{9,1},{17,25},{25,17},{2,10},{10... | collective-permute-start | bytes 1966088 | tf_op jit(solution)/shard_map/ppermute | solution.py:171
  657.2 47.2 %collective-permute-start.45 = (bf16[1,160,2048]{2,1,0:T(8,128)(2,1)}, bf16[1,160,2048]{2,1,0:T(8,128)(2,1)}, u32[]{:S(2)}, u32[]{:S(2)}) collective-permute-start(bf16[1,160,2048]{2,1,0:T(8,128)(2,1)} %add_convert_fusion.8), channel_id=1, source_target_pairs={{0,16},{8,24},{16,0},{24,8},{1,17},{9,25},{17,1},{25,9},{2,18},{10... | collective-permute-start | bytes 1966088 | tf_op jit(solution)/shard_map/ppermute | solution.py:171
  685.3 86.0 %collective-permute-start.50 = (bf16[4,256,1152]{2,1,0:T(8,128)(2,1)}, bf16[4,256,1152]{2,1,0:T(8,128)(2,1)}, u32[]{:S(2)}, u32[]{:S(2)}) collective-permute-start(bf16[4,256,1152]{2,1,0:T(8,128)(2,1)} %fusion.97), channel_id=1, source_target_pairs={{0,1},{1,0},{2,3},{3,2},{4,5},{5,4},{6,7},{7,6},{8,9},{9,8},{10,11... | collective-permute-start | bytes 7077896 | tf_op jit(solution)/shard_map/ppermute | solution.py:171
  710.8 45.6 %collective-permute-start.48 = (bf16[1,160,2048]{2,1,0:T(8,128)(2,1)S(1)}, bf16[1,160,2048]{2,1,0:T(8,128)(2,1)}, u32[]{:S(2)}, u32[]{:S(2)}) collective-permute-start(bf16[1,160,2048]{2,1,0:T(8,128)(2,1)S(1)} %pad_maximum_fusion.24), channel_id=1, source_target_pairs={{0,4},{2,6},{4,0},{6,2},{1,5},{3,7},{5,1},{7,3},{8,12},{10,14},{12... | collective-permute-start | bytes 1966088 | tf_op jit(solution)/shard_map/ppermute | solution.py:171
  724.2 69.4 %collective-permute-start.51 = (bf16[4,160,2048]{2,1,0:T(8,128)(2,1)}, bf16[4,160,2048]{2,1,0:T(8,128)(2,1)}, u32[]{:S(2)}, u32[]{:S(2)}) collective-permute-start(bf16[4,160,2048]{2,1,0:T(8,128)(2,1)} %fusion.69), channel_id=1, source_target_pairs={{0,4},{2,6},{4,0},{6,2},{1,5},{3,7},{5,1},{7,3},{8,12},{10,14},{12... | collective-permute-start | bytes 7864328 | tf_op jit(solution)/shard_map/ppermute | solution.py:171
  776.5 125.1 %all-to-all-start.3 = ((bf16[4,256,1152]{2,1,0:T(8,128)(2,1)}), bf16[4,256,1152]{2,1,0:T(8,128)(2,1)}, u32[]{:S(2)}, u32[]{:S(2)}) async-start(bf16[4,256,1152]{2,1,0:T(8,128)(2,1)} %fusion.48), calls=%async_computation.3 | async-start | bytes 4718592 | tf_op jit(solution)/shard_map/all_to_all | solution.py:327
  792.7 124.8 %collective-permute-start.60 = (bf16[4,256,1152]{2,1,0:T(8,128)(2,1)}, bf16[4,256,1152]{2,1,0:T(8,128)(2,1)}, u32[]{:S(2)}, u32[]{:S(2)}) collective-permute-start(bf16[4,256,1152]{2,1,0:T(8,128)(2,1)} %fusion.95), channel_id=1, source_target_pairs={{0,1},{1,0},{2,3},{3,2},{4,5},{5,4},{6,7},{7,6},{8,9},{9,8},{10,11... | collective-permute-start | bytes 7077896 | tf_op jit(solution)/shard_map/ppermute | solution.py:171
  808.8 49.6 %collective-permute-start.52 = (bf16[1,160,2048]{2,1,0:T(8,128)(2,1)S(1)}, bf16[1,160,2048]{2,1,0:T(8,128)(2,1)S(1)}, u32[]{:S(2)}, u32[]{:S(2)}) collective-permute-start(bf16[1,160,2048]{2,1,0:T(8,128)(2,1)S(1)} %get-tuple-element.503), channel_id=1, source_target_pairs={{0,8},{8,0},{16,24},{24,16},{1,9},{9,1},{17,25},{25,17},{2,10},{10... | collective-permute-start | bytes 1966088 | tf_op jit(solution)/shard_map/ppermute | solution.py:171
  811.3 78.7 %collective-permute-start.53 = (bf16[1,160,2048]{2,1,0:T(8,128)(2,1)S(1)}, bf16[1,160,2048]{2,1,0:T(8,128)(2,1)S(1)}, u32[]{:S(2)}, u32[]{:S(2)}) collective-permute-start(bf16[1,160,2048]{2,1,0:T(8,128)(2,1)S(1)} %get-tuple-element.505), channel_id=1, source_target_pairs={{0,16},{8,24},{16,0},{24,8},{1,17},{9,25},{17,1},{25,9},{2,18},{10... | collective-permute-start | bytes 1966088 | tf_op jit(solution)/shard_map/ppermute | solution.py:171
  813.2 76.8 %collective-permute-start.54 = (bf16[1,160,2048]{2,1,0:T(8,128)(2,1)S(1)}, bf16[1,160,2048]{2,1,0:T(8,128)(2,1)S(1)}, u32[]{:S(2)}, u32[]{:S(2)}) collective-permute-start(bf16[1,160,2048]{2,1,0:T(8,128)(2,1)S(1)} %get-tuple-element.504), channel_id=1, source_target_pairs={{0,24},{8,16},{16,8},{24,0},{1,25},{9,17},{17,9},{25,1},{2,26},{10... | collective-permute-start | bytes 1966088 | tf_op jit(solution)/shard_map/ppermute | solution.py:171
  814.2 38.5 %collective-permute-start.58 = (bf16[2,288,256]{2,1,0:T(8,128)(2,1)S(1)}, bf16[2,288,256]{2,1,0:T(8,128)(2,1)S(1)}, u32[]{:S(2)}, u32[]{:S(2)}) collective-permute-start(bf16[2,288,256]{2,1,0:T(8,128)(2,1)S(1)} %fusion.186), channel_id=1, source_target_pairs={{0,1},{1,0},{2,3},{3,2},{4,5},{5,4},{6,7},{7,6},{8,9},{9,8},{10,11... | collective-permute-start | bytes 884744 | tf_op jit(solution)/shard_map/ppermute | solution.py:171
  857.2 42.8 %collective-permute-start.71 = (bf16[4,512,384]{2,1,0:T(8,128)(2,1)S(1)}, bf16[4,512,384]{2,1,0:T(8,128)(2,1)S(1)}, u32[]{:S(2)}, u32[]{:S(2)}) collective-permute-start(bf16[4,512,384]{2,1,0:T(8,128)(2,1)S(1)} %dynamic-slice_bitcast_fusion.2), channel_id=1, source_target_pairs={{0,1},{1,0},{2,3},{3,2},{4,5},{5,4},{6,7},{7,6},{8,9},{9,8},{10,11... | collective-permute-start | bytes 4718600 | tf_op jit(solution)/shard_map/ppermute | solution.py:171
  901.6 55.1 %all-to-all-start.6 = ((bf16[4,512,384]{2,1,0:T(8,128)(2,1)}), bf16[4,512,384]{2,1,0:T(8,128)(2,1)}, u32[]{:S(2)}, u32[]{:S(2)}) async-start(bf16[4,512,384]{2,1,0:T(8,128)(2,1)} %fusion.68), calls=%async_computation.6 | async-start | bytes 3145728 | tf_op jit(solution)/shard_map/all_to_all | solution.py:327
  928.5 79.3 %collective-permute-start.65 = (bf16[4,384,768]{2,1,0:T(8,128)(2,1)}, bf16[4,384,768]{2,1,0:T(8,128)(2,1)}, u32[]{:S(2)}, u32[]{:S(2)}) collective-permute-start(bf16[4,384,768]{2,1,0:T(8,128)(2,1)} %get-tuple-element.487), channel_id=1, source_target_pairs={{0,1},{1,0},{2,3},{3,2},{4,5},{5,4},{6,7},{7,6},{8,9},{9,8},{10,11... | collective-permute-start | bytes 7077896 | tf_op jit(solution)/shard_map/ppermute | solution.py:171
  928.8 104.1 %collective-permute-start.66 = (bf16[4,1152,256]{2,1,0:T(8,128)(2,1)}, bf16[4,1152,256]{2,1,0:T(8,128)(2,1)}, u32[]{:S(2)}, u32[]{:S(2)}) collective-permute-start(bf16[4,1152,256]{2,1,0:T(8,128)(2,1)} %maximum_maximum_fusion.4), channel_id=1, source_target_pairs={{0,1},{1,0},{2,3},{3,2},{4,5},{5,4},{6,7},{7,6},{8,9},{9,8},{10,11... | collective-permute-start | bytes 7077896 | tf_op jit(solution)/shard_map/ppermute | solution.py:171
  956.7 76.1 %all-to-all-start.4 = ((bf16[4,256,1152]{2,1,0:T(8,128)(2,1)}), bf16[4,256,1152]{2,1,0:T(8,128)(2,1)}, u32[]{:S(2)}, u32[]{:S(2)}) async-start(bf16[4,256,1152]{2,1,0:T(8,128)(2,1)} %fusion.47), calls=%async_computation.4 | async-start | bytes 4718592 | tf_op jit(solution)/shard_map/all_to_all | solution.py:327
  969.6 73.0 %collective-permute-start.55 = (bf16[1,160,2048]{2,1,0:T(8,128)(2,1)}, bf16[1,160,2048]{2,1,0:T(8,128)(2,1)}, u32[]{:S(2)}, u32[]{:S(2)}) collective-permute-start(bf16[1,160,2048]{2,1,0:T(8,128)(2,1)} %pad_maximum_fusion.25), channel_id=1, source_target_pairs={{0,4},{2,6},{4,0},{6,2},{1,5},{3,7},{5,1},{7,3},{8,12},{10,14},{12... | collective-permute-start | bytes 1966088 | tf_op jit(solution)/shard_map/ppermute | solution.py:171
  971.3 74.1 %collective-permute-start.63 = (bf16[1,160,2048]{2,1,0:T(8,128)(2,1)}, bf16[1,160,2048]{2,1,0:T(8,128)(2,1)}, u32[]{:S(2)}, u32[]{:S(2)}) collective-permute-start(bf16[1,160,2048]{2,1,0:T(8,128)(2,1)} %pad_maximum_fusion.27), channel_id=1, source_target_pairs={{0,4},{2,6},{4,0},{6,2},{1,5},{3,7},{5,1},{7,3},{8,12},{10,14},{12... | collective-permute-start | bytes 1966088 | tf_op jit(solution)/shard_map/ppermute | solution.py:171
  1036.5 56.8 %all-to-all-start.7 = ((bf16[4,1152,256]{2,1,0:T(8,128)(2,1)}), bf16[4,1152,256]{2,1,0:T(8,128)(2,1)S(1)}, u32[]{:S(2)}, u32[]{:S(2)}) async-start(bf16[4,1152,256]{2,1,0:T(8,128)(2,1)} %add_convert_fusion), calls=%async_computation.7 | async-start | bytes 4718592 | tf_op jit(solution)/shard_map/all_to_all | solution.py:327
  1045.4 53.0 %collective-permute-start.56 = (bf16[2,160,2048]{2,1,0:T(8,128)(2,1)}, bf16[2,160,2048]{2,1,0:T(8,128)(2,1)}, u32[]{:S(2)}, u32[]{:S(2)}) collective-permute-start(bf16[2,160,2048]{2,1,0:T(8,128)(2,1)} %pad_maximum_fusion.20), channel_id=1, source_target_pairs={{0,2},{2,0},{4,6},{6,4},{1,3},{3,1},{5,7},{7,5},{8,10},{10,8},{12,... | collective-permute-start | bytes 3932168 | tf_op jit(solution)/shard_map/ppermute | solution.py:171
  1048.3 50.1 %collective-permute-start.64 = (bf16[2,160,2048]{2,1,0:T(8,128)(2,1)}, bf16[2,160,2048]{2,1,0:T(8,128)(2,1)}, u32[]{:S(2)}, u32[]{:S(2)}) collective-permute-start(bf16[2,160,2048]{2,1,0:T(8,128)(2,1)} %pad_maximum_fusion.21), channel_id=1, source_target_pairs={{0,2},{2,0},{4,6},{6,4},{1,3},{3,1},{5,7},{7,5},{8,10},{10,8},{12,... | collective-permute-start | bytes 3932168 | tf_op jit(solution)/shard_map/ppermute | solution.py:171
  1094.7 59.0 %all-to-all-start.5 = ((bf16[4,400,768]{2,1,0:T(8,128)(2,1)}), bf16[4,400,768]{2,1,0:T(8,128)(2,1)S(1)}, u32[]{:S(2)}, u32[]{:S(2)}) async-start(bf16[4,400,768]{2,1,0:T(8,128)(2,1)} %pad_maximum_fusion.8), calls=%async_computation.5 | async-start | bytes 4915200 | tf_op jit(solution)/shard_map/all_to_all | solution.py:327
  (275 other events, 3668.8 us)
Sparse Core Ops, SparseCore 0:
  117.4 81.3 all-gather.2

commit v3 on v2

--- a/solution.py
+++ b/solution.py
@@ -358,10 +358,9 @@
     cot_block = own_block(cot_mine, cot_suf_mine)
 
     gate_own = dp_move(gate_out)
-    *in_z, gate_own, packed_out = after(*in_z, gate_own, packed_out)
+    full_out = lax.all_gather(packed_out, both, axis=0)
+    *in_z, gate_own, up_out = after(*in_z, gate_own, up_out)
     in_far += [swap(block, "expert", 2, 1) for block in in_z[1:]]
-    full_out = lax.all_gather(packed_out, both, axis=0)
-    *in_far, up_out = after(*in_far, up_out)
     up_own = dp_move(up_out)
     full_in = jnp.zeros((dp, 2) + packed_in.shape, BF16)
     for d in range(dp):
@@ -395,9 +394,10 @@
     kv_suf = project(normed_suf, w_akv).astype(BF16)
     queries_pre = project(normed_pre, w_pq).astype(BF16)
     queries_suf = project(normed_suf, w_aq).astype(BF16)
-    queries_pre, queries_suf, kv_suf, kv_got, gate_own = after(
-        queries_pre, queries_suf, kv_suf, kv_got, gate_own
-    )
+    queries_pre, queries_suf, kv_suf, kv_got, gate_own, up_own, down_out = after(
+        queries_pre, queries_suf, kv_suf, kv_got, gate_own, up_own, down_out
+    )
+    down_own = dp_move(down_out)
     gate_got = swap(gate_own, "expert", 2, 1)
     kv_pre = jnp.concatenate([kv_pre, kv_got], axis=1)
     full_len = kv_pre.shape[1]
@@ -426,8 +426,7 @@
     normed_z = [normed_block] + [swap(normed_block, "dp", dp, d) for d in range(1, dp)]
     normed_far, up_own, gate_got = after(normed_far, up_own, gate_got)
     up_got = swap(up_own, "expert", 2, 1)
-    *normed_z, down_out = after(*normed_z, down_out)
-    down_own = dp_move(down_out)
+    normed_z[-1], down_own = after(normed_z[-1], down_own)
     w_pg, w_ag = columns_in((gate_own, gate_got), pre_gate, act_gate)
     normed_chunks, gates, inner_terms = [], [], []
 
@@ -446,7 +445,10 @@
             pre, suf, *gates[-1] = after(pre, suf, *gates[-1])
         normed_chunks.append((pre, suf))
         gates.append((gelu_terms(project(pre, w_pg)), gelu_terms(project(suf, w_ag))))
-    gates[-1], up_got = after(gates[-1], up_got)
+    gates[0], cot_block = after(gates[0], cot_block)
+    cot_z = [swap(cot_block, "dp", dp, d) for d in range(1, dp)]
+    gates[-1], up_got, down_own = after(gates[-1], up_got, down_own)
+    down_got = swap(down_own, "expert", 2, 1)
     w_pu, w_au = columns_in((up_own, up_got), pre_up, act_up)
     for d in range(dp):
         pre, suf = normed_chunks[d]
@@ -456,9 +458,6 @@
     cot_far = swap(cot_block, "tp", 4, 2)
     inner_terms[0], cot_far = after(inner_terms[0], cot_far)
     cot_chunks = [pack.spread(cot_block, cot_far)]
-    inner_terms[0], cot_block, down_own = after(inner_terms[0], cot_block, down_own)
-    down_got = swap(down_own, "expert", 2, 1)
-    cot_z = [swap(cot_block, "dp", dp, d) for d in range(1, dp)]
     cot_chunks += [pack.spread(z, swap(z, "tp", 4, 2)) for z in cot_z]
     down = jnp.stack([down_own, down_got], axis=1).reshape(shards, hid + hid_act // 2, d_slice)
     w_pd = jnp.concatenate([down[i, :hid] for i in range(shards)], axis=1)

time: 1180 us -> 1140 us (0.966)
  starting transfers between devices: 157 us -> 132 us
  local copies, waits for them, and re-layouts: 144 us -> 125 us
    all_to_all x8, starting transfers between devices: 87.1 us -> 70.9 us  [dp_move(): return lax.all_to_all(value, 'dp', 0, 0, tiled=True)]
    all_to_all x8, waiting for transfers between devices: 72.6 us -> 87.7 us  [dp_move(): return lax.all_to_all(value, 'dp', 0, 0, tiled=True)]
    ppermute x72, waiting for transfers between devices: 425 us -> 412 us  [swap(): return lax.ppermute(value, axis, [(i, i ^ mask) for i in range(size)])]
    unnamed x550 -> x516, local copies, waits for them, and re-layouts: 72.4 us -> 60.6 us
  transfers between devices with their start and end apart: 81 -> 81, of which waited for: 26 -> 28; matrix products, arithmetic and copies ran while one was open for 35% -> 34% of each run, Pallas kernels for 1% -> 1%
where the time goes in v3:
time: 1140 us; the launch traced here: 1130 us
  waiting for transfers between devices  500 us (44%)
  matrix products  190 us (17%)
  other arithmetic  152 us (13%)
  starting transfers between devices  132 us (12%)
  local copies, waits for them, and re-layouts  125 us (11%)
  between operations  19.2 us (2%)
    ppermute x72, waiting for transfers between devices, swap(): return lax.ppermute(value, axis, [(i, i ^ mask) for i in range(size)])  412 us
    all_to_all x8, waiting for transfers between devices, dp_move(): return lax.all_to_all(value, 'dp', 0, 0, tiled=True)  87.7 us
    all_to_all x8, starting transfers between devices, dp_move(): return lax.all_to_all(value, 'dp', 0, 0, tiled=True)  70.9 us
    dot_general x28, matrix products, project(): return jnp.dot(left, right, preferred_element_type=F32)  69.7 us
    dot_general x30, matrix products, project_back(): lax.dot_general(left, right, (((1,), (1,)), ((), ())), preferred_element_...  62.3 us
    ppermute x72, starting transfers between devices, swap(): return lax.ppermute(value, axis, [(i, i ^ mask) for i in range(size)])  61.5 us
    unnamed x516, local copies, waits for them, and re-layouts  60.6 us
    dot_general x12, matrix products, outer_sum(): lax.dot_general(left, right, (((0,), (0,)), ((), ())), preferred_element_...  57.6 us
  transfers between devices with their start and end apart: 81, of which 28 were waited for; matrix products, arithmetic and copies ran while one was open for 34% of the time, Pallas kernels for 1%

profile of v3, /device:TPU:0, one launch (start us, length us, event | category | flops | bytes accessed | tf_op | source)
XLA Modules:
  0.0 1127.2 jit_solution(9082923222088035723)
XLA Ops:
  12.6 6.5 all-to-all-start
  40.3 44.0 %collective-permute-done = bf16[400,768]{1,0:T(8,128)(2,1)} collective-permute-done((bf16[400,768]{1,0:T(8,128)(2,1)}, bf16[400,768]{1,0:T(8,128)(2,1)}, u32[]{:S(2)}, u32[]{:S(2)}) %collective-permute-start) | collective-permute-done | bytes 614432 | tf_op jit(solution)/shard_map/ppermute | solution.py:171
  84.3 67.3 %collective-permute-done.1 = bf16[400,768]{1,0:T(8,128)(2,1)} collective-permute-done((bf16[400,768]{1,0:T(8,128)(2,1)}, bf16[400,768]{1,0:T(8,128)(2,1)}, u32[]{:S(2)}, u32[]{:S(2)}) %collective-permute-start.1) | collective-permute-done | bytes 614432 | tf_op jit(solution)/shard_map/ppermute | solution.py:171
  155.1 14.1 %all-to-all-start.1 = ((bf16[4,256,1152]{2,1,0:T(8,128)(2,1)}), bf16[4,256,1152]{2,1,0:T(8,128)(2,1)}, u32[]{:S(2)}, u32[]{:S(2)}) async-start(bf16[4,256,1152]{2,1,0:T(8,128)(2,1)} %maximum_maximum_fusion.2), calls=%async_computation.1 | async-start | bytes 4718592 | tf_op jit(solution)/shard_map/all_to_all | solution.py:327
  175.2 6.6 collective-permute-done.5
  184.1 6.4 collective-permute-done.6
  206.9 15.1 %all-to-all-done.1 = bf16[4,256,1152]{2,1,0:T(8,128)(2,1)} async-done(((bf16[4,256,1152]{2,1,0:T(8,128)(2,1)}), bf16[4,256,1152]{2,1,0:T(8,128)(2,1)}, u32[]{:S(2)}, u32[]{:S(2)}) %all-to-all-start.1) | async-done | bytes 2359328 | tf_op jit(solution)/shard_map/all_to_all | solution.py:327
  252.7 4.8 all-to-all-start.2
  257.5 8.2 collective-permute-done.10
  279.6 25.7 %collective-permute-done.15 = bf16[4,256,1152]{2,1,0:T(8,128)(2,1)} collective-permute-done((bf16[4,256,1152]{2,1,0:T(8,128)(2,1)S(1)}, bf16[4,256,1152]{2,1,0:T(8,128)(2,1)}, u32[]{:S(2)}, u32[]{:S(2)}) %collective-permute-start.15) | collective-permute-done | bytes 2359328 | tf_op jit(solution)/shard_map/ppermute | solution.py:171
  307.1 6.2 collective-permute-done.11
  313.8 40.8 %collective-permute-done.20 = bf16[1,160,2048]{2,1,0:T(8,128)(2,1)} collective-permute-done((bf16[1,160,2048]{2,1,0:T(8,128)(2,1)S(1)}, bf16[1,160,2048]{2,1,0:T(8,128)(2,1)}, u32[]{:S(2)}, u32[]{:S(2)}) %collective-permute-start.20) | collective-permute-done | bytes 655392 | tf_op jit(solution)/shard_map/ppermute | solution.py:171
  376.5 7.0 collective-permute-done.18
  389.5 5.4 fusion.75
  399.3 5.4 fusion.81
  405.0 5.9 fusion.87
  426.1 5.5 fusion.319
  432.0 6.0 fusion.320
  452.6 13.7 %collective-permute-done.34 = bf16[1,160,2048]{2,1,0:T(8,128)(2,1)S(1)} collective-permute-done((bf16[1,160,2048]{2,1,0:T(8,128)(2,1)S(1)}, bf16[1,160,2048]{2,1,0:T(8,128)(2,1)S(1)}, u32[]{:S(2)}, u32[]{:S(2)}) %collective-permute-start.34) | collective-permute-done | bytes 655392 | tf_op jit(solution)/shard_map/ppermute | solution.py:171
  466.5 13.8 %collective-permute-done.31 = bf16[1,160,2048]{2,1,0:T(8,128)(2,1)S(1)} collective-permute-done((bf16[1,160,2048]{2,1,0:T(8,128)(2,1)S(1)}, bf16[1,160,2048]{2,1,0:T(8,128)(2,1)S(1)}, u32[]{:S(2)}, u32[]{:S(2)}) %collective-permute-start.31) | collective-permute-done | bytes 655392 | tf_op jit(solution)/shard_map/ppermute | solution.py:171
  480.5 13.4 %collective-permute-done.28 = bf16[1,160,2048]{2,1,0:T(8,128)(2,1)S(1)} collective-permute-done((bf16[1,160,2048]{2,1,0:T(8,128)(2,1)S(1)}, bf16[1,160,2048]{2,1,0:T(8,128)(2,1)S(1)}, u32[]{:S(2)}, u32[]{:S(2)}) %collective-permute-start.28) | collective-permute-done | bytes 655392 | tf_op jit(solution)/shard_map/ppermute | solution.py:171
  508.6 5.8 multiply_convert_fusion.5
  527.4 7.4 multiply_convert_fusion.3
  534.9 6.5 multiply_convert_fusion.10
  551.8 6.0 multiply_convert_fusion.1
  577.4 5.0 convolution_convert_fusion.4
  582.4 5.1 convolution_convert_fusion.3
  587.6 5.1 convolution_convert_fusion.2
  592.7 5.0 convolution_convert_fusion.1
  599.8 6.9 fusion.24
  619.7 15.6 %fusion.63 = bf16[2048,1024]{1,0:T(8,128)(2,1)} fusion(bf16[576,1024]{1,0:T(8,128)(2,1)} %get-tuple-element.350, bf16[576,1024]{1,0:T(8,128)(2,1)} %get-tuple-element.337, bf16[576,1024]{1,0:T(8,128)(2,1)} %copy-done.220, bf16[576,1024]{1,0:T(8,128)(2,1)} %get-tuple-element.374, bf16[576,2048]{1,0:T(8,128)(2,1)} %bitcast.828, ...), kind=kOutput, calls=%fused_computation.89 | convolution fusion | flops 9722396672 | bytes 18350080 | tf_op jit(solution)/shard_map/dot_general | solution.py:38
  646.9 17.0 %collective-permute-done.45 = bf16[1,160,2048]{2,1,0:T(8,128)(2,1)} collective-permute-done((bf16[1,160,2048]{2,1,0:T(8,128)(2,1)}, bf16[1,160,2048]{2,1,0:T(8,128)(2,1)}, u32[]{:S(2)}, u32[]{:S(2)}) %collective-permute-start.45) | collective-permute-done | bytes 655392 | tf_op jit(solution)/shard_map/ppermute | solution.py:171
  671.3 6.5 convert_add_fusion
  684.8 15.8 %fusion.58 = bf16[2048,1024]{1,0:T(8,128)(2,1)} fusion(bf16[576,1024]{1,0:T(8,128)(2,1)} %copy-done.219, bf16[576,1024]{1,0:T(8,128)(2,1)} %get-tuple-element.338, bf16[576,1024]{1,0:T(8,128)(2,1)} %copy-done.216, bf16[576,1024]{1,0:T(8,128)(2,1)} %get-tuple-element.375, bf16[576,2048]{1,0:T(8,128)(2,1)} %bitcast.829, bf16[576,2048]{1,0:T(8,128)(2,1)} %bitcast.825, ...), kind=kOutput, calls=%fused_computation.88 | convolution fusion | flops 9722396672 | bytes 18350080 | tf_op jit(solution)/shard_map/dot_general | solution.py:38
  700.6 15.2 %fusion.53 = bf16[1024,2048]{1,0:T(8,128)(2,1)} fusion(bf16[576,2048]{1,0:T(8,128)(2,1)} %bitcast.837, bf16[576,2048]{1,0:T(8,128)(2,1)} %bitcast.835, bf16[576,2048]{1,0:T(8,128)(2,1)} %bitcast.833, bf16[576,2048]{1,0:T(8,128)(2,1)} %bitcast.831, bf16[576,1024]{1,0:T(8,128)(2,1)S(1)} %copy-done.97, bf16[576,1024]{1,0:T(8,128)(2,1)} %get-tuple-element.430, ...), kind=kOutput, calls=%fused_computation.87 | convolution fusion | flops 9722396672 | bytes 18350080 | tf_op jit(solution)/shard_map/dot_general | solution.py:38
  736.4 14.9 %all-to-all-start.3 = ((bf16[4,256,1152]{2,1,0:T(8,128)(2,1)}), bf16[4,256,1152]{2,1,0:T(8,128)(2,1)}, u32[]{:S(2)}, u32[]{:S(2)}) async-start(bf16[4,256,1152]{2,1,0:T(8,128)(2,1)} %fusion.48), calls=%async_computation.3 | async-start | bytes 4718592 | tf_op jit(solution)/shard_map/all_to_all | solution.py:327
  756.2 6.5 attend_back.1
  778.6 32.7 %collective-permute-done.58 = bf16[2,288,256]{2,1,0:T(8,128)(2,1)S(1)} collective-permute-done((bf16[2,288,256]{2,1,0:T(8,128)(2,1)S(1)}, bf16[2,288,256]{2,1,0:T(8,128)(2,1)S(1)}, u32[]{:S(2)}, u32[]{:S(2)}) %collective-permute-start.58) | collective-permute-done | bytes 294944 | tf_op jit(solution)/shard_map/ppermute | solution.py:171
  817.0 31.7 %collective-permute-done.53 = bf16[1,160,2048]{2,1,0:T(8,128)(2,1)S(1)} collective-permute-done((bf16[1,160,2048]{2,1,0:T(8,128)(2,1)S(1)}, bf16[1,160,2048]{2,1,0:T(8,128)(2,1)S(1)}, u32[]{:S(2)}, u32[]{:S(2)}) %collective-permute-start.53) | collective-permute-done | bytes 655392 | tf_op jit(solution)/shard_map/ppermute | solution.py:171
  850.9 7.9 collective-permute-done.59
  860.5 16.5 %all-to-all-start.6 = ((bf16[4,512,384]{2,1,0:T(8,128)(2,1)}), bf16[4,512,384]{2,1,0:T(8,128)(2,1)}, u32[]{:S(2)}, u32[]{:S(2)}) async-start(bf16[4,512,384]{2,1,0:T(8,128)(2,1)} %fusion.68), calls=%async_computation.6 | async-start | bytes 3145728 | tf_op jit(solution)/shard_map/all_to_all | solution.py:327
  900.6 10.2 collective-permute-done.62
  916.2 5.4 all-to-all-start.4
  937.3 26.8 %collective-permute-done.68 = f32[8,4864]{1,0:T(8,128)S(1)} collective-permute-done((f32[8,4864]{1,0:T(8,128)S(1)}, f32[8,4864]{1,0:T(8,128)S(1)}, u32[]{:S(2)}, u32[]{:S(2)}) %collective-permute-start.68) | collective-permute-done | bytes 155680 | tf_op jit(solution)/shard_map/ppermute | solution.py:171
  967.7 24.6 %collective-permute-done.66 = bf16[4,1152,256]{2,1,0:T(8,128)(2,1)} collective-permute-done((bf16[4,1152,256]{2,1,0:T(8,128)(2,1)}, bf16[4,1152,256]{2,1,0:T(8,128)(2,1)}, u32[]{:S(2)}, u32[]{:S(2)}) %collective-permute-start.66) | collective-permute-done | bytes 2359328 | tf_op jit(solution)/shard_map/ppermute | solution.py:171
  996.0 5.1 all-to-all-start.7
  1020.2 32.6 %all-to-all-done.7 = bf16[4,1152,256]{2,1,0:T(8,128)(2,1)S(1)} async-done(((bf16[4,1152,256]{2,1,0:T(8,128)(2,1)}), bf16[4,1152,256]{2,1,0:T(8,128)(2,1)S(1)}, u32[]{:S(2)}, u32[]{:S(2)}) %all-to-all-start.7) | async-done | bytes 2359328 | tf_op jit(solution)/shard_map/all_to_all | solution.py:327
  1073.3 40.0 %all-to-all-done.5 = bf16[4,400,768]{2,1,0:T(8,128)(2,1)S(1)} async-done(((bf16[4,400,768]{2,1,0:T(8,128)(2,1)}), bf16[4,400,768]{2,1,0:T(8,128)(2,1)S(1)}, u32[]{:S(2)}, u32[]{:S(2)}) %all-to-all-start.5) | async-done | bytes 2457632 | tf_op jit(solution)/shard_map/all_to_all | solution.py:327
  (997 shorter events, 408.4 us)
Async XLA Ops:
  12.6 138.9 %all-to-all-start = ((bf16[4,256,1152]{2,1,0:T(8,128)(2,1)}), bf16[4,256,1152]{2,1,0:T(8,128)(2,1)S(1)}, u32[]{:S(2)}, u32[]{:S(2)}) async-start(bf16[4,256,1152]{2,1,0:T(8,128)(2,1)} %maximum_maximum_fusion.1), calls=%async_computation | async-start | bytes 4718592 | tf_op jit(solution)/shard_map/all_to_all | solution.py:327
  19.1 210.8 %all-gather.3.cloned.1.call-start = ((), (), s32[]{:S(2)}) async-start(), calls=%async_computation.8 | async-start | bytes 3538944 | tf_op jit(solution)/shard_map/all_gather | solution.py:361
  22.1 62.2 %collective-permute-start = (bf16[400,768]{1,0:T(8,128)(2,1)}, bf16[400,768]{1,0:T(8,128)(2,1)}, u32[]{:S(2)}, u32[]{:S(2)}) collective-permute-start(bf16[400,768]{1,0:T(8,128)(2,1)} %pad_maximum_fusion.29), channel_id=1, source_target_pairs={{0,8},{8,0},{16,24},{24,16},{1,9},{9,1},{17,25},{25,17},{2,10},{10... | collective-permute-start | bytes 1843208 | tf_op jit(solution)/shard_map/ppermute | solution.py:171
  24.1 127.4 %collective-permute-start.1 = (bf16[400,768]{1,0:T(8,128)(2,1)}, bf16[400,768]{1,0:T(8,128)(2,1)}, u32[]{:S(2)}, u32[]{:S(2)}) collective-permute-start(bf16[400,768]{1,0:T(8,128)(2,1)} %pad_maximum_fusion.29), channel_id=1, source_target_pairs={{0,16},{8,24},{16,0},{24,8},{1,17},{9,25},{17,1},{25,9},{2,18},{10... | collective-permute-start | bytes 1843208 | tf_op jit(solution)/shard_map/ppermute | solution.py:171
  26.5 125.0 %collective-permute-start.2 = (bf16[400,768]{1,0:T(8,128)(2,1)}, bf16[400,768]{1,0:T(8,128)(2,1)}, u32[]{:S(2)}, u32[]{:S(2)}) collective-permute-start(bf16[400,768]{1,0:T(8,128)(2,1)} %pad_maximum_fusion.29), channel_id=1, source_target_pairs={{0,24},{8,16},{16,8},{24,0},{1,25},{9,17},{17,9},{25,1},{2,26},{10... | collective-permute-start | bytes 1843208 | tf_op jit(solution)/shard_map/ppermute | solution.py:171
  26.5 144.2 %collective-permute-start.3 = (bf16[400,768]{1,0:T(8,128)(2,1)}, bf16[400,768]{1,0:T(8,128)(2,1)}, u32[]{:S(2)}, u32[]{:S(2)}) collective-permute-start(bf16[400,768]{1,0:T(8,128)(2,1)} %pad_maximum_fusion.29), channel_id=1, source_target_pairs={{0,1},{1,0},{2,3},{3,2},{4,5},{5,4},{6,7},{7,6},{8,9},{9,8},{10,11... | collective-permute-start | bytes 1843208 | tf_op jit(solution)/shard_map/ppermute | solution.py:171
  153.6 36.9 %collective-permute-start.6 = (bf16[400,768]{1,0:T(8,128)(2,1)}, bf16[400,768]{1,0:T(8,128)(2,1)}, u32[]{:S(2)}, u32[]{:S(2)}) collective-permute-start(bf16[400,768]{1,0:T(8,128)(2,1)} %collective-permute-done.2), channel_id=1, source_target_pairs={{0,1},{1,0},{2,3},{3,2},{4,5},{5,4},{6,7},{7,6},{8,9},{9,8},{10,11... | collective-permute-start | bytes 1843208 | tf_op jit(solution)/shard_map/ppermute | solution.py:171
  155.1 66.8 %all-to-all-start.1 = ((bf16[4,256,1152]{2,1,0:T(8,128)(2,1)}), bf16[4,256,1152]{2,1,0:T(8,128)(2,1)}, u32[]{:S(2)}, u32[]{:S(2)}) async-start(bf16[4,256,1152]{2,1,0:T(8,128)(2,1)} %maximum_maximum_fusion.2), calls=%async_computation.1 | async-start | bytes 4718592 | tf_op jit(solution)/shard_map/all_to_all | solution.py:327
  252.2 53.1 %collective-permute-start.15 = (bf16[4,256,1152]{2,1,0:T(8,128)(2,1)S(1)}, bf16[4,256,1152]{2,1,0:T(8,128)(2,1)}, u32[]{:S(2)}, u32[]{:S(2)}) collective-permute-start(bf16[4,256,1152]{2,1,0:T(8,128)(2,1)S(1)} %copy-done.15), channel_id=1, source_target_pairs={{0,1},{1,0},{2,3},{3,2},{4,5},{5,4},{6,7},{7,6},{8,9},{9,8},{10,11... | collective-permute-start | bytes 7077896 | tf_op jit(solution)/shard_map/ppermute | solution.py:171
  252.7 111.8 %all-to-all-start.2 = ((bf16[4,1152,256]{2,1,0:T(8,128)(2,1)}), bf16[4,1152,256]{2,1,0:T(8,128)(2,1)}, u32[]{:S(2)}, u32[]{:S(2)}) async-start(bf16[4,1152,256]{2,1,0:T(8,128)(2,1)} %maximum_maximum_fusion.3), calls=%async_computation.2 | async-start | bytes 4718592 | tf_op jit(solution)/shard_map/all_to_all | solution.py:327
  273.3 40.0 %collective-permute-start.11 = (bf16[1,160,2048]{2,1,0:T(8,128)(2,1)S(1)}, bf16[1,160,2048]{2,1,0:T(8,128)(2,1)}, u32[]{:S(2)}, u32[]{:S(2)}) collective-permute-start(bf16[1,160,2048]{2,1,0:T(8,128)(2,1)S(1)} %pad_maximum_fusion.22), channel_id=1, source_target_pairs={{0,8},{8,0},{16,24},{24,16},{1,9},{9,1},{17,25},{25,17},{2,10},{10... | collective-permute-start | bytes 1966088 | tf_op jit(solution)/shard_map/ppermute | solution.py:171
  273.3 81.3 %collective-permute-start.20 = (bf16[1,160,2048]{2,1,0:T(8,128)(2,1)S(1)}, bf16[1,160,2048]{2,1,0:T(8,128)(2,1)}, u32[]{:S(2)}, u32[]{:S(2)}) collective-permute-start(bf16[1,160,2048]{2,1,0:T(8,128)(2,1)S(1)} %pad_maximum_fusion.22), channel_id=1, source_target_pairs={{0,16},{8,24},{16,0},{24,8},{1,17},{9,25},{17,1},{25,9},{2,18},{10... | collective-permute-start | bytes 1966088 | tf_op jit(solution)/shard_map/ppermute | solution.py:171
  276.6 87.9 %collective-permute-start.17 = (bf16[1,160,2048]{2,1,0:T(8,128)(2,1)S(1)}, bf16[1,160,2048]{2,1,0:T(8,128)(2,1)}, u32[]{:S(2)}, u32[]{:S(2)}) collective-permute-start(bf16[1,160,2048]{2,1,0:T(8,128)(2,1)S(1)} %pad_maximum_fusion.22), channel_id=1, source_target_pairs={{0,24},{8,16},{16,8},{24,0},{1,25},{9,17},{17,9},{25,1},{2,26},{10... | collective-permute-start | bytes 1966088 | tf_op jit(solution)/shard_map/ppermute | solution.py:171
  306.6 78.3 %collective-permute-start.16 = (bf16[2,160,2048]{2,1,0:T(8,128)(2,1)}, bf16[2,160,2048]{2,1,0:T(8,128)(2,1)}, u32[]{:S(2)}, u32[]{:S(2)}) collective-permute-start(bf16[2,160,2048]{2,1,0:T(8,128)(2,1)} %pad_maximum_fusion.12), channel_id=1, source_target_pairs={{0,2},{2,0},{4,6},{6,4},{1,3},{3,1},{5,7},{7,5},{8,10},{10,8},{12,... | collective-permute-start | bytes 3932168 | tf_op jit(solution)/shard_map/ppermute | solution.py:171
  306.6 111.8 %collective-permute-start.23 = (bf16[4,256,1152]{2,1,0:T(8,128)(2,1)}, bf16[4,256,1152]{2,1,0:T(8,128)(2,1)}, u32[]{:S(2)}, u32[]{:S(2)}) collective-permute-start(bf16[4,256,1152]{2,1,0:T(8,128)(2,1)} %all-to-all-done.1), channel_id=1, source_target_pairs={{0,1},{1,0},{2,3},{3,2},{4,5},{5,4},{6,7},{7,6},{8,9},{9,8},{10,11... | collective-permute-start | bytes 7077896 | tf_op jit(solution)/shard_map/ppermute | solution.py:171
  313.3 54.0 %collective-permute-start.12 = (bf16[1,160,2048]{2,1,0:T(8,128)(2,1)}, bf16[1,160,2048]{2,1,0:T(8,128)(2,1)}, u32[]{:S(2)}, u32[]{:S(2)}) collective-permute-start(bf16[1,160,2048]{2,1,0:T(8,128)(2,1)} %collective-permute-done.11), channel_id=1, source_target_pairs={{0,4},{2,6},{4,0},{6,2},{1,5},{3,7},{5,1},{7,3},{8,12},{10,14},{12... | collective-permute-start | bytes 1966088 | tf_op jit(solution)/shard_map/ppermute | solution.py:171
  396.9 51.6 %collective-permute-start.24 = (bf16[1,160,2048]{2,1,0:T(8,128)(2,1)S(1)}, bf16[1,160,2048]{2,1,0:T(8,128)(2,1)S(1)}, u32[]{:S(2)}, u32[]{:S(2)}) collective-permute-start(bf16[1,160,2048]{2,1,0:T(8,128)(2,1)S(1)} %copy-done.38), channel_id=1, source_target_pairs={{0,4},{2,6},{4,0},{6,2},{1,5},{3,7},{5,1},{7,3},{8,12},{10,14},{12... | collective-permute-start | bytes 1966088 | tf_op jit(solution)/shard_map/ppermute | solution.py:171
  397.4 51.2 %collective-permute-start.33 = (bf16[1,160,2048]{2,1,0:T(8,128)(2,1)S(1)}, bf16[1,160,2048]{2,1,0:T(8,128)(2,1)S(1)}, u32[]{:S(2)}, u32[]{:S(2)}) collective-permute-start(bf16[1,160,2048]{2,1,0:T(8,128)(2,1)S(1)} %copy-done.38), channel_id=1, source_target_pairs={{0,8},{8,0},{16,24},{24,16},{1,9},{9,1},{17,25},{25,17},{2,10},{10... | collective-permute-start | bytes 1966088 | tf_op jit(solution)/shard_map/ppermute | solution.py:171
  398.0 52.2 %collective-permute-start.30 = (bf16[1,160,2048]{2,1,0:T(8,128)(2,1)S(1)}, bf16[1,160,2048]{2,1,0:T(8,128)(2,1)S(1)}, u32[]{:S(2)}, u32[]{:S(2)}) collective-permute-start(bf16[1,160,2048]{2,1,0:T(8,128)(2,1)S(1)} %copy-done.38), channel_id=1, source_target_pairs={{0,16},{8,24},{16,0},{24,8},{1,17},{9,25},{17,1},{25,9},{2,18},{10... | collective-permute-start | bytes 1966088 | tf_op jit(solution)/shard_map/ppermute | solution.py:171
  410.9 39.9 %collective-permute-start.27 = (bf16[1,160,2048]{2,1,0:T(8,128)(2,1)S(1)}, bf16[1,160,2048]{2,1,0:T(8,128)(2,1)S(1)}, u32[]{:S(2)}, u32[]{:S(2)}) collective-permute-start(bf16[1,160,2048]{2,1,0:T(8,128)(2,1)S(1)} %copy-done.38), channel_id=1, source_target_pairs={{0,24},{8,16},{16,8},{24,0},{1,25},{9,17},{17,9},{25,1},{2,26},{10... | collective-permute-start | bytes 1966088 | tf_op jit(solution)/shard_map/ppermute | solution.py:171
  438.1 59.5 %collective-permute-start.26 = (bf16[4,1152,256]{2,1,0:T(8,128)(2,1)}, bf16[4,1152,256]{2,1,0:T(8,128)(2,1)S(1)}, u32[]{:S(2)}, u32[]{:S(2)}) collective-permute-start(bf16[4,1152,256]{2,1,0:T(8,128)(2,1)} %all-to-all-done.2), channel_id=1, source_target_pairs={{0,1},{1,0},{2,3},{3,2},{4,5},{5,4},{6,7},{7,6},{8,9},{9,8},{10,11... | collective-permute-start | bytes 7077896 | tf_op jit(solution)/shard_map/ppermute | solution.py:171
  448.6 45.7 %collective-permute-start.25 = (bf16[2,160,2048]{2,1,0:T(8,128)(2,1)S(1)}, bf16[2,160,2048]{2,1,0:T(8,128)(2,1)S(1)}, u32[]{:S(2)}, u32[]{:S(2)}) collective-permute-start(bf16[2,160,2048]{2,1,0:T(8,128)(2,1)S(1)} %pad_maximum_fusion.15), channel_id=1, source_target_pairs={{0,2},{2,0},{4,6},{6,4},{1,3},{3,1},{5,7},{7,5},{8,10},{10,8},{12,... | collective-permute-start | bytes 3932168 | tf_op jit(solution)/shard_map/ppermute | solution.py:171
  450.8 43.1 %collective-permute-start.28 = (bf16[1,160,2048]{2,1,0:T(8,128)(2,1)S(1)}, bf16[1,160,2048]{2,1,0:T(8,128)(2,1)S(1)}, u32[]{:S(2)}, u32[]{:S(2)}) collective-permute-start(bf16[1,160,2048]{2,1,0:T(8,128)(2,1)S(1)} %collective-permute-done.27), channel_id=1, source_target_pairs={{0,4},{2,6},{4,0},{6,2},{1,5},{3,7},{5,1},{7,3},{8,12},{10,14},{12... | collective-permute-start | bytes 1966088 | tf_op jit(solution)/shard_map/ppermute | solution.py:171
  567.0 45.6 %collective-permute-start.42 = (bf16[1,160,2048]{2,1,0:T(8,128)(2,1)S(1)}, bf16[1,160,2048]{2,1,0:T(8,128)(2,1)S(1)}, u32[]{:S(2)}, u32[]{:S(2)}) collective-permute-start(bf16[1,160,2048]{2,1,0:T(8,128)(2,1)S(1)} %fusion.140), channel_id=1, source_target_pairs={{0,4},{2,6},{4,0},{6,2},{1,5},{3,7},{5,1},{7,3},{8,12},{10,14},{12... | collective-permute-start | bytes 1966088 | tf_op jit(solution)/shard_map/ppermute | solution.py:171
  576.3 36.2 %collective-permute-start.41 = (bf16[1,2,160,2048]{3,2,1,0:T(8,128)(2,1)S(1)}, bf16[1,2,160,2048]{3,2,1,0:T(8,128)(2,1)S(1)}, u32[]{:S(2)}, u32[]{:S(2)}) collective-permute-start(bf16[1,2,160,2048]{3,2,1,0:T(8,128)(2,1)S(1)} %get-tuple-element.492), channel_id=1, source_target_pairs={{0,2},{2,0},{4,6},{6,4},{1,3},{3,1},{5,7},{7,5},{8,10},{10,8},{12,... | collective-permute-start | bytes 3932168 | tf_op jit(solution)/shard_map/ppermute | solution.py:171
  609.4 37.5 %collective-permute-start.40 = (bf16[4,2,160,2048]{3,2,0,1:T(8,128)(2,1)}, bf16[4,2,160,2048]{3,2,0,1:T(8,128)(2,1)}, u32[]{:S(2)}, u32[]{:S(2)}) collective-permute-start(bf16[4,2,160,2048]{3,2,0,1:T(8,128)(2,1)} %copy.75), channel_id=1, source_target_pairs={{0,2},{2,0},{4,6},{6,4},{1,3},{3,1},{5,7},{7,5},{8,10},{10,8},{12,... | collective-permute-start | bytes 15728648 | tf_op jit(solution)/shard_map/ppermute | solution.py:171
  610.5 36.4 %collective-permute-start.44 = (bf16[1,160,2048]{2,1,0:T(8,128)(2,1)}, bf16[1,160,2048]{2,1,0:T(8,128)(2,1)}, u32[]{:S(2)}, u32[]{:S(2)}) collective-permute-start(bf16[1,160,2048]{2,1,0:T(8,128)(2,1)} %add_convert_fusion.9), channel_id=1, source_target_pairs={{0,8},{8,0},{16,24},{24,16},{1,9},{9,1},{17,25},{25,17},{2,10},{10... | collective-permute-start | bytes 1966088 | tf_op jit(solution)/shard_map/ppermute | solution.py:171
  617.0 46.9 %collective-permute-start.45 = (bf16[1,160,2048]{2,1,0:T(8,128)(2,1)}, bf16[1,160,2048]{2,1,0:T(8,128)(2,1)}, u32[]{:S(2)}, u32[]{:S(2)}) collective-permute-start(bf16[1,160,2048]{2,1,0:T(8,128)(2,1)} %add_convert_fusion.8), channel_id=1, source_target_pairs={{0,16},{8,24},{16,0},{24,8},{1,17},{9,25},{17,1},{25,9},{2,18},{10... | collective-permute-start | bytes 1966088 | tf_op jit(solution)/shard_map/ppermute | solution.py:171
  646.3 84.9 %collective-permute-start.50 = (bf16[4,256,1152]{2,1,0:T(8,128)(2,1)}, bf16[4,256,1152]{2,1,0:T(8,128)(2,1)}, u32[]{:S(2)}, u32[]{:S(2)}) collective-permute-start(bf16[4,256,1152]{2,1,0:T(8,128)(2,1)} %fusion.97), channel_id=1, source_target_pairs={{0,1},{1,0},{2,3},{3,2},{4,5},{5,4},{6,7},{7,6},{8,9},{9,8},{10,11... | collective-permute-start | bytes 7077896 | tf_op jit(solution)/shard_map/ppermute | solution.py:171
  670.4 46.0 %collective-permute-start.48 = (bf16[1,160,2048]{2,1,0:T(8,128)(2,1)S(1)}, bf16[1,160,2048]{2,1,0:T(8,128)(2,1)}, u32[]{:S(2)}, u32[]{:S(2)}) collective-permute-start(bf16[1,160,2048]{2,1,0:T(8,128)(2,1)S(1)} %pad_maximum_fusion.24), channel_id=1, source_target_pairs={{0,4},{2,6},{4,0},{6,2},{1,5},{3,7},{5,1},{7,3},{8,12},{10,14},{12... | collective-permute-start | bytes 1966088 | tf_op jit(solution)/shard_map/ppermute | solution.py:171
  683.7 68.7 %collective-permute-start.51 = (bf16[4,160,2048]{2,1,0:T(8,128)(2,1)}, bf16[4,160,2048]{2,1,0:T(8,128)(2,1)}, u32[]{:S(2)}, u32[]{:S(2)}) collective-permute-start(bf16[4,160,2048]{2,1,0:T(8,128)(2,1)} %fusion.69), channel_id=1, source_target_pairs={{0,4},{2,6},{4,0},{6,2},{1,5},{3,7},{5,1},{7,3},{8,12},{10,14},{12... | collective-permute-start | bytes 7864328 | tf_op jit(solution)/shard_map/ppermute | solution.py:171
  736.4 124.1 %all-to-all-start.3 = ((bf16[4,256,1152]{2,1,0:T(8,128)(2,1)}), bf16[4,256,1152]{2,1,0:T(8,128)(2,1)}, u32[]{:S(2)}, u32[]{:S(2)}) async-start(bf16[4,256,1152]{2,1,0:T(8,128)(2,1)} %fusion.48), calls=%async_computation.3 | async-start | bytes 4718592 | tf_op jit(solution)/shard_map/all_to_all | solution.py:327
  751.3 125.8 %collective-permute-start.60 = (bf16[4,256,1152]{2,1,0:T(8,128)(2,1)}, bf16[4,256,1152]{2,1,0:T(8,128)(2,1)}, u32[]{:S(2)}, u32[]{:S(2)}) collective-permute-start(bf16[4,256,1152]{2,1,0:T(8,128)(2,1)} %fusion.95), channel_id=1, source_target_pairs={{0,1},{1,0},{2,3},{3,2},{4,5},{5,4},{6,7},{7,6},{8,9},{9,8},{10,11... | collective-permute-start | bytes 7077896 | tf_op jit(solution)/shard_map/ppermute | solution.py:171
  767.5 49.5 %collective-permute-start.52 = (bf16[1,160,2048]{2,1,0:T(8,128)(2,1)S(1)}, bf16[1,160,2048]{2,1,0:T(8,128)(2,1)S(1)}, u32[]{:S(2)}, u32[]{:S(2)}) collective-permute-start(bf16[1,160,2048]{2,1,0:T(8,128)(2,1)S(1)} %get-tuple-element.487), channel_id=1, source_target_pairs={{0,8},{8,0},{16,24},{24,16},{1,9},{9,1},{17,25},{25,17},{2,10},{10... | collective-permute-start | bytes 1966088 | tf_op jit(solution)/shard_map/ppermute | solution.py:171
  771.0 77.6 %collective-permute-start.53 = (bf16[1,160,2048]{2,1,0:T(8,128)(2,1)S(1)}, bf16[1,160,2048]{2,1,0:T(8,128)(2,1)S(1)}, u32[]{:S(2)}, u32[]{:S(2)}) collective-permute-start(bf16[1,160,2048]{2,1,0:T(8,128)(2,1)S(1)} %get-tuple-element.489), channel_id=1, source_target_pairs={{0,16},{8,24},{16,0},{24,8},{1,17},{9,25},{17,1},{25,9},{2,18},{10... | collective-permute-start | bytes 1966088 | tf_op jit(solution)/shard_map/ppermute | solution.py:171
  772.0 76.7 %collective-permute-start.54 = (bf16[1,160,2048]{2,1,0:T(8,128)(2,1)S(1)}, bf16[1,160,2048]{2,1,0:T(8,128)(2,1)S(1)}, u32[]{:S(2)}, u32[]{:S(2)}) collective-permute-start(bf16[1,160,2048]{2,1,0:T(8,128)(2,1)S(1)} %get-tuple-element.488), channel_id=1, source_target_pairs={{0,24},{8,16},{16,8},{24,0},{1,25},{9,17},{17,9},{25,1},{2,26},{10... | collective-permute-start | bytes 1966088 | tf_op jit(solution)/shard_map/ppermute | solution.py:171
  773.8 37.4 %collective-permute-start.58 = (bf16[2,288,256]{2,1,0:T(8,128)(2,1)S(1)}, bf16[2,288,256]{2,1,0:T(8,128)(2,1)S(1)}, u32[]{:S(2)}, u32[]{:S(2)}) collective-permute-start(bf16[2,288,256]{2,1,0:T(8,128)(2,1)S(1)} %fusion.186), channel_id=1, source_target_pairs={{0,1},{1,0},{2,3},{3,2},{4,5},{5,4},{6,7},{7,6},{8,9},{9,8},{10,11... | collective-permute-start | bytes 884744 | tf_op jit(solution)/shard_map/ppermute | solution.py:171
  815.8 43.1 %collective-permute-start.71 = (bf16[4,512,384]{2,1,0:T(8,128)(2,1)S(1)}, bf16[4,512,384]{2,1,0:T(8,128)(2,1)S(1)}, u32[]{:S(2)}, u32[]{:S(2)}) collective-permute-start(bf16[4,512,384]{2,1,0:T(8,128)(2,1)S(1)} %dynamic-slice_bitcast_fusion.2), channel_id=1, source_target_pairs={{0,1},{1,0},{2,3},{3,2},{4,5},{5,4},{6,7},{7,6},{8,9},{9,8},{10,11... | collective-permute-start | bytes 4718600 | tf_op jit(solution)/shard_map/ppermute | solution.py:171
  860.5 55.7 %all-to-all-start.6 = ((bf16[4,512,384]{2,1,0:T(8,128)(2,1)}), bf16[4,512,384]{2,1,0:T(8,128)(2,1)}, u32[]{:S(2)}, u32[]{:S(2)}) async-start(bf16[4,512,384]{2,1,0:T(8,128)(2,1)} %fusion.68), calls=%async_computation.6 | async-start | bytes 3145728 | tf_op jit(solution)/shard_map/all_to_all | solution.py:327
  888.0 79.7 %collective-permute-start.65 = (bf16[4,384,768]{2,1,0:T(8,128)(2,1)}, bf16[4,384,768]{2,1,0:T(8,128)(2,1)}, u32[]{:S(2)}, u32[]{:S(2)}) collective-permute-start(bf16[4,384,768]{2,1,0:T(8,128)(2,1)} %get-tuple-element.471), channel_id=1, source_target_pairs={{0,1},{1,0},{2,3},{3,2},{4,5},{5,4},{6,7},{7,6},{8,9},{9,8},{10,11... | collective-permute-start | bytes 7077896 | tf_op jit(solution)/shard_map/ppermute | solution.py:171
  888.5 103.9 %collective-permute-start.66 = (bf16[4,1152,256]{2,1,0:T(8,128)(2,1)}, bf16[4,1152,256]{2,1,0:T(8,128)(2,1)}, u32[]{:S(2)}, u32[]{:S(2)}) collective-permute-start(bf16[4,1152,256]{2,1,0:T(8,128)(2,1)} %maximum_maximum_fusion.4), channel_id=1, source_target_pairs={{0,1},{1,0},{2,3},{3,2},{4,5},{5,4},{6,7},{7,6},{8,9},{9,8},{10,11... | collective-permute-start | bytes 7077896 | tf_op jit(solution)/shard_map/ppermute | solution.py:171
  916.2 76.1 %all-to-all-start.4 = ((bf16[4,256,1152]{2,1,0:T(8,128)(2,1)}), bf16[4,256,1152]{2,1,0:T(8,128)(2,1)}, u32[]{:S(2)}, u32[]{:S(2)}) async-start(bf16[4,256,1152]{2,1,0:T(8,128)(2,1)} %fusion.47), calls=%async_computation.4 | async-start | bytes 4718592 | tf_op jit(solution)/shard_map/all_to_all | solution.py:327
  929.4 72.7 %collective-permute-start.55 = (bf16[1,160,2048]{2,1,0:T(8,128)(2,1)}, bf16[1,160,2048]{2,1,0:T(8,128)(2,1)}, u32[]{:S(2)}, u32[]{:S(2)}) collective-permute-start(bf16[1,160,2048]{2,1,0:T(8,128)(2,1)} %pad_maximum_fusion.25), channel_id=1, source_target_pairs={{0,4},{2,6},{4,0},{6,2},{1,5},{3,7},{5,1},{7,3},{8,12},{10,14},{12... | collective-permute-start | bytes 1966088 | tf_op jit(solution)/shard_map/ppermute | solution.py:171
  931.0 73.9 %collective-permute-start.63 = (bf16[1,160,2048]{2,1,0:T(8,128)(2,1)}, bf16[1,160,2048]{2,1,0:T(8,128)(2,1)}, u32[]{:S(2)}, u32[]{:S(2)}) collective-permute-start(bf16[1,160,2048]{2,1,0:T(8,128)(2,1)} %pad_maximum_fusion.27), channel_id=1, source_target_pairs={{0,4},{2,6},{4,0},{6,2},{1,5},{3,7},{5,1},{7,3},{8,12},{10,14},{12... | collective-permute-start | bytes 1966088 | tf_op jit(solution)/shard_map/ppermute | solution.py:171
  996.0 56.8 %all-to-all-start.7 = ((bf16[4,1152,256]{2,1,0:T(8,128)(2,1)}), bf16[4,1152,256]{2,1,0:T(8,128)(2,1)S(1)}, u32[]{:S(2)}, u32[]{:S(2)}) async-start(bf16[4,1152,256]{2,1,0:T(8,128)(2,1)} %add_convert_fusion), calls=%async_computation.7 | async-start | bytes 4718592 | tf_op jit(solution)/shard_map/all_to_all | solution.py:327
  1004.9 53.0 %collective-permute-start.56 = (bf16[2,160,2048]{2,1,0:T(8,128)(2,1)}, bf16[2,160,2048]{2,1,0:T(8,128)(2,1)}, u32[]{:S(2)}, u32[]{:S(2)}) collective-permute-start(bf16[2,160,2048]{2,1,0:T(8,128)(2,1)} %pad_maximum_fusion.20), channel_id=1, source_target_pairs={{0,2},{2,0},{4,6},{6,4},{1,3},{3,1},{5,7},{7,5},{8,10},{10,8},{12,... | collective-permute-start | bytes 3932168 | tf_op jit(solution)/shard_map/ppermute | solution.py:171
  1007.8 50.1 %collective-permute-start.64 = (bf16[2,160,2048]{2,1,0:T(8,128)(2,1)}, bf16[2,160,2048]{2,1,0:T(8,128)(2,1)}, u32[]{:S(2)}, u32[]{:S(2)}) collective-permute-start(bf16[2,160,2048]{2,1,0:T(8,128)(2,1)} %pad_maximum_fusion.21), channel_id=1, source_target_pairs={{0,2},{2,0},{4,6},{6,4},{1,3},{3,1},{5,7},{7,5},{8,10},{10,8},{12,... | collective-permute-start | bytes 3932168 | tf_op jit(solution)/shard_map/ppermute | solution.py:171
  1054.2 59.0 %all-to-all-start.5 = ((bf16[4,400,768]{2,1,0:T(8,128)(2,1)}), bf16[4,400,768]{2,1,0:T(8,128)(2,1)S(1)}, u32[]{:S(2)}, u32[]{:S(2)}) async-start(bf16[4,400,768]{2,1,0:T(8,128)(2,1)} %pad_maximum_fusion.8), calls=%async_computation.5 | async-start | bytes 4915200 | tf_op jit(solution)/shard_map/all_to_all | solution.py:327
  (258 other events, 2956.4 us)
Sparse Core Ops, SparseCore 0:
  29.9 121.3 all-gather.2
